TPU v7x, 1024 devices: a whole 8x8x8 slice. The times are simulated.
1024 devices in a mesh: row: 32 (over y_hi, x, core), col: 32 (over y_lo, z).
Axes of the slice: x: 8, y: 8 (y_hi: 2, y_lo: 4; y = y_hi * 4 + y_lo), z: 8, core: 2. Of those that a mesh axis runs over, the one named last changes fastest.
Arguments:
- source_emb: float32 [32, 32, 128, 400], P('row', 'col'), may hold values from -6 to 6
- source_acc: float32 [32, 32, 128], P('row', 'col'), may hold values from 1e-05 to 0.01
- target_emb: float32 [32, 32, 128, 400], P('row', 'col'), may hold values from -7.5 to 7.5
- target_acc: float32 [32, 32, 128], P('row', 'col'), may hold values from 1e-05 to 0.01
- relations: bfloat16 [4131, 400], replicated, may hold values from -0.59765625 to 0.59765625
- src_index: int32 [32, 32, 2, 128], P('row', 'col'), may hold values from 0 to 127
- dst_index: int32 [32, 32, 2, 128], P('row', 'col'), may hold values from 0 to 127
- rel_index: int32 [32, 32, 2, 128], P('row', 'col'), may hold values from 0 to 4130
- neg_index: int32 [32, 32, 2, 1024], P('row', 'col'), may hold values from 0 to 127
Outputs:
- source_out: float32 [32, 32, 128, 400], P('row', 'col')
- source_acc_out: float32 [32, 32, 128], P('row', 'col')
- target_out: float32 [32, 32, 128, 400], P('row', 'col')
- target_acc_out: float32 [32, 32, 128], P('row', 'col')
All inputs are finite; a program needn't handle non-finite values.
Results may differ from a plain program's by a relative error of at most 0.00072.
Values sent between devices are 32-bit elements; how exact they have to be, the bound alone decides.
No kernel may reach another device: no remote copies, remote signals or barrier semaphores. Data moves between devices by JAX's collectives and lax.ppermute only.
A program may use at most 32 MiB of HBM per device.

v0:
```python
import jax
import jax.numpy as jnp
from jax import lax
from jax.sharding import PartitionSpec as P

learning_rate = 0.1


def from_behind(x, axis, by):
    length = lax.axis_size(axis)
    return lax.ppermute(x, axis, [(i, (i + by) % length) for i in range(length)])


def complex_query(entity_rows, operator_rows):
    half_width = entity_rows.shape[1] // 2
    real_part = entity_rows[:, :half_width]
    imag_part = entity_rows[:, half_width:]
    op_real = operator_rows[:, :half_width]
    op_imag = operator_rows[:, half_width:]
    return jnp.concatenate(
        [real_part * op_real - imag_part * op_imag, real_part * op_imag + imag_part * op_real],
        axis=1,
    )


def query_back(grad_rows, operator_rows):
    half_width = grad_rows.shape[1] // 2
    grad_real = grad_rows[:, :half_width]
    grad_imag = grad_rows[:, half_width:]
    op_real = operator_rows[:, :half_width]
    op_imag = operator_rows[:, half_width:]
    return jnp.concatenate(
        [grad_real * op_real + grad_imag * op_imag, grad_imag * op_real - grad_real * op_imag],
        axis=1,
    )


def adagrad(table, sums, gradient):
    new_sums = sums + jnp.mean(gradient * gradient, axis=1)
    return (table - learning_rate * gradient / jnp.sqrt(new_sums)[:, None], new_sums)


def move_source(table, sums):
    return from_behind((table, sums), "row", 1)


def move_target(table, sums):
    return from_behind((table, sums), "col", 1)


def negative_terms(queries_b, target, neg_rows):
    neg_count = neg_rows.shape[0]
    negatives_b = target[neg_rows].astype(jnp.bfloat16)
    scores = jnp.dot(queries_b, negatives_b.T, preferred_element_type=jnp.float32)
    weights = (jax.nn.sigmoid(scores) / neg_count).astype(jnp.bfloat16)
    pull_term = jnp.dot(weights, negatives_b, preferred_element_type=jnp.float32)

    def push_rows():
        grad_negs = jnp.dot(weights.T, queries_b, preferred_element_type=jnp.float32)
        return jnp.zeros_like(target).at[neg_rows].add(grad_negs)

    return (pull_term, push_rows)


def on_device(
    source_emb,
    source_acc,
    target_emb,
    target_acc,
    relations,
    src_index,
    dst_index,
    rel_index,
    neg_index,
):
    source = source_emb[0, 0]
    source_sums = source_acc[0, 0]
    target = target_emb[0, 0]
    target_sums = target_acc[0, 0]
    step_count = src_index.shape[2]
    for rotation in range(step_count):
        src_rows = src_index[0, 0, rotation]
        dst_rows = dst_index[0, 0, rotation]
        neg_rows = neg_index[0, 0, rotation]
        operator_rows = relations[rel_index[0, 0, rotation]].astype(jnp.float32)
        queries = complex_query(source[src_rows], operator_rows)
        matched = target[dst_rows]
        positive = jnp.sum(queries * matched, axis=1)
        pos_grad = -jax.nn.sigmoid(-positive)
        queries_b = queries.astype(jnp.bfloat16)
        pull_term, push_rows = negative_terms(queries_b, target, neg_rows)
        grad_query = pos_grad[:, None] * matched + pull_term
        source_grad = jnp.zeros_like(source).at[src_rows].add(query_back(grad_query, operator_rows))
        target_grad = push_rows().at[dst_rows].add(pos_grad[:, None] * queries)
        source, source_sums = adagrad(source, source_sums, source_grad)
        target, target_sums = adagrad(target, target_sums, target_grad)
        source, source_sums = move_source(source, source_sums)
        target, target_sums = move_target(target, target_sums)
    return (
        source[None, None],
        source_sums[None, None],
        target[None, None],
        target_sums[None, None],
    )


def solution(mesh):
    in_specs = (
        P("row", "col", None, None),
        P("row", "col", None),
        P("row", "col", None, None),
        P("row", "col", None),
        P(),
        P("row", "col", None, None),
        P("row", "col", None, None),
        P("row", "col", None, None),
        P("row", "col", None, None),
    )
    out_specs = (
        P("row", "col", None, None),
        P("row", "col", None),
        P("row", "col", None, None),
        P("row", "col", None),
    )
    return jax.shard_map(
        on_device, mesh=mesh, in_specs=in_specs, out_specs=out_specs, check_vma=False
    )
```

profile of v0, /device:TPU:1, one launch (start us, length us, event | category | flops | bytes accessed | tf_op | source)
XLA Modules:
  0.0 106.4 jit_solution(7246210869976143175)
XLA Ops:
  3.7 1.1 copy.29
  6.9 3.5 %gather_fusion.3 = bf16[1024,400]{1,0:T(8,128)(2,1)S(1)} fusion(f32[128,400]{1,0:T(8,128)S(1)} %bitcast.53, s32[1024]{0:T(1024)S(1)} %broadcast_clamp_fusion.1), kind=kCustom, calls=%fused_computation.3 | custom fusion | bytes 1642496 | tf_op jit(solution)/shard_map/gather | solution.py:53
  10.4 6.1 %copy.31 = bf16[4131,400]{1,0:T(8,128)(2,1)} copy(bf16[4131,400]{0,1:T(8,128)(2,1)} %param.13) | data formatting | bytes 6609600 | tf_op args[4]
  16.4 3.6 %gather_fusion.1 = bf16[128,400]{1,0:T(8,128)(2,1)S(1)} fusion(bf16[4131,400]{1,0:T(8,128)(2,1)} %copy.31, s32[1024]{0:T(1024)S(1)} %get-tuple-element.43), kind=kCustom, calls=%fused_computation.1 | custom fusion | bytes 205312 | tf_op jit(solution)/shard_map/gather | solution.py:85
  21.6 1.4 %scatter_custom_fusion = f32[128,400]{1,0:T(8,128)S(1)} fusion(s32[128]{0:T(128)S(1)} %get-tuple-element.39, f32[128,400]{1,0:T(8,128)S(1)} %copy.37, f32[]{:T(128)} %constant.8.clone.1), kind=kCustom, calls=%fused_computation.57 | custom fusion | flops 51200 | bytes 204804 | tf_op jit(solution)/shard_map/scatter-add | solution.py:93
  23.1 4.5 %collective-permute-start.2 = (f32[128]{0:T(128)S(1)}, f32[128]{0:T(128)S(1)}, u32[]{:S(2)}, u32[]{:S(2)}) collective-permute-start(f32[128]{0:T(128)S(1)} %get-tuple-element.19), channel_id=1, source_target_pairs={{0,32},{32,64},{64,96},{96,128},{128,160},{160,192},{192,224},{224... | collective-permute-start | bytes 1544 | tf_op jit(solution)/shard_map/ppermute | solution.py:11
  28.4 1.9 %collective-permute-start = (f32[128,400]{1,0:T(8,128)}, f32[128,400]{1,0:T(8,128)S(1)}, u32[]{:S(2)}, u32[]{:S(2)}) collective-permute-start(f32[128,400]{1,0:T(8,128)} %divide_subtract_fusion.3), channel_id=1, source_target_pairs={{0,32},{32,64},{64,96},{96,128},{128,160},{160,192},{192,224},{224... | collective-permute-start | bytes 614408 | tf_op jit(solution)/shard_map/ppermute | solution.py:11
  31.0 6.7 %scatter_custom_fusion.1 = f32[128,400]{1,0:T(8,128)S(1)} fusion(s32[1024]{0:T(1024)S(1)} %bitcast.60, f32[1024,400]{1,0:T(8,128)S(1)} %fusion.27, f32[]{:T(128)} %constant.8.clone.1), kind=kCustom, calls=%fused_computation.55 | custom fusion | flops 409600 | bytes 204804 | tf_op jit(solution)/shard_map/scatter-add | solution.py:60
  37.6 1.5 %scatter_fusion = f32[128,400]{1,0:T(8,128)S(1)} fusion(f32[128,400]{1,0:T(8,128)S(1)} %scatter_custom_fusion.1, s32[128]{0:T(128)S(1)} %get-tuple-element.35, f32[128,400]{1,0:T(8,128)S(1)} %copy.43), kind=kCustom, calls=%fused_computation.10 | custom fusion | flops 51200 | bytes 614912 | tf_op jit(solution)/shard_map/scatter-add | solution.py:94
  39.3 4.9 %collective-permute-start.5 = (f32[128]{0:T(128)S(1)}, f32[128]{0:T(128)S(1)}, u32[]{:S(2)}, u32[]{:S(2)}) collective-permute-start(f32[128]{0:T(128)S(1)} %get-tuple-element.17), channel_id=1, source_target_pairs={{0,1},{1,2},{2,3},{3,4},{4,5},{5,6},{6,7},{7,8},{8,9},{9,10},{10,1... | collective-permute-start | bytes 1544 | tf_op jit(solution)/shard_map/ppermute | solution.py:11
  44.3 5.1 %collective-permute-start.1 = (f32[128,400]{1,0:T(8,128)S(1)}, f32[128,400]{1,0:T(8,128)S(1)}, u32[]{:S(2)}, u32[]{:S(2)}) collective-permute-start(f32[128,400]{1,0:T(8,128)S(1)} %divide_subtract_fusion.2), channel_id=1, source_target_pairs={{0,1},{1,2},{2,3},{3,4},{4,5},{5,6},{6,7},{7,8},{8,9},{9,10},{10,1... | collective-permute-start | bytes 614408 | tf_op jit(solution)/shard_map/ppermute | solution.py:11
  49.4 3.6 %gather_fusion.5 = bf16[128,400]{1,0:T(8,128)(2,1)S(1)} fusion(bf16[4131,400]{1,0:T(8,128)(2,1)} %copy.31, s32[1024]{0:T(1024)S(1)} %get-tuple-element.42), kind=kCustom, calls=%fused_computation.5 | custom fusion | bytes 205312 | tf_op jit(solution)/shard_map/gather | solution.py:85
  54.3 13.7 %collective-permute-done.1 = f32[128,400]{1,0:T(8,128)S(1)} collective-permute-done((f32[128,400]{1,0:T(8,128)S(1)}, f32[128,400]{1,0:T(8,128)S(1)}, u32[]{:S(2)}, u32[]{:S(2)}) %collective-permute-start.1) | collective-permute-done | bytes 204832 | tf_op jit(solution)/shard_map/ppermute | solution.py:11
  69.0 3.5 %gather_fusion.7 = bf16[1024,400]{1,0:T(8,128)(2,1)S(1)} fusion(f32[128,400]{1,0:T(8,128)S(1)} %collective-permute-done.1, s32[1024]{0:T(1024)S(1)} %broadcast_clamp_fusion), kind=kCustom, calls=%fused_computation.7 | custom fusion | bytes 1642496 | tf_op jit(solution)/shard_map/gather | solution.py:53
  73.0 1.8 %fusion.30 = f32[1024,400]{1,0:T(8,128)} fusion(bf16[128,1024]{1,0:T(8,128)(2,1)S(1)} %fusion.9, f32[128,200]{0,1:T(8,128)S(1)} %get-tuple-element.23, f32[128,200]{0,1:T(8,128)S(1)} %get-tuple-element.22), kind=kOutput, calls=%fused_computation.70 | convolution fusion | flops 105062400 | bytes 2105344 | tf_op jit(solution)/shard_map/dot_general | solution.py:59
  75.5 1.4 %scatter_custom_fusion.3 = f32[128,400]{1,0:T(8,128)S(1)} fusion(s32[128]{0:T(128)S(1)} %get-tuple-element.38, f32[128,400]{1,0:T(8,128)S(1)} %copy.46, f32[]{:T(128)} %constant.8.clone.1), kind=kCustom, calls=%fused_computation.53 | custom fusion | flops 51200 | bytes 204804 | tf_op jit(solution)/shard_map/scatter-add | solution.py:93
  77.3 4.0 %collective-permute-start.3 = (f32[128,400]{1,0:T(8,128)S(1)}, f32[128,400]{1,0:T(8,128)S(1)}, u32[]{:S(2)}, u32[]{:S(2)}) collective-permute-start(f32[128,400]{1,0:T(8,128)S(1)} %divide_subtract_fusion.1), channel_id=1, source_target_pairs={{0,32},{32,64},{64,96},{96,128},{128,160},{160,192},{192,224},{224... | collective-permute-start | bytes 614408 | tf_op jit(solution)/shard_map/ppermute | solution.py:11
  81.3 7.3 %scatter_custom_fusion.4 = f32[128,400]{1,0:T(8,128)S(1)} fusion(s32[1024]{0:T(1024)S(1)} %bitcast.58, f32[1024,400]{1,0:T(8,128)} %fusion.30, f32[]{:T(128)} %constant.8.clone.1), kind=kCustom, calls=%fused_computation.51 | custom fusion | flops 409600 | bytes 205312 | tf_op jit(solution)/shard_map/scatter-add | solution.py:60
  88.6 1.5 %scatter_fusion.1 = f32[128,400]{1,0:T(8,128)S(1)} fusion(f32[128,400]{1,0:T(8,128)S(1)} %scatter_custom_fusion.4, s32[128]{0:T(128)S(1)} %get-tuple-element.34, f32[128,400]{1,0:T(8,128)S(1)} %copy.48), kind=kCustom, calls=%fused_computation.13 | custom fusion | flops 51200 | bytes 614912 | tf_op jit(solution)/shard_map/scatter-add | solution.py:94
  90.3 1.9 %collective-permute-start.6 = (f32[128,400]{1,0:T(8,128)S(1)}, f32[128,400]{1,0:T(8,128)S(1)}, u32[]{:S(2)}, u32[]{:S(2)}) collective-permute-start(f32[128,400]{1,0:T(8,128)S(1)} %divide_subtract_fusion), channel_id=1, source_target_pairs={{0,1},{1,2},{2,3},{3,4},{4,5},{5,6},{6,7},{7,8},{8,9},{9,10},{10,1... | collective-permute-start | bytes 614408 | tf_op jit(solution)/shard_map/ppermute | solution.py:11
  92.3 1.9 %collective-permute-start.4 = (f32[128]{0:T(128)S(1)}, f32[128]{0:T(128)S(1)}, u32[]{:S(2)}, u32[]{:S(2)}) collective-permute-start(f32[128]{0:T(128)S(1)} %get-tuple-element.15), channel_id=1, source_target_pairs={{0,32},{32,64},{64,96},{96,128},{128,160},{160,192},{192,224},{224... | collective-permute-start | bytes 1544 | tf_op jit(solution)/shard_map/ppermute | solution.py:11
  94.2 1.9 %collective-permute-start.7 = (f32[128]{0:T(128)S(1)}, f32[128]{0:T(128)S(1)}, u32[]{:S(2)}, u32[]{:S(2)}) collective-permute-start(f32[128]{0:T(128)S(1)} %get-tuple-element.13), channel_id=1, source_target_pairs={{0,1},{1,2},{2,3},{3,4},{4,5},{5,6},{6,7},{7,8},{8,9},{9,10},{10,1... | collective-permute-start | bytes 1544 | tf_op jit(solution)/shard_map/ppermute | solution.py:11
  96.1 7.6 %collective-permute-done.7 = f32[128]{0:T(128)S(1)} collective-permute-done((f32[128]{0:T(128)S(1)}, f32[128]{0:T(128)S(1)}, u32[]{:S(2)}, u32[]{:S(2)}) %collective-permute-start.7) | collective-permute-done | bytes 544 | tf_op jit(solution)/shard_map/ppermute | solution.py:11
  103.7 0.8 copy.49
  (75 shorter events, 14.1 us)
Async XLA Ops:
  0.6 5.2 %copy-start = (f32[1,1,128,400]{2,3,1,0:T(8,128)S(1)}, f32[1,1,128,400]{2,3,1,0:T(8,128)}, u32[]{:S(2)}) copy-start(f32[1,1,128,400]{2,3,1,0:T(8,128)} %param.11) | copy-start | bytes 614404
  20.9 2.2 %copy-start.1 = (f32[1,1,128]{2,1,0:T(1,128)S(1)}, f32[1,1,128]{2,1,0:T(1,128)}, u32[]{:S(2)}) copy-start(f32[1,1,128]{2,1,0:T(1,128)} %param.10) | copy-start | bytes 1540
  23.1 54.0 %collective-permute-start.2 = (f32[128]{0:T(128)S(1)}, f32[128]{0:T(128)S(1)}, u32[]{:S(2)}, u32[]{:S(2)}) collective-permute-start(f32[128]{0:T(128)S(1)} %get-tuple-element.19), channel_id=1, source_target_pairs={{0,32},{32,64},{64,96},{96,128},{128,160},{160,192},{192,224},{224... | collective-permute-start | bytes 1544 | tf_op jit(solution)/shard_map/ppermute | solution.py:11
  28.4 24.8 %collective-permute-start = (f32[128,400]{1,0:T(8,128)}, f32[128,400]{1,0:T(8,128)S(1)}, u32[]{:S(2)}, u32[]{:S(2)}) collective-permute-start(f32[128,400]{1,0:T(8,128)} %divide_subtract_fusion.3), channel_id=1, source_target_pairs={{0,32},{32,64},{64,96},{96,128},{128,160},{160,192},{192,224},{224... | collective-permute-start | bytes 614408 | tf_op jit(solution)/shard_map/ppermute | solution.py:11
  37.6 1.6 %copy-start.2 = (f32[1,1,128]{2,1,0:T(1,128)S(1)}, f32[1,1,128]{2,1,0:T(1,128)}, u32[]{:S(2)}) copy-start(f32[1,1,128]{2,1,0:T(1,128)} %param.12) | copy-start | bytes 1540
  39.3 51.0 %collective-permute-start.5 = (f32[128]{0:T(128)S(1)}, f32[128]{0:T(128)S(1)}, u32[]{:S(2)}, u32[]{:S(2)}) collective-permute-start(f32[128]{0:T(128)S(1)} %get-tuple-element.17), channel_id=1, source_target_pairs={{0,1},{1,2},{2,3},{3,4},{4,5},{5,6},{6,7},{7,8},{8,9},{9,10},{10,1... | collective-permute-start | bytes 1544 | tf_op jit(solution)/shard_map/ppermute | solution.py:11
  44.3 23.7 %collective-permute-start.1 = (f32[128,400]{1,0:T(8,128)S(1)}, f32[128,400]{1,0:T(8,128)S(1)}, u32[]{:S(2)}, u32[]{:S(2)}) collective-permute-start(f32[128,400]{1,0:T(8,128)S(1)} %divide_subtract_fusion.2), channel_id=1, source_target_pairs={{0,1},{1,2},{2,3},{3,4},{4,5},{5,6},{6,7},{7,8},{8,9},{9,10},{10,1... | collective-permute-start | bytes 614408 | tf_op jit(solution)/shard_map/ppermute | solution.py:11
  77.3 26.5 %collective-permute-start.3 = (f32[128,400]{1,0:T(8,128)S(1)}, f32[128,400]{1,0:T(8,128)S(1)}, u32[]{:S(2)}, u32[]{:S(2)}) collective-permute-start(f32[128,400]{1,0:T(8,128)S(1)} %divide_subtract_fusion.1), channel_id=1, source_target_pairs={{0,32},{32,64},{64,96},{96,128},{128,160},{160,192},{192,224},{224... | collective-permute-start | bytes 614408 | tf_op jit(solution)/shard_map/ppermute | solution.py:11
  90.3 14.2 %collective-permute-start.6 = (f32[128,400]{1,0:T(8,128)S(1)}, f32[128,400]{1,0:T(8,128)S(1)}, u32[]{:S(2)}, u32[]{:S(2)}) collective-permute-start(f32[128,400]{1,0:T(8,128)S(1)} %divide_subtract_fusion), channel_id=1, source_target_pairs={{0,1},{1,2},{2,3},{3,4},{4,5},{5,6},{6,7},{7,8},{8,9},{9,10},{10,1... | collective-permute-start | bytes 614408 | tf_op jit(solution)/shard_map/ppermute | solution.py:11
  92.3 3.9 %collective-permute-start.4 = (f32[128]{0:T(128)S(1)}, f32[128]{0:T(128)S(1)}, u32[]{:S(2)}, u32[]{:S(2)}) collective-permute-start(f32[128]{0:T(128)S(1)} %get-tuple-element.15), channel_id=1, source_target_pairs={{0,32},{32,64},{64,96},{96,128},{128,160},{160,192},{192,224},{224... | collective-permute-start | bytes 1544 | tf_op jit(solution)/shard_map/ppermute | solution.py:11
  94.2 9.5 %collective-permute-start.7 = (f32[128]{0:T(128)S(1)}, f32[128]{0:T(128)S(1)}, u32[]{:S(2)}, u32[]{:S(2)}) collective-permute-start(f32[128]{0:T(128)S(1)} %get-tuple-element.13), channel_id=1, source_target_pairs={{0,1},{1,2},{2,3},{3,4},{4,5},{5,6},{6,7},{7,8},{8,9},{9,10},{10,1... | collective-permute-start | bytes 1544 | tf_op jit(solution)/shard_map/ppermute | solution.py:11
where the time goes:
time: 108 us; the launch traced here: 106 us
  local copies, waits for them, and re-layouts  28.7 us (27%)
  starting transfers between devices  26.2 us (24%)
  other arithmetic  24.7 us (23%)
  waiting for transfers between devices  21.3 us (20%)
  matrix products  4.31 us (4%)
  between operations  1.17 us (1%)
    ppermute x8, starting transfers between devices, from_behind(): lax.ppermute(x, axis, [(i, (i + by) % length) for i in range(length)])  26.2 us
    ppermute x8, waiting for transfers between devices, from_behind(): lax.ppermute(x, axis, [(i, (i + by) % length) for i in range(length)])  21.3 us
    scatter-add x2, other arithmetic, push_rows(): return jnp.zeros_like(target).at[neg_rows].add(grad_negs)  14 us
    unnamed x17, local copies, waits for them, and re-layouts  10.3 us
    gather x4, local copies, waits for them, and re-layouts, on_device(): operator_rows = relations[rel_index[0, 0, rotation]].astype(jnp.float32)  7.48 us
    gather x2, local copies, waits for them, and re-layouts, negative_terms(): negatives_b = target[neg_rows].astype(jnp.bfloat16)  6.95 us
    scatter-add x2, other arithmetic, on_device(): target_grad = push_rows().at[dst_rows].add(pos_grad[:, None] * queries)  2.93 us
    scatter-add x2, other arithmetic, on_device(): jnp.zeros_like(source).at[src_rows]  2.79 us
  transfers between devices with their start and end apart: 8, of which 2 were waited for; matrix products, arithmetic and copies ran while one was open for 32% of the time, Pallas kernels for 0%

commit v1 on v0

v1 whole, which is shorter than its diff:
```python
import functools

import jax
import jax.numpy as jnp
from jax import lax
from jax.experimental import pallas as pl
from jax.experimental.pallas import tpu as pltpu
from jax.sharding import PartitionSpec as P


learning_rate = 0.1
bf16 = jnp.bfloat16
f32 = jnp.float32
PAD = 8
CHUNK = 512

plain = (((1,), (0,)), ((), ()))
left_t = (((0,), (0,)), ((), ()))
right_t = (((1,), (1,)), ((), ()))


def mm(a, b, dims=plain):
    return lax.dot_general(a, b, dims, preferred_element_type=f32)


def two_parts(x):
    hi = x.astype(bf16)
    lo = (x - hi.astype(f32)).astype(bf16)
    return hi, lo


def one_hot(index_row, size):
    at = lax.broadcasted_iota(jnp.int32, (size, index_row.shape[1]), 0)
    return jnp.where(at == index_row, 1.0, 0.0).astype(f32)


def bucket_step(src, src_sums, tgt, tgt_sums, operators, src_rows, dst_rows, neg_rows):
    width, entities = src.shape
    half = width // 2
    negs = neg_rows.shape[1]
    lanes = 128

    pick_s = one_hot(src_rows, entities).astype(bf16)
    pick_d = one_hot(dst_rows, entities).astype(bf16)
    pick_s2 = jnp.concatenate([pick_s, pick_s], axis=0)
    pick_d2 = jnp.concatenate([pick_d, pick_d], axis=0)
    held = one_hot(neg_rows[:, :lanes], entities)
    for k in range(lanes, negs, lanes):
        held = held + one_hot(neg_rows[:, k : k + lanes], entities)
    count_col = jnp.sum(held, axis=1, keepdims=True)
    count_row = mm(jnp.ones((8, lanes), bf16), held.astype(bf16), right_t)[0:1]

    op_re, op_im = operators[:half], operators[half:]
    rows = mm(jnp.concatenate(two_parts(src), axis=1), pick_s2)
    matched = mm(jnp.concatenate(two_parts(tgt), axis=1), pick_d2)
    re, im = rows[:half], rows[half:]
    queries = jnp.concatenate([re * op_re - im * op_im, re * op_im + im * op_re], axis=0)
    positive = jnp.sum(queries * matched, axis=0, keepdims=True)
    pos_grad = -1.0 / (1.0 + jnp.exp(positive))

    queries_b = queries.astype(bf16)
    target_b = tgt.astype(bf16)
    scores = mm(target_b, queries_b, left_t)
    weights = ((1.0 / (1.0 + jnp.exp(-scores))) * (1.0 / negs)).astype(bf16)
    counted = jnp.concatenate(two_parts(weights.astype(f32) * count_col), axis=0)

    pull = mm(jnp.concatenate([target_b, target_b], axis=1), counted)
    grad = pos_grad * matched + pull
    g_re, g_im = grad[:half], grad[half:]
    back = jnp.concatenate([g_re * op_re + g_im * op_im, g_im * op_re - g_re * op_im], axis=0)
    src_grad = mm(
        jnp.concatenate(two_parts(back), axis=1), jnp.concatenate([pick_s, pick_s], axis=1), right_t
    )

    tgt_grad = mm(queries_b, weights, right_t) * count_row + mm(
        jnp.concatenate(two_parts(pos_grad * queries), axis=1),
        jnp.concatenate([pick_d, pick_d], axis=1),
        right_t,
    )

    def adagrad(table, sums, g):
        new_sums = sums + jnp.sum(g * g, axis=0, keepdims=True) * (1.0 / width)
        return table - g * (learning_rate / jnp.sqrt(new_sums)), new_sums

    src, src_sums = adagrad(src, src_sums, src_grad)
    tgt, tgt_sums = adagrad(tgt, tgt_sums, tgt_grad)
    return src, src_sums, tgt, tgt_sums


def store_block(ref, table, sums):
    width = table.shape[0]
    ref[:width, :] = table
    ref[width:, :] = jnp.broadcast_to(sums, (ref.shape[0] - width, sums.shape[1]))


def first_kernel(
    src_ref, src_sums_ref, tgt_ref, tgt_sums_ref, table_ref, s_ref, d_ref, g_ref, n_ref,
    src_out, tgt_out, op_out, table_v, pick_v, sems,
):
    width = src_ref.shape[0]
    types = table_ref.shape[1]
    cut = (width // 2 + 15) // 16 * 16
    parts = [(0, cut), (cut, width - cut)]
    copies = [
        pltpu.make_async_copy(table_ref.at[pl.ds(a, n)], table_v.at[pl.ds(a, n)], sems.at[i])
        for i, (a, n) in enumerate(parts)
    ]
    for copy in copies:
        copy.start()
    wanted = jnp.concatenate([g_ref[0, 0, 0:1, :], g_ref[0, 0, 1:2, :]], axis=1)
    for k in range(0, types, CHUNK):
        n = min(CHUNK, types - k)
        pick_v[k : k + n, :] = one_hot(wanted - k, n).astype(bf16)
    pieces = []
    for copy, (a, n) in zip(copies, parts):
        copy.wait()
        pieces.append(mm(table_v[a : a + n, :], pick_v[...]))
    operators = jnp.concatenate(pieces, axis=0)
    entities = src_ref.shape[1]
    op_out[...] = operators[:, entities:]
    src, src_sums, tgt, tgt_sums = bucket_step(
        src_ref[...], src_sums_ref[0], tgt_ref[...], tgt_sums_ref[0], operators[:, :entities],
        s_ref[0, 0, 0:1, :], d_ref[0, 0, 0:1, :], n_ref[0, 0, 0:1, :],
    )
    store_block(src_out, src, src_sums)
    store_block(tgt_out, tgt, tgt_sums)


def second_kernel(src_ref, tgt_ref, op_ref, s_ref, d_ref, n_ref, src_out, tgt_out):
    width = op_ref.shape[0]
    src, src_sums, tgt, tgt_sums = bucket_step(
        src_ref[:width, :], src_ref[width : width + 1, :], tgt_ref[:width, :], tgt_ref[width : width + 1, :],
        op_ref[...],
        s_ref[0, 0, 1:2, :], d_ref[0, 0, 1:2, :], n_ref[0, 0, 1:2, :],
    )
    store_block(src_out, src, src_sums)
    store_block(tgt_out, tgt, tgt_sums)


def shift(x, axis):
    length = lax.axis_size(axis)
    return lax.ppermute(x, axis, [(i, (i + 1) % length) for i in range(length)])


def on_device(
    source_emb, source_acc, target_emb, target_acc, relations, src_index, dst_index, rel_index, neg_index
):
    src, tgt = source_emb[0, 0].T, target_emb[0, 0].T
    width, entities = src.shape
    types = relations.shape[0]
    block = jax.ShapeDtypeStruct((width + PAD, entities), f32)
    vmem = pl.BlockSpec(memory_space=pltpu.VMEM)
    params = pltpu.CompilerParams(vmem_limit_bytes=40 * 1024 * 1024)

    src, tgt, operators = pl.pallas_call(
        first_kernel,
        name="first_step",
        out_shape=(block, block, jax.ShapeDtypeStruct((width, entities), f32)),
        in_specs=[vmem] * 4 + [pl.BlockSpec(memory_space=pl.ANY)] + [vmem] * 4,
        out_specs=(vmem, vmem, vmem),
        scratch_shapes=[
            pltpu.VMEM((width, types), bf16),
            pltpu.VMEM((types, 2 * entities), bf16),
            pltpu.SemaphoreType.DMA((2,)),
        ],
        compiler_params=params,
    )(src, source_acc, tgt, target_acc, relations.T, src_index, dst_index, rel_index, neg_index)
    src = shift(src, "row")
    tgt = shift(tgt, "col")
    src, tgt = pl.pallas_call(
        second_kernel,
        name="second_step",
        out_shape=(block, block),
        in_specs=[vmem] * 6,
        out_specs=(vmem, vmem),
        compiler_params=params,
    )(src, tgt, operators, src_index, dst_index, neg_index)
    src = shift(src, "row")
    tgt = shift(tgt, "col")
    return (
        src[:width].T[None, None],
        src[width][None, None],
        tgt[:width].T[None, None],
        tgt[width][None, None],
    )


def solution(mesh):
    grid4 = P("row", "col", None, None)
    grid3 = P("row", "col", None)
    return jax.shard_map(
        on_device,
        mesh=mesh,
        in_specs=(grid4, grid3, grid4, grid3, P(), grid4, grid4, grid4, grid4),
        out_specs=(grid4, grid3, grid4, grid3),
        check_vma=False,
    )
```

time: 108 us -> 67.4 us (0.62); the launches traced: 106 us -> 67 us
  other arithmetic: 24.7 us -> 0 us
  local copies, waits for them, and re-layouts: 28.7 us -> 10.3 us
  waiting for transfers between devices: 21.3 us -> 37.8 us
  starting transfers between devices: 26.2 us -> 13.3 us
  Pallas kernels: 0 us -> 4.98 us
  matrix products: 4.31 us -> 0 us
    scatter-add x6 -> x0, other arithmetic: 19.7 us -> none  [the longest x2 14 us: push_rows(): return jnp.zeros_like(target).at[neg_rows].add(grad_negs)]
    gather x12 -> x0, local copies, waits for them, and re-layouts: 17.7 us -> none  [the longest x4 7.48 us: on_device(): operator_rows = relations[rel_index[0, 0, rotation]].astype(jnp.float32)]
    ppermute x8 -> x4, waiting for transfers between devices: 21.3 us -> 37.8 us  [shift(): return lax.ppermute(x, axis, [(i, (i + 1) % length) for i in range(length)])]
    ppermute x8 -> x4, starting transfers between devices: 26.2 us -> 13.3 us  [shift(): return lax.ppermute(x, axis, [(i, (i + 1) % length) for i in range(length)])]
    pallas_call x0 -> x2, Pallas kernels: none -> 4.98 us  [the longest x1 3.94 us: on_device(): pl.pallas_call(first_kernel, name='first_step', out_shape=(block, block,...]
    dot_general x6 -> x0, matrix products: 4.31 us -> none  [the longest x2 2.29 us: push_rows(): jnp.dot(weights.T, queries_b, preferred_element_type=jnp.float32)]
    select_n x4 -> x0, other arithmetic: 3.06 us -> none  [the longest x1 0.79 us: negative_terms(): negatives_b = target[neg_rows].astype(jnp.bfloat16)]
    unnamed x17 -> x18, local copies, waits for them, and re-layouts: 10.3 us -> 7.85 us
  transfers between devices with their start and end apart: 8 -> 4, of which waited for: 2 -> 4; matrix products, arithmetic and copies ran while one was open for 32% -> 2% of each run, Pallas kernels for 0% -> 0%
where the time goes in v1:
time: 67.4 us; the launch traced here: 67 us
  waiting for transfers between devices  37.8 us (56%)
  starting transfers between devices  13.3 us (20%)
  local copies, waits for them, and re-layouts  10.3 us (15%)
  Pallas kernels  4.98 us (7%)
  between operations  0.7 us (1%)
    ppermute x4, waiting for transfers between devices, shift(): return lax.ppermute(x, axis, [(i, (i + 1) % length) for i in range(length)])  37.8 us
    ppermute x4, starting transfers between devices, shift(): return lax.ppermute(x, axis, [(i, (i + 1) % length) for i in range(length)])  13.3 us
    unnamed x18, local copies, waits for them, and re-layouts  7.85 us
    pallas_call x1, Pallas kernels, on_device(): pl.pallas_call(first_kernel, name='first_step', out_shape=(block, block,...  3.94 us
  transfers between devices with their start and end apart: 4, of which 4 were waited for; matrix products, arithmetic and copies ran while one was open for 2% of the time, Pallas kernels for 0%

profile of v1, /device:TPU:1, one launch (start us, length us, event | category | flops | bytes accessed | tf_op | source)
XLA Modules:
  0.0 67.0 jit_solution(5409275086567425916)
XLA Ops:
  0.6 0.0 copy-start
  0.6 1.9 %copy-done = bf16[4131,400]{0,1:T(8,128)(2,1)S(1)} copy-done((bf16[4131,400]{0,1:T(8,128)(2,1)S(1)}, bf16[4131,400]{0,1:T(8,128)(2,1)}, u32[]{:S(2)}) %copy-start) | copy-done | bytes 3304824
  2.6 0.9 %copy-done.1 = f32[1,1,128,400]{2,3,1,0:T(8,128)S(1)} copy-done((f32[1,1,128,400]{2,3,1,0:T(8,128)S(1)}, f32[1,1,128,400]{2,3,1,0:T(8,128)}, u32[]{:S(2)}) %copy-start.1) | copy-done | bytes 204824
  3.5 0.9 %copy-done.2 = f32[1,1,128,400]{2,3,1,0:T(8,128)S(1)} copy-done((f32[1,1,128,400]{2,3,1,0:T(8,128)S(1)}, f32[1,1,128,400]{2,3,1,0:T(8,128)}, u32[]{:S(2)}) %copy-start.2) | copy-done | bytes 204824
  4.5 0.7 %copy-done.3 = s32[1,1,2,1024]{3,2,1,0:T(2,128)S(1)} copy-done((s32[1,1,2,1024]{3,2,1,0:T(2,128)S(1)}, s32[1,1,2,1024]{3,2,1,0:T(2,128)}, u32[]{:S(2)}) %copy-start.3) | copy-done | bytes 8216
  5.2 0.7 %copy-done.4 = s32[1,1,2,128]{3,2,1,0:T(2,128)S(1)} copy-done((s32[1,1,2,128]{3,2,1,0:T(2,128)S(1)}, s32[1,1,2,128]{3,2,1,0:T(2,128)}, u32[]{:S(2)}) %copy-start.4) | copy-done | bytes 1048
  5.8 0.7 %copy-done.5 = s32[1,1,2,128]{3,2,1,0:T(2,128)S(1)} copy-done((s32[1,1,2,128]{3,2,1,0:T(2,128)S(1)}, s32[1,1,2,128]{3,2,1,0:T(2,128)}, u32[]{:S(2)}) %copy-start.5) | copy-done | bytes 1048
  6.5 0.7 %copy-done.6 = s32[1,1,2,128]{3,2,1,0:T(2,128)S(1)} copy-done((s32[1,1,2,128]{3,2,1,0:T(2,128)S(1)}, s32[1,1,2,128]{3,2,1,0:T(2,128)}, u32[]{:S(2)}) %copy-start.6) | copy-done | bytes 1048
  7.2 0.7 copy-done.7
  7.8 0.7 copy-done.8
  8.5 3.9 %first_step.1 = (f32[408,128]{1,0:T(8,128)S(1)}, f32[408,128]{1,0:T(8,128)S(1)}, f32[400,128]{1,0:T(8,128)S(1)}) custom-call(f32[400,128]{1,0:T(8,128)S(1)} %bitcast.20, f32[1,1,128]{2,1,0:T(1,128)S(1)} %copy-done.7, f32[400,128]{1,0:T(8,128)S(1)} %bitcast.21, f32[1,1,128]{2,1,0:T(1,128)S(1)} %copy-done.8, bf16[400,4131]{1,0:T(8,128)(2,1)S(1)} %bitcast.19, ...), custom_call_target="tpu_custom_call" | custom-call | tf_op jit(solution)/shard_map/first_step/pallas_call | solution.py:155
  12.4 4.5 %collective-permute-start = (f32[408,128]{1,0:T(8,128)S(1)}, f32[408,128]{1,0:T(8,128)S(1)}, u32[]{:S(2)}, u32[]{:S(2)}) collective-permute-start(f32[408,128]{1,0:T(8,128)S(1)} %get-tuple-element.9), channel_id=1, source_target_pairs={{0,32},{32,64},{64,96},{96,128},{128,160},{160,192},{192,224},{224... | collective-permute-start | bytes 626696 | tf_op jit(solution)/shard_map/ppermute | solution.py:142
  17.0 4.9 %collective-permute-start.1 = (f32[408,128]{1,0:T(8,128)S(1)}, f32[408,128]{1,0:T(8,128)S(1)}, u32[]{:S(2)}, u32[]{:S(2)}) collective-permute-start(f32[408,128]{1,0:T(8,128)S(1)} %get-tuple-element.10), channel_id=1, source_target_pairs={{0,1},{1,2},{2,3},{3,4},{4,5},{5,6},{6,7},{7,8},{8,9},{9,10},{10,1... | collective-permute-start | bytes 626696 | tf_op jit(solution)/shard_map/ppermute | solution.py:142
  21.9 7.6 %collective-permute-done.src_ref = f32[408,128]{1,0:T(8,128)S(1)} collective-permute-done((f32[408,128]{1,0:T(8,128)S(1)}, f32[408,128]{1,0:T(8,128)S(1)}, u32[]{:S(2)}, u32[]{:S(2)}) %collective-permute-start) | collective-permute-done | bytes 208928 | tf_op jit(solution)/shard_map/ppermute | solution.py:142
  29.5 17.0 %collective-permute-done.1.tgt_ref = f32[408,128]{1,0:T(8,128)S(1)} collective-permute-done((f32[408,128]{1,0:T(8,128)S(1)}, f32[408,128]{1,0:T(8,128)S(1)}, u32[]{:S(2)}, u32[]{:S(2)}) %collective-permute-start.1) | collective-permute-done | bytes 208928 | tf_op jit(solution)/shard_map/ppermute | solution.py:142
  46.5 1.0 %second_step.1 = (f32[408,128]{1,0:T(8,128)S(1)}, f32[408,128]{1,0:T(8,128)S(1)}) custom-call(f32[408,128]{1,0:T(8,128)S(1)} %collective-permute-done.src_ref, f32[408,128]{1,0:T(8,128)S(1)} %collective-permute-done.1.tgt_ref, f32[400,128]{1,0:T(8,128)S(1)} %get-tuple-element.11.op_ref, s32[1,1,2,128]{3,2,1,0:T(2,128)S(1)} %copy-done.4, ...), custom_call_target="tpu_custom_call" | custom-call | tf_op jit(solution)/shard_map/second_step/pallas_call | solution.py:170
  47.5 1.9 %collective-permute-start.2 = (f32[408,128]{1,0:T(8,128)S(1)}, f32[408,128]{1,0:T(8,128)S(1)}, u32[]{:S(2)}, u32[]{:S(2)}) collective-permute-start(f32[408,128]{1,0:T(8,128)S(1)} %get-tuple-element.12), channel_id=1, source_target_pairs={{0,32},{32,64},{64,96},{96,128},{128,160},{160,192},{192,224},{224... | collective-permute-start | bytes 626696 | tf_op jit(solution)/shard_map/ppermute | solution.py:142
  49.5 1.9 %collective-permute-start.3 = (f32[408,128]{1,0:T(8,128)S(1)}, f32[408,128]{1,0:T(8,128)S(1)}, u32[]{:S(2)}, u32[]{:S(2)}) collective-permute-start(f32[408,128]{1,0:T(8,128)S(1)} %get-tuple-element.13), channel_id=1, source_target_pairs={{0,1},{1,2},{2,3},{3,4},{4,5},{5,6},{6,7},{7,8},{8,9},{9,10},{10,1... | collective-permute-start | bytes 626696 | tf_op jit(solution)/shard_map/ppermute | solution.py:142
  51.4 0.8 %collective-permute-done.2 = f32[408,128]{1,0:T(8,128)S(1)} collective-permute-done((f32[408,128]{1,0:T(8,128)S(1)}, f32[408,128]{1,0:T(8,128)S(1)}, u32[]{:S(2)}, u32[]{:S(2)}) %collective-permute-start.2) | collective-permute-done | bytes 208928 | tf_op jit(solution)/shard_map/ppermute | solution.py:142
  52.2 0.7 %slice_bitcast_fusion.1 = f32[1,1,128,400]{2,3,1,0:T(8,128)} fusion(f32[408,128]{1,0:T(8,128)S(1)} %collective-permute-done.2), kind=kLoop, calls=%fused_computation.1 | loop fusion | bytes 409600 | tf_op jit(solution)/shard_map/broadcast_in_dim | solution.py:181
  52.9 0.5 slice_bitcast_fusion.3
  53.4 12.4 %collective-permute-done.3 = f32[408,128]{1,0:T(8,128)S(1)} collective-permute-done((f32[408,128]{1,0:T(8,128)S(1)}, f32[408,128]{1,0:T(8,128)S(1)}, u32[]{:S(2)}, u32[]{:S(2)}) %collective-permute-start.3) | collective-permute-done | bytes 208928 | tf_op jit(solution)/shard_map/ppermute | solution.py:142
  65.8 0.5 slice_bitcast_fusion.2
  66.3 0.7 %slice_bitcast_fusion = f32[1,1,128,400]{2,3,1,0:T(8,128)} fusion(f32[408,128]{1,0:T(8,128)S(1)} %collective-permute-done.3), kind=kLoop, calls=%fused_computation | loop fusion | bytes 409600 | tf_op jit(solution)/shard_map/broadcast_in_dim | solution.py:183
  (8 shorter events, 0.0 us)
Async XLA Ops:
  0.6 2.0 %copy-start = (bf16[4131,400]{0,1:T(8,128)(2,1)S(1)}, bf16[4131,400]{0,1:T(8,128)(2,1)}, u32[]{:S(2)}) copy-start(bf16[4131,400]{0,1:T(8,128)(2,1)} %param.13) | copy-start | bytes 9914404
  2.6 0.9 %copy-start.1 = (f32[1,1,128,400]{2,3,1,0:T(8,128)S(1)}, f32[1,1,128,400]{2,3,1,0:T(8,128)}, u32[]{:S(2)}) copy-start(f32[1,1,128,400]{2,3,1,0:T(8,128)} %param.9) | copy-start | bytes 614404
  3.5 0.9 %copy-start.2 = (f32[1,1,128,400]{2,3,1,0:T(8,128)S(1)}, f32[1,1,128,400]{2,3,1,0:T(8,128)}, u32[]{:S(2)}) copy-start(f32[1,1,128,400]{2,3,1,0:T(8,128)} %param.11) | copy-start | bytes 614404
  4.5 0.7 %copy-start.3 = (s32[1,1,2,1024]{3,2,1,0:T(2,128)S(1)}, s32[1,1,2,1024]{3,2,1,0:T(2,128)}, u32[]{:S(2)}) copy-start(s32[1,1,2,1024]{3,2,1,0:T(2,128)} %n_ref.3) | copy-start | bytes 24580
  5.1 0.7 %copy-start.4 = (s32[1,1,2,128]{3,2,1,0:T(2,128)S(1)}, s32[1,1,2,128]{3,2,1,0:T(2,128)}, u32[]{:S(2)}) copy-start(s32[1,1,2,128]{3,2,1,0:T(2,128)} %s_ref.3) | copy-start | bytes 3076
  5.8 0.7 %copy-start.5 = (s32[1,1,2,128]{3,2,1,0:T(2,128)S(1)}, s32[1,1,2,128]{3,2,1,0:T(2,128)}, u32[]{:S(2)}) copy-start(s32[1,1,2,128]{3,2,1,0:T(2,128)} %d_ref.3) | copy-start | bytes 3076
  6.5 0.7 %copy-start.6 = (s32[1,1,2,128]{3,2,1,0:T(2,128)S(1)}, s32[1,1,2,128]{3,2,1,0:T(2,128)}, u32[]{:S(2)}) copy-start(s32[1,1,2,128]{3,2,1,0:T(2,128)} %g_ref.1) | copy-start | bytes 3076
  7.2 0.7 copy-start.7
  7.8 0.7 copy-start.8
  12.4 17.0 %collective-permute-start = (f32[408,128]{1,0:T(8,128)S(1)}, f32[408,128]{1,0:T(8,128)S(1)}, u32[]{:S(2)}, u32[]{:S(2)}) collective-permute-start(f32[408,128]{1,0:T(8,128)S(1)} %get-tuple-element.9), channel_id=1, source_target_pairs={{0,32},{32,64},{64,96},{96,128},{128,160},{160,192},{192,224},{224... | collective-permute-start | bytes 626696 | tf_op jit(solution)/shard_map/ppermute | solution.py:142
  17.0 29.5 %collective-permute-start.1 = (f32[408,128]{1,0:T(8,128)S(1)}, f32[408,128]{1,0:T(8,128)S(1)}, u32[]{:S(2)}, u32[]{:S(2)}) collective-permute-start(f32[408,128]{1,0:T(8,128)S(1)} %get-tuple-element.10), channel_id=1, source_target_pairs={{0,1},{1,2},{2,3},{3,4},{4,5},{5,6},{6,7},{7,8},{8,9},{9,10},{10,1... | collective-permute-start | bytes 626696 | tf_op jit(solution)/shard_map/ppermute | solution.py:142
  47.5 4.7 %collective-permute-start.2 = (f32[408,128]{1,0:T(8,128)S(1)}, f32[408,128]{1,0:T(8,128)S(1)}, u32[]{:S(2)}, u32[]{:S(2)}) collective-permute-start(f32[408,128]{1,0:T(8,128)S(1)} %get-tuple-element.12), channel_id=1, source_target_pairs={{0,32},{32,64},{64,96},{96,128},{128,160},{160,192},{192,224},{224... | collective-permute-start | bytes 626696 | tf_op jit(solution)/shard_map/ppermute | solution.py:142
  49.5 16.3 %collective-permute-start.3 = (f32[408,128]{1,0:T(8,128)S(1)}, f32[408,128]{1,0:T(8,128)S(1)}, u32[]{:S(2)}, u32[]{:S(2)}) collective-permute-start(f32[408,128]{1,0:T(8,128)S(1)} %get-tuple-element.13), channel_id=1, source_target_pairs={{0,1},{1,2},{2,3},{3,4},{4,5},{5,6},{6,7},{7,8},{8,9},{9,10},{10,1... | collective-permute-start | bytes 626696 | tf_op jit(solution)/shard_map/ppermute | solution.py:142

commit v2 on v1

--- a/solution.py
+++ b/solution.py
@@ -13,6 +13,7 @@
 f32 = jnp.float32
 PAD = 8
 CHUNK = 512
+VMEM_LIMIT = 32 * 1024 * 1024
 
 plain = (((1,), (0,)), ((), ()))
 left_t = (((0,), (0,)), ((), ()))
@@ -37,16 +38,16 @@
 def bucket_step(src, src_sums, tgt, tgt_sums, operators, src_rows, dst_rows, neg_rows):
     width, entities = src.shape
     half = width // 2
-    negs = neg_rows.shape[1]
-    lanes = 128
+    lanes = src_rows.shape[1]
+    negs = lanes * len(neg_rows)
 
     pick_s = one_hot(src_rows, entities).astype(bf16)
     pick_d = one_hot(dst_rows, entities).astype(bf16)
     pick_s2 = jnp.concatenate([pick_s, pick_s], axis=0)
     pick_d2 = jnp.concatenate([pick_d, pick_d], axis=0)
-    held = one_hot(neg_rows[:, :lanes], entities)
-    for k in range(lanes, negs, lanes):
-        held = held + one_hot(neg_rows[:, k : k + lanes], entities)
+    held = one_hot(neg_rows[0], entities)
+    for row in neg_rows[1:]:
+        held = held + one_hot(row, entities)
     count_col = jnp.sum(held, axis=1, keepdims=True)
     count_row = mm(jnp.ones((8, lanes), bf16), held.astype(bf16), right_t)[0:1]
 
@@ -94,47 +95,71 @@
 
 
 def first_kernel(
-    src_ref, src_sums_ref, tgt_ref, tgt_sums_ref, table_ref, s_ref, d_ref, g_ref, n_ref,
-    src_out, tgt_out, op_out, table_v, pick_v, sems,
+    src_hbm, src_sums_hbm, tgt_hbm, tgt_sums_hbm, table_hbm, s_hbm, d_hbm, g_hbm, n_hbm,
+    tgt_out, src_out, op_out, index_out,
+    src_ref, src_sums_ref, tgt_ref, tgt_sums_ref, table_ref, s_ref, d_ref, g_ref, n_ref, pick_ref, sems,
 ):
-    width = src_ref.shape[0]
+    width, entities = src_ref.shape
     types = table_ref.shape[1]
+    lanes = s_ref.shape[3]
     cut = (width // 2 + 15) // 16 * 16
     parts = [(0, cut), (cut, width - cut)]
-    copies = [
-        pltpu.make_async_copy(table_ref.at[pl.ds(a, n)], table_v.at[pl.ds(a, n)], sems.at[i])
-        for i, (a, n) in enumerate(parts)
+    pairs = [(g_hbm, g_ref)]
+    pairs += [(table_hbm.at[pl.ds(a, n)], table_ref.at[pl.ds(a, n)]) for a, n in parts]
+    pairs += [
+        (src_hbm, src_ref), (tgt_hbm, tgt_ref), (s_hbm, s_ref), (d_hbm, d_ref), (n_hbm, n_ref),
+        (src_sums_hbm, src_sums_ref), (tgt_sums_hbm, tgt_sums_ref),
     ]
+    copies = [pltpu.make_async_copy(a, b, sems.at[i]) for i, (a, b) in enumerate(pairs)]
     for copy in copies:
         copy.start()
+    copies[0].wait()
     wanted = jnp.concatenate([g_ref[0, 0, 0:1, :], g_ref[0, 0, 1:2, :]], axis=1)
     for k in range(0, types, CHUNK):
         n = min(CHUNK, types - k)
-        pick_v[k : k + n, :] = one_hot(wanted - k, n).astype(bf16)
+        pick_ref[k : k + n, :] = one_hot(wanted - k, n).astype(bf16)
     pieces = []
-    for copy, (a, n) in zip(copies, parts):
+    for copy, (a, n) in zip(copies[1:3], parts):
         copy.wait()
-        pieces.append(mm(table_v[a : a + n, :], pick_v[...]))
+        pieces.append(mm(table_ref[a : a + n, :], pick_ref[...]))
+    for copy in copies[3:]:
+        copy.wait()
     operators = jnp.concatenate(pieces, axis=0)
-    entities = src_ref.shape[1]
-    op_out[...] = operators[:, entities:]
+    op_out[...] = operators[:, lanes:]
+    index_out[0:1, :] = s_ref[0, 0, 1:2, :]
+    index_out[1:2, :] = d_ref[0, 0, 1:2, :]
+    for k in range(n_ref.shape[3] // lanes):
+        index_out[2 + k : 3 + k, :] = n_ref[0, 0, 1:2, k * lanes : (k + 1) * lanes]
+    negs = [n_ref[0, 0, 0:1, k * lanes : (k + 1) * lanes] for k in range(n_ref.shape[3] // lanes)]
     src, src_sums, tgt, tgt_sums = bucket_step(
-        src_ref[...], src_sums_ref[0], tgt_ref[...], tgt_sums_ref[0], operators[:, :entities],
-        s_ref[0, 0, 0:1, :], d_ref[0, 0, 0:1, :], n_ref[0, 0, 0:1, :],
+        src_ref[...], src_sums_ref[0], tgt_ref[...], tgt_sums_ref[0], operators[:, :lanes],
+        s_ref[0, 0, 0:1, :], d_ref[0, 0, 0:1, :], negs,
     )
     store_block(src_out, src, src_sums)
     store_block(tgt_out, tgt, tgt_sums)
 
 
-def second_kernel(src_ref, tgt_ref, op_ref, s_ref, d_ref, n_ref, src_out, tgt_out):
+def second_kernel(tgt_ref, src_ref, op_ref, index_ref, tgt_out, src_out):
     width = op_ref.shape[0]
+    negs = [index_ref[k : k + 1, :] for k in range(2, index_ref.shape[0])]
     src, src_sums, tgt, tgt_sums = bucket_step(
         src_ref[:width, :], src_ref[width : width + 1, :], tgt_ref[:width, :], tgt_ref[width : width + 1, :],
-        op_ref[...],
-        s_ref[0, 0, 1:2, :], d_ref[0, 0, 1:2, :], n_ref[0, 0, 1:2, :],
+        op_ref[...], index_ref[0:1, :], index_ref[1:2, :], negs,
     )
     store_block(src_out, src, src_sums)
     store_block(tgt_out, tgt, tgt_sums)
+
+
+def unpack_kernel(tgt_ref, src_ref, src_out, src_sums_out, tgt_out, tgt_sums_out, sems):
+    width = src_out.shape[0]
+    pairs = []
+    for ref, out, sums_out in ((src_ref, src_out, src_sums_out), (tgt_ref, tgt_out, tgt_sums_out)):
+        pairs += [(ref.at[pl.ds(0, width)], out), (ref.at[pl.ds(width, 1)], sums_out.at[0])]
+    copies = [pltpu.make_async_copy(a, b, sems.at[i]) for i, (a, b) in enumerate(pairs)]
+    for copy in copies:
+        copy.start()
+    for copy in copies:
+        copy.wait()
 
 
 def shift(x, axis):
@@ -148,41 +173,52 @@
     src, tgt = source_emb[0, 0].T, target_emb[0, 0].T
     width, entities = src.shape
     types = relations.shape[0]
-    block = jax.ShapeDtypeStruct((width + PAD, entities), f32)
+    edges, negs = src_index.shape[3], neg_index.shape[3]
+    block = pltpu.VMEM((width + PAD, entities), f32)
     vmem = pl.BlockSpec(memory_space=pltpu.VMEM)
-    params = pltpu.CompilerParams(vmem_limit_bytes=40 * 1024 * 1024)
-
-    src, tgt, operators = pl.pallas_call(
+    hbm = pl.BlockSpec(memory_space=pltpu.HBM)
+    params = pltpu.CompilerParams(vmem_limit_bytes=VMEM_LIMIT)
+
+    operands = (src, source_acc, tgt, target_acc, relations.T, src_index, dst_index, rel_index, neg_index)
+    tgt, src, operators, index = pl.pallas_call(
         first_kernel,
         name="first_step",
-        out_shape=(block, block, jax.ShapeDtypeStruct((width, entities), f32)),
-        in_specs=[vmem] * 4 + [pl.BlockSpec(memory_space=pl.ANY)] + [vmem] * 4,
-        out_specs=(vmem, vmem, vmem),
-        scratch_shapes=[
-            pltpu.VMEM((width, types), bf16),
-            pltpu.VMEM((types, 2 * entities), bf16),
-            pltpu.SemaphoreType.DMA((2,)),
-        ],
+        out_shape=(
+            block,
+            block,
+            pltpu.VMEM((width, edges), f32),
+            pltpu.VMEM((2 + negs // edges, edges), jnp.int32),
+        ),
+        in_specs=[hbm] * len(operands),
+        out_specs=(vmem,) * 4,
+        scratch_shapes=[pltpu.VMEM(x.shape, x.dtype) for x in operands]
+        + [pltpu.VMEM((types, 2 * edges), bf16), pltpu.SemaphoreType.DMA((len(operands) + 1,))],
         compiler_params=params,
-    )(src, source_acc, tgt, target_acc, relations.T, src_index, dst_index, rel_index, neg_index)
+    )(*[pltpu.with_memory_space_constraint(x, pltpu.HBM) for x in operands])
+    tgt = shift(tgt, "col")
     src = shift(src, "row")
-    tgt = shift(tgt, "col")
-    src, tgt = pl.pallas_call(
+    tgt, src = pl.pallas_call(
         second_kernel,
         name="second_step",
         out_shape=(block, block),
-        in_specs=[vmem] * 6,
+        in_specs=[vmem] * 4,
         out_specs=(vmem, vmem),
         compiler_params=params,
-    )(src, tgt, operators, src_index, dst_index, neg_index)
+    )(tgt, src, operators, index)
+    tgt = shift(tgt, "col")
     src = shift(src, "row")
-    tgt = shift(tgt, "col")
-    return (
-        src[:width].T[None, None],
-        src[width][None, None],
-        tgt[:width].T[None, None],
-        tgt[width][None, None],
-    )
+    table = pltpu.HBM((width, entities), f32)
+    sums = pltpu.HBM((1, 1, entities), f32)
+    src, src_sums, tgt, tgt_sums = pl.pallas_call(
+        unpack_kernel,
+        name="unpack",
+        out_shape=(table, sums, table, sums),
+        in_specs=[vmem] * 2,
+        out_specs=(hbm,) * 4,
+        scratch_shapes=[pltpu.SemaphoreType.DMA((4,))],
+        compiler_params=params,
+    )(tgt, src)
+    return src.T[None, None], src_sums, tgt.T[None, None], tgt_sums
 
 
 def solution(mesh):

time: 67.4 us -> 49.7 us (0.74)
  the two profiles are of different devices: /device:TPU:1 before, /device:TPU:288 now
where the time goes in v2:
time: 49.7 us; the launch traced here: 49.5 us
  waiting for transfers between devices  26.8 us (54%)
  starting transfers between devices  15.4 us (31%)
  Pallas kernels  6.63 us (13%)
  between operations  0.68 us (1%)
    ppermute x4, waiting for transfers between devices, shift(): return lax.ppermute(x, axis, [(i, (i + 1) % length) for i in range(length)])  26.8 us
    ppermute x4, starting transfers between devices, shift(): return lax.ppermute(x, axis, [(i, (i + 1) % length) for i in range(length)])  15.4 us
    pallas_call x1, Pallas kernels, on_device(): pl.pallas_call(first_kernel, name='first_step', out_shape=(block, block,...  4.81 us
    pallas_call x1, Pallas kernels, on_device(): pl.pallas_call(second_kernel, name='second_step', out_shape=(block, block...  1.04 us
  transfers between devices with their start and end apart: 4, of which 4 were waited for; matrix products, arithmetic and copies ran while one was open for 0% of the time, Pallas kernels for 0%

profile of v2, /device:TPU:288, one launch (start us, length us, event | category | flops | bytes accessed | tf_op | source)
XLA Modules:
  0.0 49.5 jit_solution(4501527647252714076)
XLA Ops:
  0.6 4.8 %first_step.1 = (f32[408,128]{1,0:T(8,128)S(1)}, f32[408,128]{1,0:T(8,128)S(1)}, f32[400,128]{1,0:T(8,128)S(1)}, s32[10,128]{1,0:T(8,128)S(1)}) custom-call(f32[400,128]{1,0:T(8,128)} %bitcast.14, f32[1,1,128]{2,1,0:T(1,128)} %src_sums_hbm.1, f32[400,128]{1,0:T(8,128)} %bitcast.15, f32[1,1,128]{2,1,0:T(1,128)} %tgt_sums_hbm.1, bf16[400,4131]{1,0:T(8,128)(2,1)} %bitcast.13, ...), custom_call_target="tpu_custom_call" | custom-call | tf_op jit(solution)/shard_map/first_step/pallas_call | solution.py:183
  5.5 5.2 %collective-permute-start = (f32[408,128]{1,0:T(8,128)S(1)}, f32[408,128]{1,0:T(8,128)S(1)}, u32[]{:S(2)}, u32[]{:S(2)}) collective-permute-start(f32[408,128]{1,0:T(8,128)S(1)} %get-tuple-element.14), channel_id=1, source_target_pairs={{0,1},{1,2},{2,3},{3,4},{4,5},{5,6},{6,7},{7,8},{8,9},{9,10},{10,1... | collective-permute-start | bytes 626696 | tf_op jit(solution)/shard_map/ppermute | solution.py:167
  10.7 1.9 %collective-permute-start.1 = (f32[408,128]{1,0:T(8,128)S(1)}, f32[408,128]{1,0:T(8,128)S(1)}, u32[]{:S(2)}, u32[]{:S(2)}) collective-permute-start(f32[408,128]{1,0:T(8,128)S(1)} %get-tuple-element.15), channel_id=1, source_target_pairs={{0,32},{32,64},{64,96},{96,128},{128,160},{160,192},{192,224},{224... | collective-permute-start | bytes 626696 | tf_op jit(solution)/shard_map/ppermute | solution.py:167
  12.6 2.5 %collective-permute-done.tgt_ref = f32[408,128]{1,0:T(8,128)S(1)} collective-permute-done((f32[408,128]{1,0:T(8,128)S(1)}, f32[408,128]{1,0:T(8,128)S(1)}, u32[]{:S(2)}, u32[]{:S(2)}) %collective-permute-start) | collective-permute-done | bytes 208928 | tf_op jit(solution)/shard_map/ppermute | solution.py:167
  15.0 11.2 %collective-permute-done.1.src_ref = f32[408,128]{1,0:T(8,128)S(1)} collective-permute-done((f32[408,128]{1,0:T(8,128)S(1)}, f32[408,128]{1,0:T(8,128)S(1)}, u32[]{:S(2)}, u32[]{:S(2)}) %collective-permute-start.1) | collective-permute-done | bytes 208928 | tf_op jit(solution)/shard_map/ppermute | solution.py:167
  26.3 1.0 %second_step.1 = (f32[408,128]{1,0:T(8,128)S(1)}, f32[408,128]{1,0:T(8,128)S(1)}) custom-call(f32[408,128]{1,0:T(8,128)S(1)} %collective-permute-done.tgt_ref, f32[408,128]{1,0:T(8,128)S(1)} %collective-permute-done.1.src_ref, f32[400,128]{1,0:T(8,128)S(1)} %get-tuple-element.16.op_ref, s32[10,128]{1,0:T(8,128)S(1)} %get-tuple-element.17.index_ref), custom_call_target="tpu_custom_call" | custom-call | tf_op jit(solution)/shard_map/second_step/pallas_call | solution.py:200
  27.3 6.4 %collective-permute-start.2 = (f32[408,128]{1,0:T(8,128)S(1)}, f32[408,128]{1,0:T(8,128)S(1)}, u32[]{:S(2)}, u32[]{:S(2)}) collective-permute-start(f32[408,128]{1,0:T(8,128)S(1)} %get-tuple-element.18), channel_id=1, source_target_pairs={{0,1},{1,2},{2,3},{3,4},{4,5},{5,6},{6,7},{7,8},{8,9},{9,10},{10,1... | collective-permute-start | bytes 626696 | tf_op jit(solution)/shard_map/ppermute | solution.py:167
  33.7 1.9 %collective-permute-start.3 = (f32[408,128]{1,0:T(8,128)S(1)}, f32[408,128]{1,0:T(8,128)S(1)}, u32[]{:S(2)}, u32[]{:S(2)}) collective-permute-start(f32[408,128]{1,0:T(8,128)S(1)} %get-tuple-element.19), channel_id=1, source_target_pairs={{0,32},{32,64},{64,96},{96,128},{128,160},{160,192},{192,224},{224... | collective-permute-start | bytes 626696 | tf_op jit(solution)/shard_map/ppermute | solution.py:167
  35.6 1.4 %collective-permute-done.2.tgt_ref = f32[408,128]{1,0:T(8,128)S(1)} collective-permute-done((f32[408,128]{1,0:T(8,128)S(1)}, f32[408,128]{1,0:T(8,128)S(1)}, u32[]{:S(2)}, u32[]{:S(2)}) %collective-permute-start.2) | collective-permute-done | bytes 208928 | tf_op jit(solution)/shard_map/ppermute | solution.py:167
  37.0 11.7 %collective-permute-done.3.src_ref = f32[408,128]{1,0:T(8,128)S(1)} collective-permute-done((f32[408,128]{1,0:T(8,128)S(1)}, f32[408,128]{1,0:T(8,128)S(1)}, u32[]{:S(2)}, u32[]{:S(2)}) %collective-permute-start.3) | collective-permute-done | bytes 208928 | tf_op jit(solution)/shard_map/ppermute | solution.py:167
  48.7 0.8 %unpack.1 = (f32[400,128]{1,0:T(8,128)}, f32[1,1,128]{2,1,0:T(1,128)}, f32[400,128]{1,0:T(8,128)}, f32[1,1,128]{2,1,0:T(1,128)}) custom-call(f32[408,128]{1,0:T(8,128)S(1)} %collective-permute-done.2.tgt_ref, f32[408,128]{1,0:T(8,128)S(1)} %collective-permute-done.3.src_ref), custom_call_target="tpu_custom_call" | custom-call | tf_op jit(solution)/shard_map/unpack/pallas_call | solution.py:212
Async XLA Ops:
  5.5 9.6 %collective-permute-start = (f32[408,128]{1,0:T(8,128)S(1)}, f32[408,128]{1,0:T(8,128)S(1)}, u32[]{:S(2)}, u32[]{:S(2)}) collective-permute-start(f32[408,128]{1,0:T(8,128)S(1)} %get-tuple-element.14), channel_id=1, source_target_pairs={{0,1},{1,2},{2,3},{3,4},{4,5},{5,6},{6,7},{7,8},{8,9},{9,10},{10,1... | collective-permute-start | bytes 626696 | tf_op jit(solution)/shard_map/ppermute | solution.py:167
  10.7 15.6 %collective-permute-start.1 = (f32[408,128]{1,0:T(8,128)S(1)}, f32[408,128]{1,0:T(8,128)S(1)}, u32[]{:S(2)}, u32[]{:S(2)}) collective-permute-start(f32[408,128]{1,0:T(8,128)S(1)} %get-tuple-element.15), channel_id=1, source_target_pairs={{0,32},{32,64},{64,96},{96,128},{128,160},{160,192},{192,224},{224... | collective-permute-start | bytes 626696 | tf_op jit(solution)/shard_map/ppermute | solution.py:167
  27.3 9.7 %collective-permute-start.2 = (f32[408,128]{1,0:T(8,128)S(1)}, f32[408,128]{1,0:T(8,128)S(1)}, u32[]{:S(2)}, u32[]{:S(2)}) collective-permute-start(f32[408,128]{1,0:T(8,128)S(1)} %get-tuple-element.18), channel_id=1, source_target_pairs={{0,1},{1,2},{2,3},{3,4},{4,5},{5,6},{6,7},{7,8},{8,9},{9,10},{10,1... | collective-permute-start | bytes 626696 | tf_op jit(solution)/shard_map/ppermute | solution.py:167
  33.7 15.0 %collective-permute-start.3 = (f32[408,128]{1,0:T(8,128)S(1)}, f32[408,128]{1,0:T(8,128)S(1)}, u32[]{:S(2)}, u32[]{:S(2)}) collective-permute-start(f32[408,128]{1,0:T(8,128)S(1)} %get-tuple-element.19), channel_id=1, source_target_pairs={{0,32},{32,64},{64,96},{96,128},{128,160},{160,192},{192,224},{224... | collective-permute-start | bytes 626696 | tf_op jit(solution)/shard_map/ppermute | solution.py:167

commit v3 on v2

--- a/solution.py
+++ b/solution.py
@@ -13,11 +13,16 @@
 f32 = jnp.float32
 PAD = 8
 CHUNK = 512
+FINAL_COST = 50
 VMEM_LIMIT = 32 * 1024 * 1024
 
 plain = (((1,), (0,)), ((), ()))
 left_t = (((0,), (0,)), ((), ()))
 right_t = (((1,), (1,)), ((), ()))
+
+
+def cost(microseconds):
+    return pl.CostEstimate(flops=int(microseconds * 1e9), bytes_accessed=0, transcendentals=0)
 
 
 def mm(a, b, dims=plain):
@@ -92,6 +97,53 @@
     width = table.shape[0]
     ref[:width, :] = table
     ref[width:, :] = jnp.broadcast_to(sums, (ref.shape[0] - width, sums.shape[1]))
+
+
+def crosses(row, rows):
+    return lax.rem(row + 1, rows // 2) == 0
+
+
+def follows_cross(row, rows):
+    return lax.rem(row, rows // 2) == 0
+
+
+def early_first_kernel(*refs):
+    rows = lax.axis_size("row")
+    pl.when(crosses(lax.axis_index("row"), rows))(lambda: first_kernel(*refs))
+
+
+def late_first_kernel(done_tgt, done_op, done_index, *refs):
+    rows = lax.axis_size("row")
+    early = crosses(lax.axis_index("row"), rows)
+    pl.when(jnp.logical_not(early))(lambda: first_kernel(*refs))
+
+    @pl.when(early)
+    def _():
+        tgt_out, _, op_out, index_out = refs[9:13]
+        tgt_out[...] = done_tgt[...]
+        op_out[...] = done_op[...]
+        index_out[...] = done_index[...]
+
+
+def arrived_kernel(_, tgt_ref, out):
+    out[...] = tgt_ref[: out.shape[0], :]
+
+
+def early_second_kernel(_, __, *refs):
+    rows = lax.axis_size("row")
+    pl.when(jnp.logical_not(follows_cross(lax.axis_index("row"), rows)))(lambda: second_kernel(*refs))
+
+
+def late_second_kernel(done_tgt, done_src, *refs):
+    rows = lax.axis_size("row")
+    late = follows_cross(lax.axis_index("row"), rows)
+    pl.when(late)(lambda: second_kernel(*refs))
+
+    @pl.when(jnp.logical_not(late))
+    def _():
+        tgt_out, src_out = refs[-2:]
+        tgt_out[...] = done_tgt[...]
+        src_out[...] = done_src[...]
 
 
 def first_kernel(
@@ -150,11 +202,9 @@
     store_block(tgt_out, tgt, tgt_sums)
 
 
-def unpack_kernel(tgt_ref, src_ref, src_out, src_sums_out, tgt_out, tgt_sums_out, sems):
-    width = src_out.shape[0]
-    pairs = []
-    for ref, out, sums_out in ((src_ref, src_out, src_sums_out), (tgt_ref, tgt_out, tgt_sums_out)):
-        pairs += [(ref.at[pl.ds(0, width)], out), (ref.at[pl.ds(width, 1)], sums_out.at[0])]
+def unpack(ref, out, sums_out, sems):
+    width = out.shape[0]
+    pairs = [(ref.at[pl.ds(0, width)], out), (ref.at[pl.ds(width, 1)], sums_out.at[0])]
     copies = [pltpu.make_async_copy(a, b, sems.at[i]) for i, (a, b) in enumerate(pairs)]
     for copy in copies:
         copy.start()
@@ -162,9 +212,26 @@
         copy.wait()
 
 
-def shift(x, axis):
-    length = lax.axis_size(axis)
-    return lax.ppermute(x, axis, [(i, (i + 1) % length) for i in range(length)])
+def unpack_far_kernel(far_ref, out, sums_out, sems):
+    far = follows_cross(lax.axis_index("row"), lax.axis_size("row"))
+    pl.when(far)(lambda: unpack(far_ref, out, sums_out, sems))
+
+
+def unpack_kernel(_, __, tgt_ref, src_ref, out, sums_out, tgt_out, tgt_sums_out, sems, src_sems):
+    near = jnp.logical_not(follows_cross(lax.axis_index("row"), lax.axis_size("row")))
+    pl.when(near)(lambda: unpack(src_ref, out, sums_out, src_sems))
+    unpack(tgt_ref, tgt_out, tgt_sums_out, sems)
+
+
+def moves(mesh_shape, axis, keep):
+    rows, cols = mesh_shape
+    pairs = []
+    for r in range(rows):
+        for c in range(cols):
+            if keep(r):
+                to = ((r + 1) % rows, c) if axis == "row" else (r, (c + 1) % cols)
+                pairs.append((r * cols + c, to[0] * cols + to[1]))
+    return pairs
 
 
 def on_device(
@@ -180,44 +247,93 @@
     params = pltpu.CompilerParams(vmem_limit_bytes=VMEM_LIMIT)
 
     operands = (src, source_acc, tgt, target_acc, relations.T, src_index, dst_index, rel_index, neg_index)
-    tgt, src, operators, index = pl.pallas_call(
-        first_kernel,
-        name="first_step",
-        out_shape=(
-            block,
-            block,
-            pltpu.VMEM((width, edges), f32),
-            pltpu.VMEM((2 + negs // edges, edges), jnp.int32),
-        ),
-        in_specs=[hbm] * len(operands),
-        out_specs=(vmem,) * 4,
-        scratch_shapes=[pltpu.VMEM(x.shape, x.dtype) for x in operands]
-        + [pltpu.VMEM((types, 2 * edges), bf16), pltpu.SemaphoreType.DMA((len(operands) + 1,))],
+    operands = [pltpu.with_memory_space_constraint(x, pltpu.HBM) for x in operands]
+    mesh_shape = (lax.axis_size("row"), lax.axis_size("col"))
+    half = mesh_shape[0] // 2
+
+    def shift(x, axis, keep):
+        return lax.ppermute(x, ("row", "col"), moves(mesh_shape, axis, keep))
+
+    def to_far(r):
+        return (r + 1) % half == 0
+
+    def from_far(r):
+        return r % half == 0
+
+    def first_step(kernel, done):
+        return pl.pallas_call(
+            kernel,
+            name=kernel.__name__,
+            out_shape=(
+                block,
+                block,
+                pltpu.VMEM((width, edges), f32),
+                pltpu.VMEM((2 + negs // edges, edges), jnp.int32),
+            ),
+            in_specs=[vmem] * len(done) + [hbm] * len(operands),
+            out_specs=(vmem,) * 4,
+            scratch_shapes=[pltpu.VMEM(x.shape, x.dtype) for x in operands]
+            + [pltpu.VMEM((types, 2 * edges), bf16), pltpu.SemaphoreType.DMA((len(operands) + 1,))],
+            compiler_params=params,
+            cost_estimate=cost(0.001),
+        )(*done, *operands)
+
+    def second_step(kernel, *inputs):
+        return pl.pallas_call(
+            kernel,
+            name=kernel.__name__,
+            out_shape=(block, block),
+            in_specs=[vmem] * len(inputs),
+            out_specs=(vmem, vmem),
+            compiler_params=params,
+            cost_estimate=cost(0.001),
+        )(*inputs)
+
+    tgt, src, operators, index = first_step(early_first_kernel, ())
+    far_src = shift(src, "row", to_far)
+    tgt, src, operators, index = first_step(late_first_kernel, (tgt, operators, index))
+    near_tgt = shift(tgt, "col", lambda r: not from_far(r))
+    near_src = shift(src, "row", lambda r: not to_far(r))
+    far_tgt = shift(tgt, "col", from_far)
+    arrived = pl.pallas_call(
+        arrived_kernel,
+        name="arrived",
+        out_shape=pltpu.VMEM((PAD, entities), f32),
+        in_specs=[vmem] * 2,
+        out_specs=vmem,
         compiler_params=params,
-    )(*[pltpu.with_memory_space_constraint(x, pltpu.HBM) for x in operands])
-    tgt = shift(tgt, "col")
-    src = shift(src, "row")
-    tgt, src = pl.pallas_call(
-        second_kernel,
-        name="second_step",
-        out_shape=(block, block),
-        in_specs=[vmem] * 4,
-        out_specs=(vmem, vmem),
-        compiler_params=params,
-    )(tgt, src, operators, index)
-    tgt = shift(tgt, "col")
-    src = shift(src, "row")
+        cost_estimate=cost(FINAL_COST),
+    )(far_src, near_tgt)
+    tgt, src = second_step(early_second_kernel, arrived, far_src, near_tgt, near_src, operators, index)
+    early_src = src
+    tgt, src = second_step(late_second_kernel, tgt, src, far_tgt, far_src, operators, index)
+    tgt = shift(tgt, "col", lambda r: True)
+    src = shift(src, "row", lambda r: not to_far(r))
+    far_src_out = shift(early_src, "row", to_far)
     table = pltpu.HBM((width, entities), f32)
     sums = pltpu.HBM((1, 1, entities), f32)
+
+    out = pl.pallas_call(
+        unpack_far_kernel,
+        name="unpack_far",
+        out_shape=(table, sums),
+        in_specs=[vmem],
+        out_specs=(hbm,) * 2,
+        scratch_shapes=[pltpu.SemaphoreType.DMA((2,))],
+        compiler_params=params,
+        cost_estimate=cost(FINAL_COST),
+    )(far_src_out)
     src, src_sums, tgt, tgt_sums = pl.pallas_call(
         unpack_kernel,
         name="unpack",
         out_shape=(table, sums, table, sums),
-        in_specs=[vmem] * 2,
+        in_specs=[hbm, hbm, vmem, vmem],
         out_specs=(hbm,) * 4,
-        scratch_shapes=[pltpu.SemaphoreType.DMA((4,))],
+        input_output_aliases={0: 0, 1: 1},
+        scratch_shapes=[pltpu.SemaphoreType.DMA((2,))] * 2,
         compiler_params=params,
-    )(tgt, src)
+        cost_estimate=cost(FINAL_COST),
+    )(*out, tgt, src)
     return src.T[None, None], src_sums, tgt.T[None, None], tgt_sums
 
 

time: 49.7 us -> 55.7 us (1.12)
  the two profiles are of different devices: /device:TPU:288 before, /device:TPU:1 now
where the time goes in v3:
time: 55.7 us; the launch traced here: 55.4 us
  waiting for transfers between devices  31.7 us (57%)
  starting transfers between devices  15.6 us (28%)
  Pallas kernels  7.46 us (13%)
  between operations  0.75 us (1%)
    ppermute x7, waiting for transfers between devices, shift(): return lax.ppermute(x, ('row', 'col'), moves(mesh_shape, axis, keep))  31.7 us
    ppermute x7, starting transfers between devices, shift(): return lax.ppermute(x, ('row', 'col'), moves(mesh_shape, axis, keep))  15.6 us
    pallas_call x2, Pallas kernels, first_step(): pl.pallas_call(kernel, name=kernel.__name__, out_shape=(block, block, plt...  4.94 us
    pallas_call x1, Pallas kernels, on_device(): pl.pallas_call(unpack_kernel, name='unpack', out_shape=(table, sums, tabl...  1.4 us
  transfers between devices with their start and end apart: 7, of which 2 were waited for; matrix products, arithmetic and copies ran while one was open for 0% of the time, Pallas kernels for 11%

profile of v3, /device:TPU:1, one launch (start us, length us, event | category | flops | bytes accessed | tf_op | source)
XLA Modules:
  0.0 55.4 jit_solution(14583373124998765015)
XLA Ops:
  0.6 0.1 early_first_kernel.1
  0.8 0.7 %collective-permute-start = (f32[408,128]{1,0:T(8,128)S(1)}, f32[408,128]{1,0:T(8,128)S(1)}, u32[]{:S(2)}, u32[]{:S(2)}) collective-permute-start(f32[408,128]{1,0:T(8,128)S(1)} %get-tuple-element.22), channel_id=1, source_target_pairs={{480,512},{481,513},{482,514},{483,515},{484,516},{485,517},{486,5... | collective-permute-start | bytes 626696 | tf_op jit(solution)/shard_map/ppermute | solution.py:255
  1.4 4.8 %late_first_kernel.1 = (f32[408,128]{1,0:T(8,128)S(1)}, f32[408,128]{1,0:T(8,128)S(1)}, f32[400,128]{1,0:T(8,128)S(1)}, s32[10,128]{1,0:T(8,128)S(1)}) custom-call(f32[408,128]{1,0:T(8,128)S(1)} %get-tuple-element.23.done_tgt, f32[400,128]{1,0:T(8,128)S(1)} %get-tuple-element.24.done_op, s32[10,128]{1,0:T(8,128)S(1)} %get-tuple-element.25.done_index, ...), custom_call_target="tpu_custom_call" | custom-call | flops 1000000 | tf_op jit(solution)/shard_map/late_first_kernel/pallas_call | solution.py:264
  6.3 5.7 %collective-permute-start.1 = (f32[408,128]{1,0:T(8,128)S(1)}, f32[408,128]{1,0:T(8,128)S(1)}, u32[]{:S(2)}, u32[]{:S(2)}) collective-permute-start(f32[408,128]{1,0:T(8,128)S(1)} %get-tuple-element.26), channel_id=1, source_target_pairs={{32,33},{33,34},{34,35},{35,36},{36,37},{37,38},{38,39},{39,40},{4... | collective-permute-start | bytes 626696 | tf_op jit(solution)/shard_map/ppermute | solution.py:255
  12.0 0.7 %collective-permute-start.4 = (f32[408,128]{1,0:T(8,128)S(1)}, f32[408,128]{1,0:T(8,128)S(1)}, u32[]{:S(2)}, u32[]{:S(2)}) collective-permute-start(f32[408,128]{1,0:T(8,128)S(1)} %get-tuple-element.26), channel_id=1, source_target_pairs={{0,1},{1,2},{2,3},{3,4},{4,5},{5,6},{6,7},{7,8},{8,9},{9,10},{10,1... | collective-permute-start | bytes 626696 | tf_op jit(solution)/shard_map/ppermute | solution.py:255
  12.7 4.0 %collective-permute-start.2 = (f32[408,128]{1,0:T(8,128)S(1)}, f32[408,128]{1,0:T(8,128)S(1)}, u32[]{:S(2)}, u32[]{:S(2)}) collective-permute-start(f32[408,128]{1,0:T(8,128)S(1)} %get-tuple-element.27), channel_id=1, source_target_pairs={{0,32},{1,33},{2,34},{3,35},{4,36},{5,37},{6,38},{7,39},{8,40},{9,... | collective-permute-start | bytes 626696 | tf_op jit(solution)/shard_map/ppermute | solution.py:255
  16.7 0.0 collective-permute-done._.__.refs_1_
  16.7 21.4 %collective-permute-done.1.tgt_ref.refs_0_ = f32[408,128]{1,0:T(8,128)S(1)} collective-permute-done((f32[408,128]{1,0:T(8,128)S(1)}, f32[408,128]{1,0:T(8,128)S(1)}, u32[]{:S(2)}, u32[]{:S(2)}) %collective-permute-start.1) | collective-permute-done | bytes 208928 | tf_op jit(solution)/shard_map/ppermute | solution.py:255
  38.0 0.0 collective-permute-done.2.refs_1_
  38.0 1.0 %early_second_kernel.1 = (f32[408,128]{1,0:T(8,128)S(1)}, f32[408,128]{1,0:T(8,128)S(1)}) custom-call(f32[8,128]{1,0:T(8,128)S(1)} %arrived.1._, f32[408,128]{1,0:T(8,128)S(1)} %collective-permute-done._.__.refs_1_, f32[408,128]{1,0:T(8,128)S(1)} %collective-permute-done.1.tgt_ref.refs_0_, f32[408,128]{1,0:T(8,128)S(1)} %collective-permute-done.2.refs_1_, ...), custom_call_target="tpu_custom_call" | custom-call | flops 1000000 | tf_op jit(solution)/shard_map/early_second_kernel/pallas_call | solution.py:282
  39.1 0.7 %collective-permute-start.3 = (f32[408,128]{1,0:T(8,128)S(1)}, f32[408,128]{1,0:T(8,128)S(1)}, u32[]{:S(2)}, u32[]{:S(2)}) collective-permute-start(f32[408,128]{1,0:T(8,128)S(1)} %get-tuple-element.30.done_src), channel_id=1, source_target_pairs={{480,512},{481,513},{482,514},{483,515},{484,516},{485,517},{486,5... | collective-permute-start | bytes 626696 | tf_op jit(solution)/shard_map/ppermute | solution.py:255
  39.8 0.0 collective-permute-done.4.refs_0_
  39.8 1.9 %collective-permute-start.5 = (f32[408,128]{1,0:T(8,128)S(1)}, f32[408,128]{1,0:T(8,128)S(1)}, u32[]{:S(2)}, u32[]{:S(2)}) collective-permute-start(f32[408,128]{1,0:T(8,128)S(1)} %get-tuple-element.34), channel_id=1, source_target_pairs={{0,1},{1,2},{2,3},{3,4},{4,5},{5,6},{6,7},{7,8},{8,9},{9,10},{10,1... | collective-permute-start | bytes 626696 | tf_op jit(solution)/shard_map/ppermute | solution.py:255
  41.8 1.9 %collective-permute-start.6 = (f32[408,128]{1,0:T(8,128)S(1)}, f32[408,128]{1,0:T(8,128)S(1)}, u32[]{:S(2)}, u32[]{:S(2)}) collective-permute-start(f32[408,128]{1,0:T(8,128)S(1)} %get-tuple-element.35), channel_id=1, source_target_pairs={{0,32},{1,33},{2,34},{3,35},{4,36},{5,37},{6,38},{7,39},{8,40},{9,... | collective-permute-start | bytes 626696 | tf_op jit(solution)/shard_map/ppermute | solution.py:255
  43.7 0.0 collective-permute-done.3.far_ref
  43.8 10.3 %collective-permute-done.5.tgt_ref = f32[408,128]{1,0:T(8,128)S(1)} collective-permute-done((f32[408,128]{1,0:T(8,128)S(1)}, f32[408,128]{1,0:T(8,128)S(1)}, u32[]{:S(2)}, u32[]{:S(2)}) %collective-permute-start.5) | collective-permute-done | bytes 208928 | tf_op jit(solution)/shard_map/ppermute | solution.py:255
  54.0 0.0 collective-permute-done.6.src_ref
  54.0 1.4 %unpack.1 = (f32[400,128]{1,0:T(8,128)}, f32[1,1,128]{2,1,0:T(1,128)}, f32[400,128]{1,0:T(8,128)}, f32[1,1,128]{2,1,0:T(1,128)}) custom-call(f32[400,128]{1,0:T(8,128)} %get-tuple-element.31._, f32[1,1,128]{2,1,0:T(1,128)} %get-tuple-element.32.__, f32[408,128]{1,0:T(8,128)S(1)} %collective-permute-done.5.tgt_ref, ...), custom_call_target="tpu_custom_call", output_to_operand_aliasing={{0}: (0, {}), {1}: (1, {})} | custom-call | flops 49999998976 | tf_op jit(solution)/shard_map/unpack/pallas_call | solution.py:326
  (3 shorter events, 0.1 us)
Async XLA Ops:
  0.8 15.9 %collective-permute-start = (f32[408,128]{1,0:T(8,128)S(1)}, f32[408,128]{1,0:T(8,128)S(1)}, u32[]{:S(2)}, u32[]{:S(2)}) collective-permute-start(f32[408,128]{1,0:T(8,128)S(1)} %get-tuple-element.22), channel_id=1, source_target_pairs={{480,512},{481,513},{482,514},{483,515},{484,516},{485,517},{486,5... | collective-permute-start | bytes 626696 | tf_op jit(solution)/shard_map/ppermute | solution.py:255
  6.3 31.8 %collective-permute-start.1 = (f32[408,128]{1,0:T(8,128)S(1)}, f32[408,128]{1,0:T(8,128)S(1)}, u32[]{:S(2)}, u32[]{:S(2)}) collective-permute-start(f32[408,128]{1,0:T(8,128)S(1)} %get-tuple-element.26), channel_id=1, source_target_pairs={{32,33},{33,34},{34,35},{35,36},{36,37},{37,38},{38,39},{39,40},{4... | collective-permute-start | bytes 626696 | tf_op jit(solution)/shard_map/ppermute | solution.py:255
  12.0 27.8 %collective-permute-start.4 = (f32[408,128]{1,0:T(8,128)S(1)}, f32[408,128]{1,0:T(8,128)S(1)}, u32[]{:S(2)}, u32[]{:S(2)}) collective-permute-start(f32[408,128]{1,0:T(8,128)S(1)} %get-tuple-element.26), channel_id=1, source_target_pairs={{0,1},{1,2},{2,3},{3,4},{4,5},{5,6},{6,7},{7,8},{8,9},{9,10},{10,1... | collective-permute-start | bytes 626696 | tf_op jit(solution)/shard_map/ppermute | solution.py:255
  12.7 25.4 %collective-permute-start.2 = (f32[408,128]{1,0:T(8,128)S(1)}, f32[408,128]{1,0:T(8,128)S(1)}, u32[]{:S(2)}, u32[]{:S(2)}) collective-permute-start(f32[408,128]{1,0:T(8,128)S(1)} %get-tuple-element.27), channel_id=1, source_target_pairs={{0,32},{1,33},{2,34},{3,35},{4,36},{5,37},{6,38},{7,39},{8,40},{9,... | collective-permute-start | bytes 626696 | tf_op jit(solution)/shard_map/ppermute | solution.py:255
  39.1 4.6 %collective-permute-start.3 = (f32[408,128]{1,0:T(8,128)S(1)}, f32[408,128]{1,0:T(8,128)S(1)}, u32[]{:S(2)}, u32[]{:S(2)}) collective-permute-start(f32[408,128]{1,0:T(8,128)S(1)} %get-tuple-element.30.done_src), channel_id=1, source_target_pairs={{480,512},{481,513},{482,514},{483,515},{484,516},{485,517},{486,5... | collective-permute-start | bytes 626696 | tf_op jit(solution)/shard_map/ppermute | solution.py:255
  39.8 14.2 %collective-permute-start.5 = (f32[408,128]{1,0:T(8,128)S(1)}, f32[408,128]{1,0:T(8,128)S(1)}, u32[]{:S(2)}, u32[]{:S(2)}) collective-permute-start(f32[408,128]{1,0:T(8,128)S(1)} %get-tuple-element.34), channel_id=1, source_target_pairs={{0,1},{1,2},{2,3},{3,4},{4,5},{5,6},{6,7},{7,8},{8,9},{9,10},{10,1... | collective-permute-start | bytes 626696 | tf_op jit(solution)/shard_map/ppermute | solution.py:255
  41.8 12.3 %collective-permute-start.6 = (f32[408,128]{1,0:T(8,128)S(1)}, f32[408,128]{1,0:T(8,128)S(1)}, u32[]{:S(2)}, u32[]{:S(2)}) collective-permute-start(f32[408,128]{1,0:T(8,128)S(1)} %get-tuple-element.35), channel_id=1, source_target_pairs={{0,32},{1,33},{2,34},{3,35},{4,36},{5,37},{6,38},{7,39},{8,40},{9,... | collective-permute-start | bytes 626696 | tf_op jit(solution)/shard_map/ppermute | solution.py:255

commit v4 on v2

--- a/solution.py
+++ b/solution.py
@@ -13,6 +13,8 @@
 f32 = jnp.float32
 PAD = 8
 CHUNK = 512
+RUN = 8
+LATE_FROM = 5
 VMEM_LIMIT = 32 * 1024 * 1024
 
 plain = (((1,), (0,)), ((), ()))
@@ -96,7 +98,7 @@
 
 def first_kernel(
     src_hbm, src_sums_hbm, tgt_hbm, tgt_sums_hbm, table_hbm, s_hbm, d_hbm, g_hbm, n_hbm,
-    tgt_out, src_out, op_out, index_out,
+    tgt_a_out, src_out, tgt_b_out, op_out, index_out,
     src_ref, src_sums_ref, tgt_ref, tgt_sums_ref, table_ref, s_ref, d_ref, g_ref, n_ref, pick_ref, sems,
 ):
     width, entities = src_ref.shape
@@ -136,35 +138,57 @@
         s_ref[0, 0, 0:1, :], d_ref[0, 0, 0:1, :], negs,
     )
     store_block(src_out, src, src_sums)
-    store_block(tgt_out, tgt, tgt_sums)
-
-
-def second_kernel(tgt_ref, src_ref, op_ref, index_ref, tgt_out, src_out):
+    store_block(tgt_a_out, tgt, tgt_sums)
+    store_block(tgt_b_out, tgt, tgt_sums)
+
+
+def second_kernel(tgt_a_ref, src_ref, tgt_b_ref, op_ref, index_ref, tgt_a_out, src_out, tgt_b_out):
     width = op_ref.shape[0]
+    tgt = jnp.where(from_late(lax.axis_index("col")), tgt_a_ref[...], tgt_b_ref[...])
     negs = [index_ref[k : k + 1, :] for k in range(2, index_ref.shape[0])]
     src, src_sums, tgt, tgt_sums = bucket_step(
-        src_ref[:width, :], src_ref[width : width + 1, :], tgt_ref[:width, :], tgt_ref[width : width + 1, :],
+        src_ref[:width, :], src_ref[width : width + 1, :], tgt[:width, :], tgt[width : width + 1, :],
         op_ref[...], index_ref[0:1, :], index_ref[1:2, :], negs,
     )
     store_block(src_out, src, src_sums)
-    store_block(tgt_out, tgt, tgt_sums)
-
-
-def unpack_kernel(tgt_ref, src_ref, src_out, src_sums_out, tgt_out, tgt_sums_out, sems):
+    store_block(tgt_a_out, tgt, tgt_sums)
+    store_block(tgt_b_out, tgt, tgt_sums)
+
+
+def late(col):
+    return col % RUN >= LATE_FROM
+
+
+def from_late(col):
+    return lax.rem(col + RUN - 1, RUN) >= LATE_FROM
+
+
+def unpack_kernel(tgt_a_ref, src_ref, tgt_b_ref, src_out, src_sums_out, tgt_out, tgt_sums_out, sems):
     width = src_out.shape[0]
-    pairs = []
-    for ref, out, sums_out in ((src_ref, src_out, src_sums_out), (tgt_ref, tgt_out, tgt_sums_out)):
-        pairs += [(ref.at[pl.ds(0, width)], out), (ref.at[pl.ds(width, 1)], sums_out.at[0])]
-    copies = [pltpu.make_async_copy(a, b, sems.at[i]) for i, (a, b) in enumerate(pairs)]
-    for copy in copies:
-        copy.start()
-    for copy in copies:
-        copy.wait()
-
-
-def shift(x, axis):
+
+    def send(ref, out, sums_out, first):
+        pairs = [(ref.at[pl.ds(0, width)], out), (ref.at[pl.ds(width, 1)], sums_out.at[0])]
+        return [pltpu.make_async_copy(a, b, sems.at[first + i]) for i, (a, b) in enumerate(pairs)]
+
+    def move(tgt_ref):
+        copies = send(src_ref, src_out, src_sums_out, 0) + send(tgt_ref, tgt_out, tgt_sums_out, 2)
+        for copy in copies:
+            copy.start()
+        for copy in copies:
+            copy.wait()
+
+    a = from_late(lax.axis_index("col"))
+    pl.when(a)(lambda: move(tgt_a_ref))
+    pl.when(jnp.logical_not(a))(lambda: move(tgt_b_ref))
+
+
+def shift(x, axis, keep=None):
     length = lax.axis_size(axis)
-    return lax.ppermute(x, axis, [(i, (i + 1) % length) for i in range(length)])
+    return lax.ppermute(x, axis, [(i, (i + 1) % length) for i in range(length) if keep is None or keep(i)])
+
+
+def early(col):
+    return not late(col)
 
 
 def on_device(
@@ -180,44 +204,47 @@
     params = pltpu.CompilerParams(vmem_limit_bytes=VMEM_LIMIT)
 
     operands = (src, source_acc, tgt, target_acc, relations.T, src_index, dst_index, rel_index, neg_index)
-    tgt, src, operators, index = pl.pallas_call(
+    tgt_a, src, tgt_b, operators, index = pl.pallas_call(
         first_kernel,
         name="first_step",
         out_shape=(
+            block,
             block,
             block,
             pltpu.VMEM((width, edges), f32),
             pltpu.VMEM((2 + negs // edges, edges), jnp.int32),
         ),
         in_specs=[hbm] * len(operands),
-        out_specs=(vmem,) * 4,
+        out_specs=(vmem,) * 5,
         scratch_shapes=[pltpu.VMEM(x.shape, x.dtype) for x in operands]
         + [pltpu.VMEM((types, 2 * edges), bf16), pltpu.SemaphoreType.DMA((len(operands) + 1,))],
         compiler_params=params,
     )(*[pltpu.with_memory_space_constraint(x, pltpu.HBM) for x in operands])
-    tgt = shift(tgt, "col")
+    tgt_a = shift(tgt_a, "col", late)
     src = shift(src, "row")
-    tgt, src = pl.pallas_call(
+    tgt_b = shift(tgt_b, "col", early)
+    tgt_a, src, tgt_b = pl.pallas_call(
         second_kernel,
         name="second_step",
-        out_shape=(block, block),
-        in_specs=[vmem] * 4,
-        out_specs=(vmem, vmem),
+        out_shape=(block, block, block),
+        in_specs=[vmem] * 5,
+        out_specs=(vmem,) * 3,
         compiler_params=params,
-    )(tgt, src, operators, index)
-    tgt = shift(tgt, "col")
+    )(tgt_a, src, tgt_b, operators, index)
+    tgt_a = shift(tgt_a, "col", late)
     src = shift(src, "row")
+    tgt_b = shift(tgt_b, "col", early)
     table = pltpu.HBM((width, entities), f32)
     sums = pltpu.HBM((1, 1, entities), f32)
     src, src_sums, tgt, tgt_sums = pl.pallas_call(
         unpack_kernel,
         name="unpack",
         out_shape=(table, sums, table, sums),
-        in_specs=[vmem] * 2,
+        in_specs=[vmem] * 3,
         out_specs=(hbm,) * 4,
         scratch_shapes=[pltpu.SemaphoreType.DMA((4,))],
         compiler_params=params,
-    )(tgt, src)
+    )(tgt_a, src, tgt_b)
     return src.T[None, None], src_sums, tgt.T[None, None], tgt_sums
 
 

time: 49.7 us -> 48.7 us (0.980)
  the two profiles are of different devices: /device:TPU:288 before, /device:TPU:80 now
where the time goes in v4:
time: 48.7 us; the launch traced here: 48.5 us
  waiting for transfers between devices  28.8 us (59%)
  starting transfers between devices  12.3 us (25%)
  Pallas kernels  6.67 us (14%)
  between operations  0.7 us (1%)
    ppermute x6, waiting for transfers between devices, shift(): lax.ppermute(x, axis, [(i, (i + 1) % length) for i in range(length) if ke...  28.8 us
    ppermute x6, starting transfers between devices, shift(): lax.ppermute(x, axis, [(i, (i + 1) % length) for i in range(length) if ke...  12.3 us
    pallas_call x1, Pallas kernels, on_device(): pl.pallas_call(first_kernel, name='first_step', out_shape=(block, block,...  4.82 us
    pallas_call x1, Pallas kernels, on_device(): pl.pallas_call(second_kernel, name='second_step', out_shape=(block, block...  1.06 us
  transfers between devices with their start and end apart: 6, of which 3 were waited for; matrix products, arithmetic and copies ran while one was open for 0% of the time, Pallas kernels for 0%

profile of v4, /device:TPU:80, one launch (start us, length us, event | category | flops | bytes accessed | tf_op | source)
XLA Modules:
  0.0 48.5 jit_solution(17182322500911595339)
XLA Ops:
  0.6 4.8 %first_step.1 = (f32[408,128]{1,0:T(8,128)S(1)}, f32[408,128]{1,0:T(8,128)S(1)}, f32[408,128]{1,0:T(8,128)S(1)}, f32[400,128]{1,0:T(8,128)S(1)}, s32[10,128]{1,0:T(8,128)S(1)}) custom-call(f32[400,128]{1,0:T(8,128)} %bitcast.14, f32[1,1,128]{2,1,0:T(1,128)} %src_sums_hbm.1, f32[400,128]{1,0:T(8,128)} %bitcast.15, f32[1,1,128]{2,1,0:T(1,128)} %tgt_sums_hbm.1, ...), custom_call_target="tpu_custom_call" | custom-call | tf_op jit(solution)/shard_map/first_step/pallas_call | solution.py:207
  5.5 1.3 %collective-permute-start = (f32[408,128]{1,0:T(8,128)S(1)}, f32[408,128]{1,0:T(8,128)S(1)}, u32[]{:S(2)}, u32[]{:S(2)}) collective-permute-start(f32[408,128]{1,0:T(8,128)S(1)} %get-tuple-element.16), channel_id=1, source_target_pairs={{5,6},{6,7},{7,8},{13,14},{14,15},{15,16},{21,22},{22,23},{23,24},... | collective-permute-start | bytes 626696 | tf_op jit(solution)/shard_map/ppermute | solution.py:187
  6.8 1.9 %collective-permute-start.1 = (f32[408,128]{1,0:T(8,128)S(1)}, f32[408,128]{1,0:T(8,128)S(1)}, u32[]{:S(2)}, u32[]{:S(2)}) collective-permute-start(f32[408,128]{1,0:T(8,128)S(1)} %get-tuple-element.17), channel_id=1, source_target_pairs={{0,32},{32,64},{64,96},{96,128},{128,160},{160,192},{192,224},{224... | collective-permute-start | bytes 626696 | tf_op jit(solution)/shard_map/ppermute | solution.py:187
  8.7 4.6 %collective-permute-start.2 = (f32[408,128]{1,0:T(8,128)S(1)}, f32[408,128]{1,0:T(8,128)S(1)}, u32[]{:S(2)}, u32[]{:S(2)}) collective-permute-start(f32[408,128]{1,0:T(8,128)S(1)} %get-tuple-element.18), channel_id=1, source_target_pairs={{0,1},{1,2},{2,3},{3,4},{4,5},{8,9},{9,10},{10,11},{11,12},{12,13}... | collective-permute-start | bytes 626696 | tf_op jit(solution)/shard_map/ppermute | solution.py:187
  13.3 17.6 %collective-permute-done.tgt_a_ref = f32[408,128]{1,0:T(8,128)S(1)} collective-permute-done((f32[408,128]{1,0:T(8,128)S(1)}, f32[408,128]{1,0:T(8,128)S(1)}, u32[]{:S(2)}, u32[]{:S(2)}) %collective-permute-start) | collective-permute-done | bytes 208928 | tf_op jit(solution)/shard_map/ppermute | solution.py:187
  30.8 0.0 collective-permute-done.1.src_ref
  30.8 0.0 collective-permute-done.2.tgt_b_ref
  30.9 1.1 %second_step.1 = (f32[408,128]{1,0:T(8,128)S(1)}, f32[408,128]{1,0:T(8,128)S(1)}, f32[408,128]{1,0:T(8,128)S(1)}) custom-call(f32[408,128]{1,0:T(8,128)S(1)} %collective-permute-done.tgt_a_ref, f32[408,128]{1,0:T(8,128)S(1)} %collective-permute-done.1.src_ref, f32[408,128]{1,0:T(8,128)S(1)} %collective-permute-done.2.tgt_b_ref, ...), custom_call_target="tpu_custom_call" | custom-call | tf_op jit(solution)/shard_map/second_step/pallas_call | solution.py:226
  31.9 1.3 %collective-permute-start.3 = (f32[408,128]{1,0:T(8,128)S(1)}, f32[408,128]{1,0:T(8,128)S(1)}, u32[]{:S(2)}, u32[]{:S(2)}) collective-permute-start(f32[408,128]{1,0:T(8,128)S(1)} %get-tuple-element.21), channel_id=1, source_target_pairs={{5,6},{6,7},{7,8},{13,14},{14,15},{15,16},{21,22},{22,23},{23,24},... | collective-permute-start | bytes 626696 | tf_op jit(solution)/shard_map/ppermute | solution.py:187
  33.2 1.9 %collective-permute-start.4 = (f32[408,128]{1,0:T(8,128)S(1)}, f32[408,128]{1,0:T(8,128)S(1)}, u32[]{:S(2)}, u32[]{:S(2)}) collective-permute-start(f32[408,128]{1,0:T(8,128)S(1)} %get-tuple-element.22), channel_id=1, source_target_pairs={{0,32},{32,64},{64,96},{96,128},{128,160},{160,192},{192,224},{224... | collective-permute-start | bytes 626696 | tf_op jit(solution)/shard_map/ppermute | solution.py:187
  35.1 1.3 %collective-permute-start.5 = (f32[408,128]{1,0:T(8,128)S(1)}, f32[408,128]{1,0:T(8,128)S(1)}, u32[]{:S(2)}, u32[]{:S(2)}) collective-permute-start(f32[408,128]{1,0:T(8,128)S(1)} %get-tuple-element.23), channel_id=1, source_target_pairs={{0,1},{1,2},{2,3},{3,4},{4,5},{8,9},{9,10},{10,11},{11,12},{12,13}... | collective-permute-start | bytes 626696 | tf_op jit(solution)/shard_map/ppermute | solution.py:187
  36.5 8.7 %collective-permute-done.3.tgt_a_ref = f32[408,128]{1,0:T(8,128)S(1)} collective-permute-done((f32[408,128]{1,0:T(8,128)S(1)}, f32[408,128]{1,0:T(8,128)S(1)}, u32[]{:S(2)}, u32[]{:S(2)}) %collective-permute-start.3) | collective-permute-done | bytes 208928 | tf_op jit(solution)/shard_map/ppermute | solution.py:187
  45.2 2.5 %collective-permute-done.4.src_ref = f32[408,128]{1,0:T(8,128)S(1)} collective-permute-done((f32[408,128]{1,0:T(8,128)S(1)}, f32[408,128]{1,0:T(8,128)S(1)}, u32[]{:S(2)}, u32[]{:S(2)}) %collective-permute-start.4) | collective-permute-done | bytes 208928 | tf_op jit(solution)/shard_map/ppermute | solution.py:187
  47.7 0.0 collective-permute-done.5.tgt_b_ref
  47.7 0.8 %unpack.1 = (f32[400,128]{1,0:T(8,128)}, f32[1,1,128]{2,1,0:T(1,128)}, f32[400,128]{1,0:T(8,128)}, f32[1,1,128]{2,1,0:T(1,128)}) custom-call(f32[408,128]{1,0:T(8,128)S(1)} %collective-permute-done.3.tgt_a_ref, f32[408,128]{1,0:T(8,128)S(1)} %collective-permute-done.4.src_ref, f32[408,128]{1,0:T(8,128)S(1)} %collective-permute-done.5.tgt_b_ref), custom_call_target="tpu_custom_call" | custom-call | tf_op jit(solution)/shard_map/unpack/pallas_call | solution.py:239
Async XLA Ops:
  5.5 25.4 %collective-permute-start = (f32[408,128]{1,0:T(8,128)S(1)}, f32[408,128]{1,0:T(8,128)S(1)}, u32[]{:S(2)}, u32[]{:S(2)}) collective-permute-start(f32[408,128]{1,0:T(8,128)S(1)} %get-tuple-element.16), channel_id=1, source_target_pairs={{5,6},{6,7},{7,8},{13,14},{14,15},{15,16},{21,22},{22,23},{23,24},... | collective-permute-start | bytes 626696 | tf_op jit(solution)/shard_map/ppermute | solution.py:187
  6.8 24.1 %collective-permute-start.1 = (f32[408,128]{1,0:T(8,128)S(1)}, f32[408,128]{1,0:T(8,128)S(1)}, u32[]{:S(2)}, u32[]{:S(2)}) collective-permute-start(f32[408,128]{1,0:T(8,128)S(1)} %get-tuple-element.17), channel_id=1, source_target_pairs={{0,32},{32,64},{64,96},{96,128},{128,160},{160,192},{192,224},{224... | collective-permute-start | bytes 626696 | tf_op jit(solution)/shard_map/ppermute | solution.py:187
  8.7 22.2 %collective-permute-start.2 = (f32[408,128]{1,0:T(8,128)S(1)}, f32[408,128]{1,0:T(8,128)S(1)}, u32[]{:S(2)}, u32[]{:S(2)}) collective-permute-start(f32[408,128]{1,0:T(8,128)S(1)} %get-tuple-element.18), channel_id=1, source_target_pairs={{0,1},{1,2},{2,3},{3,4},{4,5},{8,9},{9,10},{10,11},{11,12},{12,13}... | collective-permute-start | bytes 626696 | tf_op jit(solution)/shard_map/ppermute | solution.py:187
  31.9 13.2 %collective-permute-start.3 = (f32[408,128]{1,0:T(8,128)S(1)}, f32[408,128]{1,0:T(8,128)S(1)}, u32[]{:S(2)}, u32[]{:S(2)}) collective-permute-start(f32[408,128]{1,0:T(8,128)S(1)} %get-tuple-element.21), channel_id=1, source_target_pairs={{5,6},{6,7},{7,8},{13,14},{14,15},{15,16},{21,22},{22,23},{23,24},... | collective-permute-start | bytes 626696 | tf_op jit(solution)/shard_map/ppermute | solution.py:187
  33.2 14.5 %collective-permute-start.4 = (f32[408,128]{1,0:T(8,128)S(1)}, f32[408,128]{1,0:T(8,128)S(1)}, u32[]{:S(2)}, u32[]{:S(2)}) collective-permute-start(f32[408,128]{1,0:T(8,128)S(1)} %get-tuple-element.22), channel_id=1, source_target_pairs={{0,32},{32,64},{64,96},{96,128},{128,160},{160,192},{192,224},{224... | collective-permute-start | bytes 626696 | tf_op jit(solution)/shard_map/ppermute | solution.py:187
  35.1 12.5 %collective-permute-start.5 = (f32[408,128]{1,0:T(8,128)S(1)}, f32[408,128]{1,0:T(8,128)S(1)}, u32[]{:S(2)}, u32[]{:S(2)}) collective-permute-start(f32[408,128]{1,0:T(8,128)S(1)} %get-tuple-element.23), channel_id=1, source_target_pairs={{0,1},{1,2},{2,3},{3,4},{4,5},{8,9},{9,10},{10,11},{11,12},{12,13}... | collective-permute-start | bytes 626696 | tf_op jit(solution)/shard_map/ppermute | solution.py:187

commit v5 on v4

--- a/solution.py
+++ b/solution.py
@@ -14,7 +14,8 @@
 PAD = 8
 CHUNK = 512
 RUN = 8
-LATE_FROM = 5
+LATE_FIRST = 6
+LATE_SECOND = 7
 VMEM_LIMIT = 32 * 1024 * 1024
 
 plain = (((1,), (0,)), ((), ()))
@@ -37,25 +38,22 @@
     return jnp.where(at == index_row, 1.0, 0.0).astype(f32)
 
 
-def bucket_step(src, src_sums, tgt, tgt_sums, operators, src_rows, dst_rows, neg_rows):
-    width, entities = src.shape
-    half = width // 2
-    lanes = src_rows.shape[1]
-    negs = lanes * len(neg_rows)
-
-    pick_s = one_hot(src_rows, entities).astype(bf16)
-    pick_d = one_hot(dst_rows, entities).astype(bf16)
-    pick_s2 = jnp.concatenate([pick_s, pick_s], axis=0)
-    pick_d2 = jnp.concatenate([pick_d, pick_d], axis=0)
+def count_rows(neg_rows, entities):
     held = one_hot(neg_rows[0], entities)
     for row in neg_rows[1:]:
         held = held + one_hot(row, entities)
-    count_col = jnp.sum(held, axis=1, keepdims=True)
-    count_row = mm(jnp.ones((8, lanes), bf16), held.astype(bf16), right_t)[0:1]
-
+    return mm(jnp.ones((8, held.shape[1]), bf16), held.astype(bf16), right_t)[0:1]
+
+
+def bucket_step(src, src_sums, tgt, tgt_sums, operators, src_rows, dst_rows, counts, negs):
+    width, entities = src.shape
+    half = width // 2
+
+    pick_s = one_hot(src_rows, entities).astype(bf16)
+    pick_d = one_hot(dst_rows, entities).astype(bf16)
     op_re, op_im = operators[:half], operators[half:]
-    rows = mm(jnp.concatenate(two_parts(src), axis=1), pick_s2)
-    matched = mm(jnp.concatenate(two_parts(tgt), axis=1), pick_d2)
+    rows = mm(jnp.concatenate(two_parts(src), axis=1), jnp.concatenate([pick_s, pick_s], axis=0))
+    matched = mm(jnp.concatenate(two_parts(tgt), axis=1), jnp.concatenate([pick_d, pick_d], axis=0))
     re, im = rows[:half], rows[half:]
     queries = jnp.concatenate([re * op_re - im * op_im, re * op_im + im * op_re], axis=0)
     positive = jnp.sum(queries * matched, axis=0, keepdims=True)
@@ -65,9 +63,9 @@
     target_b = tgt.astype(bf16)
     scores = mm(target_b, queries_b, left_t)
     weights = ((1.0 / (1.0 + jnp.exp(-scores))) * (1.0 / negs)).astype(bf16)
-    counted = jnp.concatenate(two_parts(weights.astype(f32) * count_col), axis=0)
-
-    pull = mm(jnp.concatenate([target_b, target_b], axis=1), counted)
+
+    counted = jnp.concatenate(two_parts(target_b.astype(f32) * counts), axis=1)
+    pull = mm(counted, jnp.concatenate([weights, weights], axis=0))
     grad = pos_grad * matched + pull
     g_re, g_im = grad[:half], grad[half:]
     back = jnp.concatenate([g_re * op_re + g_im * op_im, g_im * op_re - g_re * op_im], axis=0)
@@ -75,7 +73,7 @@
         jnp.concatenate(two_parts(back), axis=1), jnp.concatenate([pick_s, pick_s], axis=1), right_t
     )
 
-    tgt_grad = mm(queries_b, weights, right_t) * count_row + mm(
+    tgt_grad = mm(queries_b, weights, right_t) * counts + mm(
         jnp.concatenate(two_parts(pos_grad * queries), axis=1),
         jnp.concatenate([pick_d, pick_d], axis=1),
         right_t,
@@ -98,7 +96,7 @@
 
 def first_kernel(
     src_hbm, src_sums_hbm, tgt_hbm, tgt_sums_hbm, table_hbm, s_hbm, d_hbm, g_hbm, n_hbm,
-    tgt_a_out, src_out, tgt_b_out, op_out, index_out,
+    tgt_a_out, src_out, move_out, tgt_b_out, own_out,
     src_ref, src_sums_ref, tgt_ref, tgt_sums_ref, table_ref, s_ref, d_ref, g_ref, n_ref, pick_ref, sems,
 ):
     width, entities = src_ref.shape
@@ -127,40 +125,56 @@
     for copy in copies[3:]:
         copy.wait()
     operators = jnp.concatenate(pieces, axis=0)
-    op_out[...] = operators[:, lanes:]
-    index_out[0:1, :] = s_ref[0, 0, 1:2, :]
-    index_out[1:2, :] = d_ref[0, 0, 1:2, :]
-    for k in range(n_ref.shape[3] // lanes):
-        index_out[2 + k : 3 + k, :] = n_ref[0, 0, 1:2, k * lanes : (k + 1) * lanes]
-    negs = [n_ref[0, 0, 0:1, k * lanes : (k + 1) * lanes] for k in range(n_ref.shape[3] // lanes)]
+    negs = n_ref.shape[3]
+    counts = [
+        count_rows([n_ref[0, 0, t : t + 1, k : k + lanes] for k in range(0, negs, lanes)], src_ref.shape[1])
+        for t in range(2)
+    ]
+    index = [s_ref[0, 0, 1:2, :].astype(f32), d_ref[0, 0, 1:2, :].astype(f32), counts[1]]
+    index = jnp.concatenate(index + [jnp.zeros((PAD - len(index), lanes), f32)], axis=0)
+    for out in (move_out, own_out):
+        out[:width, :] = operators[:, lanes:]
+        out[width:, :] = index
     src, src_sums, tgt, tgt_sums = bucket_step(
         src_ref[...], src_sums_ref[0], tgt_ref[...], tgt_sums_ref[0], operators[:, :lanes],
-        s_ref[0, 0, 0:1, :], d_ref[0, 0, 0:1, :], negs,
+        s_ref[0, 0, 0:1, :], d_ref[0, 0, 0:1, :], counts[0], negs,
     )
     store_block(src_out, src, src_sums)
     store_block(tgt_a_out, tgt, tgt_sums)
     store_block(tgt_b_out, tgt, tgt_sums)
 
 
-def second_kernel(tgt_a_ref, src_ref, tgt_b_ref, op_ref, index_ref, tgt_a_out, src_out, tgt_b_out):
-    width = op_ref.shape[0]
-    tgt = jnp.where(from_late(lax.axis_index("col")), tgt_a_ref[...], tgt_b_ref[...])
-    negs = [index_ref[k : k + 1, :] for k in range(2, index_ref.shape[0])]
+def second_kernel(negs, tgt_a_ref, src_ref, moved_ref, tgt_b_ref, own_ref, tgt_a_out, src_out, tgt_b_out):
+    row, col = lax.axis_index("row"), lax.axis_index("col")
+    width = src_ref.shape[0] - PAD
+    tgt = jnp.where(from_late(col, LATE_FIRST), tgt_a_ref[...], tgt_b_ref[...])
+    pack = jnp.where(takes_moved(row, col, lax.axis_size("row")), moved_ref[...], own_ref[...])
     src, src_sums, tgt, tgt_sums = bucket_step(
-        src_ref[:width, :], src_ref[width : width + 1, :], tgt[:width, :], tgt[width : width + 1, :],
-        op_ref[...], index_ref[0:1, :], index_ref[1:2, :], negs,
+        src_ref[:width, :], src_ref[width : width + 1, :], tgt[:width], tgt[width : width + 1], pack[:width],
+        pack[width : width + 1].astype(jnp.int32), pack[width + 1 : width + 2].astype(jnp.int32),
+        pack[width + 2 : width + 3], negs,
     )
     store_block(src_out, src, src_sums)
     store_block(tgt_a_out, tgt, tgt_sums)
     store_block(tgt_b_out, tgt, tgt_sums)
 
 
-def late(col):
-    return col % RUN >= LATE_FROM
-
-
-def from_late(col):
-    return lax.rem(col + RUN - 1, RUN) >= LATE_FROM
+def from_late(col, late):
+    return lax.rem(col + RUN - 1, RUN) >= late
+
+
+def takes_moved(row, col, rows):
+    z = lax.rem(col, RUN)
+    return jnp.logical_or(z == 0, jnp.logical_and(z == RUN - 1, lax.rem(row, rows // 2) == 0))
+
+
+def place(row, col, rows, cols):
+    group, z = divmod(col, RUN)
+    if z == 0:
+        group -= 1
+    elif z == RUN - 1 and row % (rows // 2) == 0:
+        group += 1
+    return row, group % (cols // RUN) * RUN + z
 
 
 def unpack_kernel(tgt_a_ref, src_ref, tgt_b_ref, src_out, src_sums_out, tgt_out, tgt_sums_out, sems):
@@ -177,18 +191,57 @@
         for copy in copies:
             copy.wait()
 
-    a = from_late(lax.axis_index("col"))
+    a = from_late(lax.axis_index("col"), LATE_SECOND)
     pl.when(a)(lambda: move(tgt_a_ref))
     pl.when(jnp.logical_not(a))(lambda: move(tgt_b_ref))
 
 
-def shift(x, axis, keep=None):
-    length = lax.axis_size(axis)
-    return lax.ppermute(x, axis, [(i, (i + 1) % length) for i in range(length) if keep is None or keep(i)])
-
-
-def early(col):
-    return not late(col)
+def routes(rows, cols):
+    def pairs(source, target, keep=lambda r, c: True):
+        found = []
+        for r in range(rows):
+            for c in range(cols):
+                (r0, c0), (r1, c1) = source(r, c), target(r, c)
+                if keep(r, c):
+                    found.append((r0 * cols + c0, r1 * cols + c1))
+        return found
+
+    def home(r, c):
+        return r, c
+
+    def there(r, c):
+        return place(r, c, rows, cols)
+
+    def back_row(r, c):
+        return (r - 1) % rows, c
+
+    def back_col(r, c):
+        return r, (c - 1) % cols
+
+    def next_row(r, c):
+        return (r + 1) % rows, c
+
+    def next_col(r, c):
+        return r, (c + 1) % cols
+
+    def late_first(r, c):
+        return (c - 1) % RUN >= LATE_FIRST
+
+    def late_second(r, c):
+        return c % RUN >= LATE_SECOND
+
+    def negate(f):
+        return lambda r, c: not f(r, c)
+
+    return {
+        "first_tgt_a": pairs(back_col, there, late_first),
+        "first_src": pairs(back_row, there),
+        "moved": pairs(home, there, lambda r, c: there(r, c) != (r, c)),
+        "first_tgt_b": pairs(back_col, there, negate(late_first)),
+        "second_tgt_a": pairs(there, next_col, late_second),
+        "second_src": pairs(there, next_row),
+        "second_tgt_b": pairs(there, next_col, negate(late_second)),
+    }
 
 
 def on_device(
@@ -199,20 +252,25 @@
     types = relations.shape[0]
     edges, negs = src_index.shape[3], neg_index.shape[3]
     block = pltpu.VMEM((width + PAD, entities), f32)
+    route = routes(lax.axis_size("row"), lax.axis_size("col"))
+
+    def send(x, name):
+        return lax.ppermute(x, ("row", "col"), route[name])
+
     vmem = pl.BlockSpec(memory_space=pltpu.VMEM)
     hbm = pl.BlockSpec(memory_space=pltpu.HBM)
     params = pltpu.CompilerParams(vmem_limit_bytes=VMEM_LIMIT)
 
     operands = (src, source_acc, tgt, target_acc, relations.T, src_index, dst_index, rel_index, neg_index)
-    tgt_a, src, tgt_b, operators, index = pl.pallas_call(
+    tgt_a, src, moved, tgt_b, own = pl.pallas_call(
         first_kernel,
         name="first_step",
         out_shape=(
             block,
             block,
             block,
-            pltpu.VMEM((width, edges), f32),
-            pltpu.VMEM((2 + negs // edges, edges), jnp.int32),
+            block,
+            block,
         ),
         in_specs=[hbm] * len(operands),
         out_specs=(vmem,) * 5,
@@ -220,20 +278,21 @@
         + [pltpu.VMEM((types, 2 * edges), bf16), pltpu.SemaphoreType.DMA((len(operands) + 1,))],
         compiler_params=params,
     )(*[pltpu.with_memory_space_constraint(x, pltpu.HBM) for x in operands])
-    tgt_a = shift(tgt_a, "col", late)
-    src = shift(src, "row")
-    tgt_b = shift(tgt_b, "col", early)
+    tgt_a = send(tgt_a, "first_tgt_a")
+    src = send(src, "first_src")
+    moved = send(moved, "moved")
+    tgt_b = send(tgt_b, "first_tgt_b")
     tgt_a, src, tgt_b = pl.pallas_call(
-        second_kernel,
+        functools.partial(second_kernel, negs),
         name="second_step",
         out_shape=(block, block, block),
         in_specs=[vmem] * 5,
         out_specs=(vmem,) * 3,
         compiler_params=params,
-    )(tgt_a, src, tgt_b, operators, index)
-    tgt_a = shift(tgt_a, "col", late)
-    src = shift(src, "row")
-    tgt_b = shift(tgt_b, "col", early)
+    )(tgt_a, src, moved, tgt_b, own)
+    tgt_a = send(tgt_a, "second_tgt_a")
+    src = send(src, "second_src")
+    tgt_b = send(tgt_b, "second_tgt_b")
     table = pltpu.HBM((width, entities), f32)
     sums = pltpu.HBM((1, 1, entities), f32)
     src, src_sums, tgt, tgt_sums = pl.pallas_call(

time: 48.7 us -> 52.8 us (1.084)
  the two profiles are of different devices: /device:TPU:80 before, /device:TPU:1 now
where the time goes in v5:
time: 52.8 us; the launch traced here: 52.5 us
  waiting for transfers between devices  24.1 us (46%)
  starting transfers between devices  21 us (40%)
  Pallas kernels  6.75 us (13%)
  between operations  0.71 us (1%)
    ppermute x7, waiting for transfers between devices, send(): return lax.ppermute(x, ('row', 'col'), route[name])  24.1 us
    ppermute x7, starting transfers between devices, send(): return lax.ppermute(x, ('row', 'col'), route[name])  21 us
    pallas_call x1, Pallas kernels, on_device(): pl.pallas_call(first_kernel, name='first_step', out_shape=(block, block,...  4.88 us
    pallas_call x1, Pallas kernels, on_device(): pl.pallas_call(functools.partial(second_kernel, negs), name='second_step'...  1.08 us
  transfers between devices with their start and end apart: 7, of which 3 were waited for; matrix products, arithmetic and copies ran while one was open for 0% of the time, Pallas kernels for 0%

profile of v5, /device:TPU:1, one launch (start us, length us, event | category | flops | bytes accessed | tf_op | source)
XLA Modules:
  0.0 52.5 jit_solution(15657750245921616448)
XLA Ops:
  0.6 4.9 %first_step.1 = (f32[408,128]{1,0:T(8,128)S(1)}, f32[408,128]{1,0:T(8,128)S(1)}, f32[408,128]{1,0:T(8,128)S(1)}, f32[408,128]{1,0:T(8,128)S(1)}, f32[408,128]{1,0:T(8,128)S(1)}) custom-call(f32[400,128]{1,0:T(8,128)} %bitcast.14, f32[1,1,128]{2,1,0:T(1,128)} %src_sums_hbm.1, f32[400,128]{1,0:T(8,128)} %bitcast.15, f32[1,1,128]{2,1,0:T(1,128)} %tgt_sums_hbm.1, ...), custom_call_target="tpu_custom_call" | custom-call | tf_op jit(solution)/shard_map/first_step/pallas_call | solution.py:265
  5.5 1.3 %collective-permute-start = (f32[408,128]{1,0:T(8,128)S(1)}, f32[408,128]{1,0:T(8,128)S(1)}, u32[]{:S(2)}, u32[]{:S(2)}) collective-permute-start(f32[408,128]{1,0:T(8,128)S(1)} %get-tuple-element.16), channel_id=1, source_target_pairs={{31,24},{6,15},{7,0},{14,23},{15,8},{22,31},{23,16},{30,7},{63,56}... | collective-permute-start | bytes 626696 | tf_op jit(solution)/shard_map/ppermute | solution.py:258
  6.8 7.9 %collective-permute-start.1 = (f32[408,128]{1,0:T(8,128)S(1)}, f32[408,128]{1,0:T(8,128)S(1)}, u32[]{:S(2)}, u32[]{:S(2)}) collective-permute-start(f32[408,128]{1,0:T(8,128)S(1)} %get-tuple-element.17), channel_id=1, source_target_pairs={{992,24},{993,1},{994,2},{995,3},{996,4},{997,5},{998,6},{999,15},... | collective-permute-start | bytes 626696 | tf_op jit(solution)/shard_map/ppermute | solution.py:258
  14.7 2.0 %collective-permute-start.2 = (f32[408,128]{1,0:T(8,128)S(1)}, f32[408,128]{1,0:T(8,128)S(1)}, u32[]{:S(2)}, u32[]{:S(2)}) collective-permute-start(f32[408,128]{1,0:T(8,128)S(1)} %get-tuple-element.18), channel_id=1, source_target_pairs={{0,24},{7,15},{8,0},{15,23},{16,8},{23,31},{24,16},{31,7},{32,56},... | collective-permute-start | bytes 626696 | tf_op jit(solution)/shard_map/ppermute | solution.py:258
  16.7 1.3 %collective-permute-start.3 = (f32[408,128]{1,0:T(8,128)S(1)}, f32[408,128]{1,0:T(8,128)S(1)}, u32[]{:S(2)}, u32[]{:S(2)}) collective-permute-start(f32[408,128]{1,0:T(8,128)S(1)} %get-tuple-element.19), channel_id=1, source_target_pairs={{0,1},{1,2},{2,3},{3,4},{4,5},{5,6},{8,9},{9,10},{10,11},{11,12},{... | collective-permute-start | bytes 626696 | tf_op jit(solution)/shard_map/ppermute | solution.py:258
  18.0 9.7 %collective-permute-done.tgt_a_ref = f32[408,128]{1,0:T(8,128)S(1)} collective-permute-done((f32[408,128]{1,0:T(8,128)S(1)}, f32[408,128]{1,0:T(8,128)S(1)}, u32[]{:S(2)}, u32[]{:S(2)}) %collective-permute-start) | collective-permute-done | bytes 208928 | tf_op jit(solution)/shard_map/ppermute | solution.py:258
  27.7 0.0 collective-permute-done.1.src_ref
  27.7 0.0 collective-permute-done.2.moved_ref
  27.7 0.0 collective-permute-done.3.tgt_b_ref
  27.7 1.1 %second_step.1 = (f32[408,128]{1,0:T(8,128)S(1)}, f32[408,128]{1,0:T(8,128)S(1)}, f32[408,128]{1,0:T(8,128)S(1)}) custom-call(f32[408,128]{1,0:T(8,128)S(1)} %collective-permute-done.tgt_a_ref, f32[408,128]{1,0:T(8,128)S(1)} %collective-permute-done.1.src_ref, f32[408,128]{1,0:T(8,128)S(1)} %collective-permute-done.2.moved_ref, ...), custom_call_target="tpu_custom_call" | custom-call | tf_op jit(solution)/shard_map/second_step/pallas_call | solution.py:285
  28.8 1.3 %collective-permute-start.4 = (f32[408,128]{1,0:T(8,128)S(1)}, f32[408,128]{1,0:T(8,128)S(1)}, u32[]{:S(2)}, u32[]{:S(2)}) collective-permute-start(f32[408,128]{1,0:T(8,128)S(1)} %get-tuple-element.21), channel_id=1, source_target_pairs={{15,8},{23,16},{31,24},{7,0},{39,40},{47,48},{55,56},{63,32},{71,7... | collective-permute-start | bytes 626696 | tf_op jit(solution)/shard_map/ppermute | solution.py:258
  30.1 5.9 %collective-permute-start.5 = (f32[408,128]{1,0:T(8,128)S(1)}, f32[408,128]{1,0:T(8,128)S(1)}, u32[]{:S(2)}, u32[]{:S(2)}) collective-permute-start(f32[408,128]{1,0:T(8,128)S(1)} %get-tuple-element.22), channel_id=1, source_target_pairs={{24,32},{1,33},{2,34},{3,35},{4,36},{5,37},{6,38},{15,39},{0,40},{... | collective-permute-start | bytes 626696 | tf_op jit(solution)/shard_map/ppermute | solution.py:258
  36.0 1.3 %collective-permute-start.6 = (f32[408,128]{1,0:T(8,128)S(1)}, f32[408,128]{1,0:T(8,128)S(1)}, u32[]{:S(2)}, u32[]{:S(2)}) collective-permute-start(f32[408,128]{1,0:T(8,128)S(1)} %get-tuple-element.23), channel_id=1, source_target_pairs={{24,1},{1,2},{2,3},{3,4},{4,5},{5,6},{6,7},{0,9},{9,10},{10,11},{1... | collective-permute-start | bytes 626696 | tf_op jit(solution)/shard_map/ppermute | solution.py:258
  37.4 7.7 %collective-permute-done.4.tgt_a_ref = f32[408,128]{1,0:T(8,128)S(1)} collective-permute-done((f32[408,128]{1,0:T(8,128)S(1)}, f32[408,128]{1,0:T(8,128)S(1)}, u32[]{:S(2)}, u32[]{:S(2)}) %collective-permute-start.4) | collective-permute-done | bytes 208928 | tf_op jit(solution)/shard_map/ppermute | solution.py:258
  45.1 6.6 %collective-permute-done.5.src_ref = f32[408,128]{1,0:T(8,128)S(1)} collective-permute-done((f32[408,128]{1,0:T(8,128)S(1)}, f32[408,128]{1,0:T(8,128)S(1)}, u32[]{:S(2)}, u32[]{:S(2)}) %collective-permute-start.5) | collective-permute-done | bytes 208928 | tf_op jit(solution)/shard_map/ppermute | solution.py:258
  51.7 0.0 collective-permute-done.6.tgt_b_ref
  51.7 0.8 %unpack.1 = (f32[400,128]{1,0:T(8,128)}, f32[1,1,128]{2,1,0:T(1,128)}, f32[400,128]{1,0:T(8,128)}, f32[1,1,128]{2,1,0:T(1,128)}) custom-call(f32[408,128]{1,0:T(8,128)S(1)} %collective-permute-done.4.tgt_a_ref, f32[408,128]{1,0:T(8,128)S(1)} %collective-permute-done.5.src_ref, f32[408,128]{1,0:T(8,128)S(1)} %collective-permute-done.6.tgt_b_ref), custom_call_target="tpu_custom_call" | custom-call | tf_op jit(solution)/shard_map/unpack/pallas_call | solution.py:298
Async XLA Ops:
  5.5 22.2 %collective-permute-start = (f32[408,128]{1,0:T(8,128)S(1)}, f32[408,128]{1,0:T(8,128)S(1)}, u32[]{:S(2)}, u32[]{:S(2)}) collective-permute-start(f32[408,128]{1,0:T(8,128)S(1)} %get-tuple-element.16), channel_id=1, source_target_pairs={{31,24},{6,15},{7,0},{14,23},{15,8},{22,31},{23,16},{30,7},{63,56}... | collective-permute-start | bytes 626696 | tf_op jit(solution)/shard_map/ppermute | solution.py:258
  6.8 20.9 %collective-permute-start.1 = (f32[408,128]{1,0:T(8,128)S(1)}, f32[408,128]{1,0:T(8,128)S(1)}, u32[]{:S(2)}, u32[]{:S(2)}) collective-permute-start(f32[408,128]{1,0:T(8,128)S(1)} %get-tuple-element.17), channel_id=1, source_target_pairs={{992,24},{993,1},{994,2},{995,3},{996,4},{997,5},{998,6},{999,15},... | collective-permute-start | bytes 626696 | tf_op jit(solution)/shard_map/ppermute | solution.py:258
  14.7 13.0 %collective-permute-start.2 = (f32[408,128]{1,0:T(8,128)S(1)}, f32[408,128]{1,0:T(8,128)S(1)}, u32[]{:S(2)}, u32[]{:S(2)}) collective-permute-start(f32[408,128]{1,0:T(8,128)S(1)} %get-tuple-element.18), channel_id=1, source_target_pairs={{0,24},{7,15},{8,0},{15,23},{16,8},{23,31},{24,16},{31,7},{32,56},... | collective-permute-start | bytes 626696 | tf_op jit(solution)/shard_map/ppermute | solution.py:258
  16.7 11.0 %collective-permute-start.3 = (f32[408,128]{1,0:T(8,128)S(1)}, f32[408,128]{1,0:T(8,128)S(1)}, u32[]{:S(2)}, u32[]{:S(2)}) collective-permute-start(f32[408,128]{1,0:T(8,128)S(1)} %get-tuple-element.19), channel_id=1, source_target_pairs={{0,1},{1,2},{2,3},{3,4},{4,5},{5,6},{8,9},{9,10},{10,11},{11,12},{... | collective-permute-start | bytes 626696 | tf_op jit(solution)/shard_map/ppermute | solution.py:258
  28.8 16.3 %collective-permute-start.4 = (f32[408,128]{1,0:T(8,128)S(1)}, f32[408,128]{1,0:T(8,128)S(1)}, u32[]{:S(2)}, u32[]{:S(2)}) collective-permute-start(f32[408,128]{1,0:T(8,128)S(1)} %get-tuple-element.21), channel_id=1, source_target_pairs={{15,8},{23,16},{31,24},{7,0},{39,40},{47,48},{55,56},{63,32},{71,7... | collective-permute-start | bytes 626696 | tf_op jit(solution)/shard_map/ppermute | solution.py:258
  30.1 21.6 %collective-permute-start.5 = (f32[408,128]{1,0:T(8,128)S(1)}, f32[408,128]{1,0:T(8,128)S(1)}, u32[]{:S(2)}, u32[]{:S(2)}) collective-permute-start(f32[408,128]{1,0:T(8,128)S(1)} %get-tuple-element.22), channel_id=1, source_target_pairs={{24,32},{1,33},{2,34},{3,35},{4,36},{5,37},{6,38},{15,39},{0,40},{... | collective-permute-start | bytes 626696 | tf_op jit(solution)/shard_map/ppermute | solution.py:258
  36.0 15.7 %collective-permute-start.6 = (f32[408,128]{1,0:T(8,128)S(1)}, f32[408,128]{1,0:T(8,128)S(1)}, u32[]{:S(2)}, u32[]{:S(2)}) collective-permute-start(f32[408,128]{1,0:T(8,128)S(1)} %get-tuple-element.23), channel_id=1, source_target_pairs={{24,1},{1,2},{2,3},{3,4},{4,5},{5,6},{6,7},{0,9},{9,10},{10,11},{1... | collective-permute-start | bytes 626696 | tf_op jit(solution)/shard_map/ppermute | solution.py:258

commit v6 on v5

--- a/solution.py
+++ b/solution.py
@@ -14,8 +14,8 @@
 PAD = 8
 CHUNK = 512
 RUN = 8
-LATE_FIRST = 6
-LATE_SECOND = 7
+LATE_FIRST = 5
+LATE_SECOND = 5
 VMEM_LIMIT = 32 * 1024 * 1024
 
 plain = (((1,), (0,)), ((), ()))
@@ -163,17 +163,18 @@
     return lax.rem(col + RUN - 1, RUN) >= late
 
 
+def crosses(row, rows):
+    return (row + 1) % (rows // 2) == 0
+
+
 def takes_moved(row, col, rows):
-    z = lax.rem(col, RUN)
-    return jnp.logical_or(z == 0, jnp.logical_and(z == RUN - 1, lax.rem(row, rows // 2) == 0))
+    return jnp.logical_and(lax.rem(col, RUN) == 0, lax.rem(row + 1, rows // 2) == 0)
 
 
 def place(row, col, rows, cols):
     group, z = divmod(col, RUN)
-    if z == 0:
+    if z == 0 and crosses(row, rows):
         group -= 1
-    elif z == RUN - 1 and row % (rows // 2) == 0:
-        group += 1
     return row, group % (cols // RUN) * RUN + z
 
 
@@ -191,7 +192,9 @@
         for copy in copies:
             copy.wait()
 
-    a = from_late(lax.axis_index("col"), LATE_SECOND)
+    row, col = lax.axis_index("row"), lax.axis_index("col")
+    from_moved = jnp.logical_and(lax.rem(col, RUN) == 1, lax.rem(row + 1, lax.axis_size("row") // 2) == 0)
+    a = jnp.logical_or(from_late(col, LATE_SECOND), from_moved)
     pl.when(a)(lambda: move(tgt_a_ref))
     pl.when(jnp.logical_not(a))(lambda: move(tgt_b_ref))
 
@@ -228,7 +231,7 @@
         return (c - 1) % RUN >= LATE_FIRST
 
     def late_second(r, c):
-        return c % RUN >= LATE_SECOND
+        return c % RUN >= LATE_SECOND or (c % RUN == 0 and crosses(r, rows))
 
     def negate(f):
         return lambda r, c: not f(r, c)

time: 52.8 us -> 49.1 us (0.930)
  the two profiles are of different devices: /device:TPU:1 before, /device:TPU:16 now
where the time goes in v6:
time: 49.1 us; the launch traced here: 48.8 us
  waiting for transfers between devices  28.4 us (58%)
  starting transfers between devices  13 us (26%)
  Pallas kernels  6.74 us (14%)
  between operations  0.71 us (1%)
    ppermute x7, waiting for transfers between devices, send(): return lax.ppermute(x, ('row', 'col'), route[name])  28.4 us
    ppermute x7, starting transfers between devices, send(): return lax.ppermute(x, ('row', 'col'), route[name])  13 us
    pallas_call x1, Pallas kernels, on_device(): pl.pallas_call(first_kernel, name='first_step', out_shape=(block, block,...  4.88 us
    pallas_call x1, Pallas kernels, on_device(): pl.pallas_call(functools.partial(second_kernel, negs), name='second_step'...  1.07 us
  transfers between devices with their start and end apart: 7, of which 3 were waited for; matrix products, arithmetic and copies ran while one was open for 0% of the time, Pallas kernels for 0%

profile of v6, /device:TPU:16, one launch (start us, length us, event | category | flops | bytes accessed | tf_op | source)
XLA Modules:
  0.0 48.8 jit_solution(13118866363038725404)
XLA Ops:
  0.6 4.9 %first_step.1 = (f32[408,128]{1,0:T(8,128)S(1)}, f32[408,128]{1,0:T(8,128)S(1)}, f32[408,128]{1,0:T(8,128)S(1)}, f32[408,128]{1,0:T(8,128)S(1)}, f32[408,128]{1,0:T(8,128)S(1)}) custom-call(f32[400,128]{1,0:T(8,128)} %bitcast.14, f32[1,1,128]{2,1,0:T(1,128)} %src_sums_hbm.1, f32[400,128]{1,0:T(8,128)} %bitcast.15, f32[1,1,128]{2,1,0:T(1,128)} %tgt_sums_hbm.1, ...), custom_call_target="tpu_custom_call" | custom-call | tf_op jit(solution)/shard_map/first_step/pallas_call | solution.py:268
  5.5 1.3 %collective-permute-start = (f32[408,128]{1,0:T(8,128)S(1)}, f32[408,128]{1,0:T(8,128)S(1)}, u32[]{:S(2)}, u32[]{:S(2)}) collective-permute-start(f32[408,128]{1,0:T(8,128)S(1)} %get-tuple-element.16), channel_id=1, source_target_pairs={{31,0},{5,6},{6,7},{7,8},{13,14},{14,15},{15,16},{21,22},{22,23},{... | collective-permute-start | bytes 626696 | tf_op jit(solution)/shard_map/ppermute | solution.py:261
  6.8 1.9 %collective-permute-start.1 = (f32[408,128]{1,0:T(8,128)S(1)}, f32[408,128]{1,0:T(8,128)S(1)}, u32[]{:S(2)}, u32[]{:S(2)}) collective-permute-start(f32[408,128]{1,0:T(8,128)S(1)} %get-tuple-element.17), channel_id=1, source_target_pairs={{992,0},{993,1},{994,2},{995,3},{996,4},{997,5},{998,6},{999,7},{1... | collective-permute-start | bytes 626696 | tf_op jit(solution)/shard_map/ppermute | solution.py:261
  8.8 0.7 %collective-permute-start.2 = (f32[408,128]{1,0:T(8,128)S(1)}, f32[408,128]{1,0:T(8,128)S(1)}, u32[]{:S(2)}, u32[]{:S(2)}) collective-permute-start(f32[408,128]{1,0:T(8,128)S(1)} %get-tuple-element.18), channel_id=1, source_target_pairs={{480,504},{488,480},{496,488},{504,496},{992,1016},{1000,992},{100... | collective-permute-start | bytes 626696 | tf_op jit(solution)/shard_map/ppermute | solution.py:261
  9.4 4.6 %collective-permute-start.3 = (f32[408,128]{1,0:T(8,128)S(1)}, f32[408,128]{1,0:T(8,128)S(1)}, u32[]{:S(2)}, u32[]{:S(2)}) collective-permute-start(f32[408,128]{1,0:T(8,128)S(1)} %get-tuple-element.19), channel_id=1, source_target_pairs={{0,1},{1,2},{2,3},{3,4},{4,5},{8,9},{9,10},{10,11},{11,12},{12,13}... | collective-permute-start | bytes 626696 | tf_op jit(solution)/shard_map/ppermute | solution.py:261
  14.0 13.7 %collective-permute-done.tgt_a_ref = f32[408,128]{1,0:T(8,128)S(1)} collective-permute-done((f32[408,128]{1,0:T(8,128)S(1)}, f32[408,128]{1,0:T(8,128)S(1)}, u32[]{:S(2)}, u32[]{:S(2)}) %collective-permute-start) | collective-permute-done | bytes 208928 | tf_op jit(solution)/shard_map/ppermute | solution.py:261
  27.8 0.0 collective-permute-done.1.src_ref
  27.8 0.0 collective-permute-done.2.moved_ref
  27.8 0.0 collective-permute-done.3.tgt_b_ref
  27.8 1.1 %second_step.1 = (f32[408,128]{1,0:T(8,128)S(1)}, f32[408,128]{1,0:T(8,128)S(1)}, f32[408,128]{1,0:T(8,128)S(1)}) custom-call(f32[408,128]{1,0:T(8,128)S(1)} %collective-permute-done.tgt_a_ref, f32[408,128]{1,0:T(8,128)S(1)} %collective-permute-done.1.src_ref, f32[408,128]{1,0:T(8,128)S(1)} %collective-permute-done.2.moved_ref, ...), custom_call_target="tpu_custom_call" | custom-call | tf_op jit(solution)/shard_map/second_step/pallas_call | solution.py:288
  28.9 1.3 %collective-permute-start.4 = (f32[408,128]{1,0:T(8,128)S(1)}, f32[408,128]{1,0:T(8,128)S(1)}, u32[]{:S(2)}, u32[]{:S(2)}) collective-permute-start(f32[408,128]{1,0:T(8,128)S(1)} %get-tuple-element.21), channel_id=1, source_target_pairs={{5,6},{6,7},{7,8},{13,14},{14,15},{15,16},{21,22},{22,23},{23,24},... | collective-permute-start | bytes 626696 | tf_op jit(solution)/shard_map/ppermute | solution.py:261
  30.2 1.9 %collective-permute-start.5 = (f32[408,128]{1,0:T(8,128)S(1)}, f32[408,128]{1,0:T(8,128)S(1)}, u32[]{:S(2)}, u32[]{:S(2)}) collective-permute-start(f32[408,128]{1,0:T(8,128)S(1)} %get-tuple-element.22), channel_id=1, source_target_pairs={{0,32},{1,33},{2,34},{3,35},{4,36},{5,37},{6,38},{7,39},{8,40},{9,... | collective-permute-start | bytes 626696 | tf_op jit(solution)/shard_map/ppermute | solution.py:261
  32.1 1.3 %collective-permute-start.6 = (f32[408,128]{1,0:T(8,128)S(1)}, f32[408,128]{1,0:T(8,128)S(1)}, u32[]{:S(2)}, u32[]{:S(2)}) collective-permute-start(f32[408,128]{1,0:T(8,128)S(1)} %get-tuple-element.23), channel_id=1, source_target_pairs={{0,1},{1,2},{2,3},{3,4},{4,5},{8,9},{9,10},{10,11},{11,12},{12,13}... | collective-permute-start | bytes 626696 | tf_op jit(solution)/shard_map/ppermute | solution.py:261
  33.4 11.8 %collective-permute-done.4.tgt_a_ref = f32[408,128]{1,0:T(8,128)S(1)} collective-permute-done((f32[408,128]{1,0:T(8,128)S(1)}, f32[408,128]{1,0:T(8,128)S(1)}, u32[]{:S(2)}, u32[]{:S(2)}) %collective-permute-start.4) | collective-permute-done | bytes 208928 | tf_op jit(solution)/shard_map/ppermute | solution.py:261
  45.2 2.9 %collective-permute-done.5.src_ref = f32[408,128]{1,0:T(8,128)S(1)} collective-permute-done((f32[408,128]{1,0:T(8,128)S(1)}, f32[408,128]{1,0:T(8,128)S(1)}, u32[]{:S(2)}, u32[]{:S(2)}) %collective-permute-start.5) | collective-permute-done | bytes 208928 | tf_op jit(solution)/shard_map/ppermute | solution.py:261
  48.0 0.0 collective-permute-done.6.tgt_b_ref
  48.0 0.8 %unpack.1 = (f32[400,128]{1,0:T(8,128)}, f32[1,1,128]{2,1,0:T(1,128)}, f32[400,128]{1,0:T(8,128)}, f32[1,1,128]{2,1,0:T(1,128)}) custom-call(f32[408,128]{1,0:T(8,128)S(1)} %collective-permute-done.4.tgt_a_ref, f32[408,128]{1,0:T(8,128)S(1)} %collective-permute-done.5.src_ref, f32[408,128]{1,0:T(8,128)S(1)} %collective-permute-done.6.tgt_b_ref), custom_call_target="tpu_custom_call" | custom-call | tf_op jit(solution)/shard_map/unpack/pallas_call | solution.py:301
Async XLA Ops:
  5.5 22.2 %collective-permute-start = (f32[408,128]{1,0:T(8,128)S(1)}, f32[408,128]{1,0:T(8,128)S(1)}, u32[]{:S(2)}, u32[]{:S(2)}) collective-permute-start(f32[408,128]{1,0:T(8,128)S(1)} %get-tuple-element.16), channel_id=1, source_target_pairs={{31,0},{5,6},{6,7},{7,8},{13,14},{14,15},{15,16},{21,22},{22,23},{... | collective-permute-start | bytes 626696 | tf_op jit(solution)/shard_map/ppermute | solution.py:261
  6.8 20.9 %collective-permute-start.1 = (f32[408,128]{1,0:T(8,128)S(1)}, f32[408,128]{1,0:T(8,128)S(1)}, u32[]{:S(2)}, u32[]{:S(2)}) collective-permute-start(f32[408,128]{1,0:T(8,128)S(1)} %get-tuple-element.17), channel_id=1, source_target_pairs={{992,0},{993,1},{994,2},{995,3},{996,4},{997,5},{998,6},{999,7},{1... | collective-permute-start | bytes 626696 | tf_op jit(solution)/shard_map/ppermute | solution.py:261
  8.8 19.0 %collective-permute-start.2 = (f32[408,128]{1,0:T(8,128)S(1)}, f32[408,128]{1,0:T(8,128)S(1)}, u32[]{:S(2)}, u32[]{:S(2)}) collective-permute-start(f32[408,128]{1,0:T(8,128)S(1)} %get-tuple-element.18), channel_id=1, source_target_pairs={{480,504},{488,480},{496,488},{504,496},{992,1016},{1000,992},{100... | collective-permute-start | bytes 626696 | tf_op jit(solution)/shard_map/ppermute | solution.py:261
  9.4 18.3 %collective-permute-start.3 = (f32[408,128]{1,0:T(8,128)S(1)}, f32[408,128]{1,0:T(8,128)S(1)}, u32[]{:S(2)}, u32[]{:S(2)}) collective-permute-start(f32[408,128]{1,0:T(8,128)S(1)} %get-tuple-element.19), channel_id=1, source_target_pairs={{0,1},{1,2},{2,3},{3,4},{4,5},{8,9},{9,10},{10,11},{11,12},{12,13}... | collective-permute-start | bytes 626696 | tf_op jit(solution)/shard_map/ppermute | solution.py:261
  28.9 16.3 %collective-permute-start.4 = (f32[408,128]{1,0:T(8,128)S(1)}, f32[408,128]{1,0:T(8,128)S(1)}, u32[]{:S(2)}, u32[]{:S(2)}) collective-permute-start(f32[408,128]{1,0:T(8,128)S(1)} %get-tuple-element.21), channel_id=1, source_target_pairs={{5,6},{6,7},{7,8},{13,14},{14,15},{15,16},{21,22},{22,23},{23,24},... | collective-permute-start | bytes 626696 | tf_op jit(solution)/shard_map/ppermute | solution.py:261
  30.2 17.9 %collective-permute-start.5 = (f32[408,128]{1,0:T(8,128)S(1)}, f32[408,128]{1,0:T(8,128)S(1)}, u32[]{:S(2)}, u32[]{:S(2)}) collective-permute-start(f32[408,128]{1,0:T(8,128)S(1)} %get-tuple-element.22), channel_id=1, source_target_pairs={{0,32},{1,33},{2,34},{3,35},{4,36},{5,37},{6,38},{7,39},{8,40},{9,... | collective-permute-start | bytes 626696 | tf_op jit(solution)/shard_map/ppermute | solution.py:261
  32.1 15.9 %collective-permute-start.6 = (f32[408,128]{1,0:T(8,128)S(1)}, f32[408,128]{1,0:T(8,128)S(1)}, u32[]{:S(2)}, u32[]{:S(2)}) collective-permute-start(f32[408,128]{1,0:T(8,128)S(1)} %get-tuple-element.23), channel_id=1, source_target_pairs={{0,1},{1,2},{2,3},{3,4},{4,5},{8,9},{9,10},{10,11},{11,12},{12,13}... | collective-permute-start | bytes 626696 | tf_op jit(solution)/shard_map/ppermute | solution.py:261

commit v7 on v6

--- a/solution.py
+++ b/solution.py
@@ -144,7 +144,7 @@
     store_block(tgt_b_out, tgt, tgt_sums)
 
 
-def second_kernel(negs, tgt_a_ref, src_ref, moved_ref, tgt_b_ref, own_ref, tgt_a_out, src_out, tgt_b_out):
+def second_kernel(negs, tgt_a_ref, src_ref, moved_ref, tgt_b_ref, own_ref, src_far_out, tgt_a_out, src_out, tgt_b_out):
     row, col = lax.axis_index("row"), lax.axis_index("col")
     width = src_ref.shape[0] - PAD
     tgt = jnp.where(from_late(col, LATE_FIRST), tgt_a_ref[...], tgt_b_ref[...])
@@ -154,6 +154,7 @@
         pack[width : width + 1].astype(jnp.int32), pack[width + 1 : width + 2].astype(jnp.int32),
         pack[width + 2 : width + 3], negs,
     )
+    store_block(src_far_out, src, src_sums)
     store_block(src_out, src, src_sums)
     store_block(tgt_a_out, tgt, tgt_sums)
     store_block(tgt_b_out, tgt, tgt_sums)
@@ -167,25 +168,29 @@
     return (row + 1) % (rows // 2) == 0
 
 
+def moves(row, rows):
+    return jnp.logical_or(lax.rem(row + 1, rows // 2) == 0, row == rows // 2)
+
+
 def takes_moved(row, col, rows):
-    return jnp.logical_and(lax.rem(col, RUN) == 0, lax.rem(row + 1, rows // 2) == 0)
+    return jnp.logical_and(lax.rem(col, RUN) == 0, moves(row, rows))
 
 
 def place(row, col, rows, cols):
     group, z = divmod(col, RUN)
-    if z == 0 and crosses(row, rows):
+    if z == 0 and (crosses(row, rows) or row == rows // 2):
         group -= 1
     return row, group % (cols // RUN) * RUN + z
 
 
-def unpack_kernel(tgt_a_ref, src_ref, tgt_b_ref, src_out, src_sums_out, tgt_out, tgt_sums_out, sems):
+def unpack_kernel(src_far_ref, tgt_a_ref, src_ref, tgt_b_ref, src_out, src_sums_out, tgt_out, tgt_sums_out, sems):
     width = src_out.shape[0]
 
     def send(ref, out, sums_out, first):
         pairs = [(ref.at[pl.ds(0, width)], out), (ref.at[pl.ds(width, 1)], sums_out.at[0])]
         return [pltpu.make_async_copy(a, b, sems.at[first + i]) for i, (a, b) in enumerate(pairs)]
 
-    def move(tgt_ref):
+    def move(src_ref, tgt_ref):
         copies = send(src_ref, src_out, src_sums_out, 0) + send(tgt_ref, tgt_out, tgt_sums_out, 2)
         for copy in copies:
             copy.start()
@@ -193,10 +198,16 @@
             copy.wait()
 
     row, col = lax.axis_index("row"), lax.axis_index("col")
-    from_moved = jnp.logical_and(lax.rem(col, RUN) == 1, lax.rem(row + 1, lax.axis_size("row") // 2) == 0)
-    a = jnp.logical_or(from_late(col, LATE_SECOND), from_moved)
-    pl.when(a)(lambda: move(tgt_a_ref))
-    pl.when(jnp.logical_not(a))(lambda: move(tgt_b_ref))
+    rows = lax.axis_size("row")
+    z = lax.rem(col, RUN)
+    src_far = jnp.logical_and(z == 0, lax.rem(row, rows // 2) == 0)
+    from_moved = jnp.logical_and(z == 1, lax.rem(row + 1, rows // 2) == 0)
+    tgt_a = jnp.logical_or(from_late(col, LATE_SECOND), from_moved)
+    for far in (False, True):
+        for a in (False, True):
+            chosen = jnp.logical_and(src_far == far, tgt_a == a)
+            refs = (src_far_ref if far else src_ref, tgt_a_ref if a else tgt_b_ref)
+            pl.when(chosen)(functools.partial(move, *refs))
 
 
 def routes(rows, cols):
@@ -233,6 +244,9 @@
     def late_second(r, c):
         return c % RUN >= LATE_SECOND or (c % RUN == 0 and crosses(r, rows))
 
+    def wraps_early(r, c):
+        return c % RUN == 0 and crosses(r, rows)
+
     def negate(f):
         return lambda r, c: not f(r, c)
 
@@ -242,7 +256,8 @@
         "moved": pairs(home, there, lambda r, c: there(r, c) != (r, c)),
         "first_tgt_b": pairs(back_col, there, negate(late_first)),
         "second_tgt_a": pairs(there, next_col, late_second),
-        "second_src": pairs(there, next_row),
+        "second_src_far": pairs(there, next_row, wraps_early),
+        "second_src": pairs(there, next_row, negate(wraps_early)),
         "second_tgt_b": pairs(there, next_col, negate(late_second)),
     }
 
@@ -285,14 +300,15 @@
     src = send(src, "first_src")
     moved = send(moved, "moved")
     tgt_b = send(tgt_b, "first_tgt_b")
-    tgt_a, src, tgt_b = pl.pallas_call(
+    src_far, tgt_a, src, tgt_b = pl.pallas_call(
         functools.partial(second_kernel, negs),
         name="second_step",
-        out_shape=(block, block, block),
+        out_shape=(block,) * 4,
         in_specs=[vmem] * 5,
-        out_specs=(vmem,) * 3,
+        out_specs=(vmem,) * 4,
         compiler_params=params,
     )(tgt_a, src, moved, tgt_b, own)
+    src_far = send(src_far, "second_src_far")
     tgt_a = send(tgt_a, "second_tgt_a")
     src = send(src, "second_src")
     tgt_b = send(tgt_b, "second_tgt_b")
@@ -302,11 +318,11 @@
         unpack_kernel,
         name="unpack",
         out_shape=(table, sums, table, sums),
-        in_specs=[vmem] * 3,
+        in_specs=[vmem] * 4,
         out_specs=(hbm,) * 4,
         scratch_shapes=[pltpu.SemaphoreType.DMA((4,))],
         compiler_params=params,
-    )(tgt_a, src, tgt_b)
+    )(src_far, tgt_a, src, tgt_b)
     return src.T[None, None], src_sums, tgt.T[None, None], tgt_sums
 
 

time: 49.1 us -> 48.9 us (level)
  the two profiles are of different devices: /device:TPU:16 before, /device:TPU:15 now
where the time goes in v7:
time: 48.9 us; the launch traced here: 48.6 us
  starting transfers between devices  29 us (59%)
  waiting for transfers between devices  12.2 us (25%)
  Pallas kernels  6.76 us (14%)
  between operations  0.73 us (1%)
    ppermute x8, starting transfers between devices, send(): return lax.ppermute(x, ('row', 'col'), route[name])  29 us
    ppermute x8, waiting for transfers between devices, send(): return lax.ppermute(x, ('row', 'col'), route[name])  12.2 us
    pallas_call x1, Pallas kernels, on_device(): pl.pallas_call(first_kernel, name='first_step', out_shape=(block, block,...  4.89 us
    pallas_call x1, Pallas kernels, on_device(): pl.pallas_call(functools.partial(second_kernel, negs), name='second_step'...  1.08 us
  transfers between devices with their start and end apart: 8, of which 2 were waited for; matrix products, arithmetic and copies ran while one was open for 0% of the time, Pallas kernels for 0%

profile of v7, /device:TPU:15, one launch (start us, length us, event | category | flops | bytes accessed | tf_op | source)
XLA Modules:
  0.0 48.6 jit_solution(3859440919578547524)
XLA Ops:
  0.6 4.9 %first_step.1 = (f32[408,128]{1,0:T(8,128)S(1)}, f32[408,128]{1,0:T(8,128)S(1)}, f32[408,128]{1,0:T(8,128)S(1)}, f32[408,128]{1,0:T(8,128)S(1)}, f32[408,128]{1,0:T(8,128)S(1)}) custom-call(f32[400,128]{1,0:T(8,128)} %bitcast.14, f32[1,1,128]{2,1,0:T(1,128)} %src_sums_hbm.1, f32[400,128]{1,0:T(8,128)} %bitcast.15, f32[1,1,128]{2,1,0:T(1,128)} %tgt_sums_hbm.1, ...), custom_call_target="tpu_custom_call" | custom-call | tf_op jit(solution)/shard_map/first_step/pallas_call | solution.py:283
  5.5 1.3 %collective-permute-start = (f32[408,128]{1,0:T(8,128)S(1)}, f32[408,128]{1,0:T(8,128)S(1)}, u32[]{:S(2)}, u32[]{:S(2)}) collective-permute-start(f32[408,128]{1,0:T(8,128)S(1)} %get-tuple-element.17), channel_id=1, source_target_pairs={{31,0},{5,6},{6,7},{7,8},{13,14},{14,15},{15,16},{21,22},{22,23},{... | collective-permute-start | bytes 626696 | tf_op jit(solution)/shard_map/ppermute | solution.py:276
  6.8 6.3 %collective-permute-start.1 = (f32[408,128]{1,0:T(8,128)S(1)}, f32[408,128]{1,0:T(8,128)S(1)}, u32[]{:S(2)}, u32[]{:S(2)}) collective-permute-start(f32[408,128]{1,0:T(8,128)S(1)} %get-tuple-element.18), channel_id=1, source_target_pairs={{992,0},{993,1},{994,2},{995,3},{996,4},{997,5},{998,6},{999,7},{1... | collective-permute-start | bytes 626696 | tf_op jit(solution)/shard_map/ppermute | solution.py:276
  13.1 4.7 %collective-permute-start.2 = (f32[408,128]{1,0:T(8,128)S(1)}, f32[408,128]{1,0:T(8,128)S(1)}, u32[]{:S(2)}, u32[]{:S(2)}) collective-permute-start(f32[408,128]{1,0:T(8,128)S(1)} %get-tuple-element.19), channel_id=1, source_target_pairs={{480,504},{488,480},{496,488},{504,496},{512,536},{520,512},{528,5... | collective-permute-start | bytes 626696 | tf_op jit(solution)/shard_map/ppermute | solution.py:276
  17.8 2.3 %collective-permute-start.3 = (f32[408,128]{1,0:T(8,128)S(1)}, f32[408,128]{1,0:T(8,128)S(1)}, u32[]{:S(2)}, u32[]{:S(2)}) collective-permute-start(f32[408,128]{1,0:T(8,128)S(1)} %get-tuple-element.20), channel_id=1, source_target_pairs={{0,1},{1,2},{2,3},{3,4},{4,5},{8,9},{9,10},{10,11},{11,12},{12,13}... | collective-permute-start | bytes 626696 | tf_op jit(solution)/shard_map/ppermute | solution.py:276
  20.1 5.6 %collective-permute-done.tgt_a_ref = f32[408,128]{1,0:T(8,128)S(1)} collective-permute-done((f32[408,128]{1,0:T(8,128)S(1)}, f32[408,128]{1,0:T(8,128)S(1)}, u32[]{:S(2)}, u32[]{:S(2)}) %collective-permute-start) | collective-permute-done | bytes 208928 | tf_op jit(solution)/shard_map/ppermute | solution.py:276
  25.7 0.0 collective-permute-done.1.src_ref
  25.7 0.0 collective-permute-done.2.moved_ref
  25.7 0.0 collective-permute-done.3.tgt_b_ref
  25.8 1.1 %second_step.1 = (f32[408,128]{1,0:T(8,128)S(1)}, f32[408,128]{1,0:T(8,128)S(1)}, f32[408,128]{1,0:T(8,128)S(1)}, f32[408,128]{1,0:T(8,128)S(1)}) custom-call(f32[408,128]{1,0:T(8,128)S(1)} %collective-permute-done.tgt_a_ref, f32[408,128]{1,0:T(8,128)S(1)} %collective-permute-done.1.src_ref, f32[408,128]{1,0:T(8,128)S(1)} %collective-permute-done.2.moved_ref, ...), custom_call_target="tpu_custom_call" | custom-call | tf_op jit(solution)/shard_map/second_step/pallas_call | solution.py:303
  26.8 10.5 %collective-permute-start.4 = (f32[408,128]{1,0:T(8,128)S(1)}, f32[408,128]{1,0:T(8,128)S(1)}, u32[]{:S(2)}, u32[]{:S(2)}) collective-permute-start(f32[408,128]{1,0:T(8,128)S(1)} %get-tuple-element.22), channel_id=1, source_target_pairs={{504,512},{480,520},{488,528},{496,536},{1016,0},{992,8},{1000,16}... | collective-permute-start | bytes 626696 | tf_op jit(solution)/shard_map/ppermute | solution.py:276
  37.4 1.9 %collective-permute-start.5 = (f32[408,128]{1,0:T(8,128)S(1)}, f32[408,128]{1,0:T(8,128)S(1)}, u32[]{:S(2)}, u32[]{:S(2)}) collective-permute-start(f32[408,128]{1,0:T(8,128)S(1)} %get-tuple-element.23), channel_id=1, source_target_pairs={{5,6},{6,7},{7,8},{13,14},{14,15},{15,16},{21,22},{22,23},{23,24},... | collective-permute-start | bytes 626696 | tf_op jit(solution)/shard_map/ppermute | solution.py:276
  39.3 1.3 %collective-permute-start.6 = (f32[408,128]{1,0:T(8,128)S(1)}, f32[408,128]{1,0:T(8,128)S(1)}, u32[]{:S(2)}, u32[]{:S(2)}) collective-permute-start(f32[408,128]{1,0:T(8,128)S(1)} %get-tuple-element.24), channel_id=1, source_target_pairs={{0,32},{1,33},{2,34},{3,35},{4,36},{5,37},{6,38},{7,39},{8,40},{9,... | collective-permute-start | bytes 626696 | tf_op jit(solution)/shard_map/ppermute | solution.py:276
  40.6 0.7 %collective-permute-start.7 = (f32[408,128]{1,0:T(8,128)S(1)}, f32[408,128]{1,0:T(8,128)S(1)}, u32[]{:S(2)}, u32[]{:S(2)}) collective-permute-start(f32[408,128]{1,0:T(8,128)S(1)} %get-tuple-element.25), channel_id=1, source_target_pairs={{0,1},{1,2},{2,3},{3,4},{4,5},{8,9},{9,10},{10,11},{11,12},{12,13}... | collective-permute-start | bytes 626696 | tf_op jit(solution)/shard_map/ppermute | solution.py:276
  41.3 0.0 collective-permute-done.4.src_far_ref
  41.3 6.5 %collective-permute-done.5.tgt_a_ref = f32[408,128]{1,0:T(8,128)S(1)} collective-permute-done((f32[408,128]{1,0:T(8,128)S(1)}, f32[408,128]{1,0:T(8,128)S(1)}, u32[]{:S(2)}, u32[]{:S(2)}) %collective-permute-start.5) | collective-permute-done | bytes 208928 | tf_op jit(solution)/shard_map/ppermute | solution.py:276
  47.8 0.0 collective-permute-done.6.src_ref
  47.8 0.0 collective-permute-done.7.tgt_b_ref
  47.8 0.8 %unpack.1 = (f32[400,128]{1,0:T(8,128)}, f32[1,1,128]{2,1,0:T(1,128)}, f32[400,128]{1,0:T(8,128)}, f32[1,1,128]{2,1,0:T(1,128)}) custom-call(f32[408,128]{1,0:T(8,128)S(1)} %collective-permute-done.4.src_far_ref, f32[408,128]{1,0:T(8,128)S(1)} %collective-permute-done.5.tgt_a_ref, f32[408,128]{1,0:T(8,128)S(1)} %collective-permute-done.6.src_ref, ...), custom_call_target="tpu_custom_call" | custom-call | tf_op jit(solution)/shard_map/unpack/pallas_call | solution.py:317
Async XLA Ops:
  5.5 20.2 %collective-permute-start = (f32[408,128]{1,0:T(8,128)S(1)}, f32[408,128]{1,0:T(8,128)S(1)}, u32[]{:S(2)}, u32[]{:S(2)}) collective-permute-start(f32[408,128]{1,0:T(8,128)S(1)} %get-tuple-element.17), channel_id=1, source_target_pairs={{31,0},{5,6},{6,7},{7,8},{13,14},{14,15},{15,16},{21,22},{22,23},{... | collective-permute-start | bytes 626696 | tf_op jit(solution)/shard_map/ppermute | solution.py:276
  6.8 18.9 %collective-permute-start.1 = (f32[408,128]{1,0:T(8,128)S(1)}, f32[408,128]{1,0:T(8,128)S(1)}, u32[]{:S(2)}, u32[]{:S(2)}) collective-permute-start(f32[408,128]{1,0:T(8,128)S(1)} %get-tuple-element.18), channel_id=1, source_target_pairs={{992,0},{993,1},{994,2},{995,3},{996,4},{997,5},{998,6},{999,7},{1... | collective-permute-start | bytes 626696 | tf_op jit(solution)/shard_map/ppermute | solution.py:276
  13.1 12.7 %collective-permute-start.2 = (f32[408,128]{1,0:T(8,128)S(1)}, f32[408,128]{1,0:T(8,128)S(1)}, u32[]{:S(2)}, u32[]{:S(2)}) collective-permute-start(f32[408,128]{1,0:T(8,128)S(1)} %get-tuple-element.19), channel_id=1, source_target_pairs={{480,504},{488,480},{496,488},{504,496},{512,536},{520,512},{528,5... | collective-permute-start | bytes 626696 | tf_op jit(solution)/shard_map/ppermute | solution.py:276
  17.8 8.0 %collective-permute-start.3 = (f32[408,128]{1,0:T(8,128)S(1)}, f32[408,128]{1,0:T(8,128)S(1)}, u32[]{:S(2)}, u32[]{:S(2)}) collective-permute-start(f32[408,128]{1,0:T(8,128)S(1)} %get-tuple-element.20), channel_id=1, source_target_pairs={{0,1},{1,2},{2,3},{3,4},{4,5},{8,9},{9,10},{10,11},{11,12},{12,13}... | collective-permute-start | bytes 626696 | tf_op jit(solution)/shard_map/ppermute | solution.py:276
  26.8 14.5 %collective-permute-start.4 = (f32[408,128]{1,0:T(8,128)S(1)}, f32[408,128]{1,0:T(8,128)S(1)}, u32[]{:S(2)}, u32[]{:S(2)}) collective-permute-start(f32[408,128]{1,0:T(8,128)S(1)} %get-tuple-element.22), channel_id=1, source_target_pairs={{504,512},{480,520},{488,528},{496,536},{1016,0},{992,8},{1000,16}... | collective-permute-start | bytes 626696 | tf_op jit(solution)/shard_map/ppermute | solution.py:276
  37.4 10.5 %collective-permute-start.5 = (f32[408,128]{1,0:T(8,128)S(1)}, f32[408,128]{1,0:T(8,128)S(1)}, u32[]{:S(2)}, u32[]{:S(2)}) collective-permute-start(f32[408,128]{1,0:T(8,128)S(1)} %get-tuple-element.23), channel_id=1, source_target_pairs={{5,6},{6,7},{7,8},{13,14},{14,15},{15,16},{21,22},{22,23},{23,24},... | collective-permute-start | bytes 626696 | tf_op jit(solution)/shard_map/ppermute | solution.py:276
  39.3 8.5 %collective-permute-start.6 = (f32[408,128]{1,0:T(8,128)S(1)}, f32[408,128]{1,0:T(8,128)S(1)}, u32[]{:S(2)}, u32[]{:S(2)}) collective-permute-start(f32[408,128]{1,0:T(8,128)S(1)} %get-tuple-element.24), channel_id=1, source_target_pairs={{0,32},{1,33},{2,34},{3,35},{4,36},{5,37},{6,38},{7,39},{8,40},{9,... | collective-permute-start | bytes 626696 | tf_op jit(solution)/shard_map/ppermute | solution.py:276
  40.6 7.2 %collective-permute-start.7 = (f32[408,128]{1,0:T(8,128)S(1)}, f32[408,128]{1,0:T(8,128)S(1)}, u32[]{:S(2)}, u32[]{:S(2)}) collective-permute-start(f32[408,128]{1,0:T(8,128)S(1)} %get-tuple-element.25), channel_id=1, source_target_pairs={{0,1},{1,2},{2,3},{3,4},{4,5},{8,9},{9,10},{10,11},{11,12},{12,13}... | collective-permute-start | bytes 626696 | tf_op jit(solution)/shard_map/ppermute | solution.py:276

commit v8 on v5

--- a/solution.py
+++ b/solution.py
@@ -14,13 +14,17 @@
 PAD = 8
 CHUNK = 512
 RUN = 8
-LATE_FIRST = 6
-LATE_SECOND = 7
+LATE = 5
+FINAL_COST = 50
 VMEM_LIMIT = 32 * 1024 * 1024
 
 plain = (((1,), (0,)), ((), ()))
 left_t = (((0,), (0,)), ((), ()))
 right_t = (((1,), (1,)), ((), ()))
+
+
+def cost(microseconds):
+    return pl.CostEstimate(flops=int(microseconds * 1e9), bytes_accessed=0, transcendentals=0)
 
 
 def mm(a, b, dims=plain):
@@ -96,7 +100,7 @@
 
 def first_kernel(
     src_hbm, src_sums_hbm, tgt_hbm, tgt_sums_hbm, table_hbm, s_hbm, d_hbm, g_hbm, n_hbm,
-    tgt_a_out, src_out, move_out, tgt_b_out, own_out,
+    tgt_a_out, src_out, tgt_b_out, tgt_c_out, own_out,
     src_ref, src_sums_ref, tgt_ref, tgt_sums_ref, table_ref, s_ref, d_ref, g_ref, n_ref, pick_ref, sems,
 ):
     width, entities = src_ref.shape
@@ -132,91 +136,105 @@
     ]
     index = [s_ref[0, 0, 1:2, :].astype(f32), d_ref[0, 0, 1:2, :].astype(f32), counts[1]]
     index = jnp.concatenate(index + [jnp.zeros((PAD - len(index), lanes), f32)], axis=0)
-    for out in (move_out, own_out):
-        out[:width, :] = operators[:, lanes:]
-        out[width:, :] = index
+    own_out[:width, :] = operators[:, lanes:]
+    own_out[width:, :] = index
     src, src_sums, tgt, tgt_sums = bucket_step(
         src_ref[...], src_sums_ref[0], tgt_ref[...], tgt_sums_ref[0], operators[:, :lanes],
         s_ref[0, 0, 0:1, :], d_ref[0, 0, 0:1, :], counts[0], negs,
     )
     store_block(src_out, src, src_sums)
     store_block(tgt_a_out, tgt, tgt_sums)
+    store_block(tgt_c_out, tgt, tgt_sums)
     store_block(tgt_b_out, tgt, tgt_sums)
 
 
-def second_kernel(negs, tgt_a_ref, src_ref, moved_ref, tgt_b_ref, own_ref, tgt_a_out, src_out, tgt_b_out):
-    row, col = lax.axis_index("row"), lax.axis_index("col")
+def second(negs, tgt, src_ref, own_ref):
     width = src_ref.shape[0] - PAD
-    tgt = jnp.where(from_late(col, LATE_FIRST), tgt_a_ref[...], tgt_b_ref[...])
-    pack = jnp.where(takes_moved(row, col, lax.axis_size("row")), moved_ref[...], own_ref[...])
-    src, src_sums, tgt, tgt_sums = bucket_step(
+    pack = own_ref[...]
+    return bucket_step(
         src_ref[:width, :], src_ref[width : width + 1, :], tgt[:width], tgt[width : width + 1], pack[:width],
         pack[width : width + 1].astype(jnp.int32), pack[width + 1 : width + 2].astype(jnp.int32),
         pack[width + 2 : width + 3], negs,
     )
-    store_block(src_out, src, src_sums)
-    store_block(tgt_a_out, tgt, tgt_sums)
-    store_block(tgt_b_out, tgt, tgt_sums)
+
+
+def second_kernel(negs, tgt_a_ref, src_ref, tgt_b_ref, own_ref, tgt_a_out, src_out, tgt_out):
+    row, col = lax.axis_index("row"), lax.axis_index("col")
+
+    @pl.when(jnp.logical_not(is_last(row, col, lax.axis_size("row"))))
+    def _():
+        tgt = jnp.where(from_late(col, LATE), tgt_a_ref[...], tgt_b_ref[...])
+        src, src_sums, tgt, tgt_sums = second(negs, tgt, src_ref, own_ref)
+        store_block(src_out, src, src_sums)
+        store_block(tgt_a_out, tgt, tgt_sums)
+        store_block(tgt_out, tgt, tgt_sums)
+
+
+def last_kernel(negs, done_tgt_ref, tgt_c_ref, src_ref, own_ref, tgt_b_out, src_out):
+    last = is_last(lax.axis_index("row"), lax.axis_index("col"), lax.axis_size("row"))
+
+    @pl.when(last)
+    def _():
+        src, src_sums, tgt, tgt_sums = second(negs, tgt_c_ref[...], src_ref, own_ref)
+        store_block(src_out, src, src_sums)
+        store_block(tgt_b_out, tgt, tgt_sums)
+
+    @pl.when(jnp.logical_not(last))
+    def _():
+        tgt_b_out[...] = done_tgt_ref[...]
 
 
 def from_late(col, late):
     return lax.rem(col + RUN - 1, RUN) >= late
 
 
-def takes_moved(row, col, rows):
-    z = lax.rem(col, RUN)
-    return jnp.logical_or(z == 0, jnp.logical_and(z == RUN - 1, lax.rem(row, rows // 2) == 0))
-
-
-def place(row, col, rows, cols):
-    group, z = divmod(col, RUN)
-    if z == 0:
-        group -= 1
-    elif z == RUN - 1 and row % (rows // 2) == 0:
-        group += 1
-    return row, group % (cols // RUN) * RUN + z
-
-
-def unpack_kernel(tgt_a_ref, src_ref, tgt_b_ref, src_out, src_sums_out, tgt_out, tgt_sums_out, sems):
-    width = src_out.shape[0]
-
-    def send(ref, out, sums_out, first):
-        pairs = [(ref.at[pl.ds(0, width)], out), (ref.at[pl.ds(width, 1)], sums_out.at[0])]
-        return [pltpu.make_async_copy(a, b, sems.at[first + i]) for i, (a, b) in enumerate(pairs)]
-
-    def move(tgt_ref):
-        copies = send(src_ref, src_out, src_sums_out, 0) + send(tgt_ref, tgt_out, tgt_sums_out, 2)
-        for copy in copies:
-            copy.start()
-        for copy in copies:
-            copy.wait()
-
-    a = from_late(lax.axis_index("col"), LATE_SECOND)
-    pl.when(a)(lambda: move(tgt_a_ref))
-    pl.when(jnp.logical_not(a))(lambda: move(tgt_b_ref))
+def is_last(row, col, rows):
+    return jnp.logical_and(lax.rem(col, RUN) == 0, lax.rem(row, rows // 2) == 0)
+
+
+def unpack(ref, out, sums_out, sems):
+    width = out.shape[0]
+    pairs = [(ref.at[pl.ds(0, width)], out), (ref.at[pl.ds(width, 1)], sums_out.at[0])]
+    return [pltpu.make_async_copy(a, b, sems.at[i]) for i, (a, b) in enumerate(pairs)]
+
+
+def run(copies):
+    for copy in copies:
+        copy.start()
+    for copy in copies:
+        copy.wait()
+
+
+def receives(row, col, rows):
+    return jnp.logical_not(is_last(row + rows - 1, col, rows)), from_late(col, LATE)
+
+
+def unpack_kernel(tgt_ref, src_ref, src_out, src_sums_out, tgt_out, tgt_sums_out, src_sems, tgt_sems):
+    takes_src, takes_tgt = receives(lax.axis_index("row"), lax.axis_index("col"), lax.axis_size("row"))
+    src = lambda: unpack(src_ref, src_out, src_sums_out, src_sems)
+    tgt = lambda: unpack(tgt_ref, tgt_out, tgt_sums_out, tgt_sems)
+    pl.when(jnp.logical_and(takes_src, takes_tgt))(lambda: run(src() + tgt()))
+    pl.when(jnp.logical_and(takes_src, jnp.logical_not(takes_tgt)))(lambda: run(src()))
+    pl.when(jnp.logical_and(jnp.logical_not(takes_src), takes_tgt))(lambda: run(tgt()))
+
+
+def unpack_rest_kernel(
+    _0, _1, _2, _3, src_ref, tgt_ref, src_out, src_sums_out, tgt_out, tgt_sums_out, src_sems, tgt_sems
+):
+    takes_src, takes_tgt = receives(lax.axis_index("row"), lax.axis_index("col"), lax.axis_size("row"))
+    pl.when(jnp.logical_not(takes_src))(lambda: run(unpack(src_ref, src_out, src_sums_out, src_sems)))
+    pl.when(jnp.logical_not(takes_tgt))(lambda: run(unpack(tgt_ref, tgt_out, tgt_sums_out, tgt_sems)))
 
 
 def routes(rows, cols):
-    def pairs(source, target, keep=lambda r, c: True):
+    def pairs(to, keep):
         found = []
         for r in range(rows):
             for c in range(cols):
-                (r0, c0), (r1, c1) = source(r, c), target(r, c)
                 if keep(r, c):
-                    found.append((r0 * cols + c0, r1 * cols + c1))
+                    r1, c1 = to(r, c)
+                    found.append((r * cols + c, r1 * cols + c1))
         return found
-
-    def home(r, c):
-        return r, c
-
-    def there(r, c):
-        return place(r, c, rows, cols)
-
-    def back_row(r, c):
-        return (r - 1) % rows, c
-
-    def back_col(r, c):
-        return r, (c - 1) % cols
 
     def next_row(r, c):
         return (r + 1) % rows, c
@@ -224,23 +242,24 @@
     def next_col(r, c):
         return r, (c + 1) % cols
 
-    def late_first(r, c):
-        return (c - 1) % RUN >= LATE_FIRST
-
-    def late_second(r, c):
-        return c % RUN >= LATE_SECOND
-
-    def negate(f):
-        return lambda r, c: not f(r, c)
+    def late(r, c):
+        return c % RUN >= LATE
+
+    def last(r, c):
+        return r % (rows // 2) == 0 and c % RUN == 0
+
+    def to_last(r, c):
+        return last(*next_col(r, c))
 
     return {
-        "first_tgt_a": pairs(back_col, there, late_first),
-        "first_src": pairs(back_row, there),
-        "moved": pairs(home, there, lambda r, c: there(r, c) != (r, c)),
-        "first_tgt_b": pairs(back_col, there, negate(late_first)),
-        "second_tgt_a": pairs(there, next_col, late_second),
-        "second_src": pairs(there, next_row),
-        "second_tgt_b": pairs(there, next_col, negate(late_second)),
+        "first_tgt_a": pairs(next_col, lambda r, c: late(r, c) and not to_last(r, c)),
+        "first_src": pairs(next_row, lambda r, c: True),
+        "first_tgt_b": pairs(next_col, lambda r, c: not late(r, c)),
+        "first_tgt_c": pairs(next_col, to_last),
+        "second_tgt_a": pairs(next_col, late),
+        "second_src": pairs(next_row, lambda r, c: not last(r, c)),
+        "second_src_c": pairs(next_row, last),
+        "second_tgt_b": pairs(next_col, lambda r, c: not late(r, c)),
     }
 
 
@@ -262,7 +281,7 @@
     params = pltpu.CompilerParams(vmem_limit_bytes=VMEM_LIMIT)
 
     operands = (src, source_acc, tgt, target_acc, relations.T, src_index, dst_index, rel_index, neg_index)
-    tgt_a, src, moved, tgt_b, own = pl.pallas_call(
+    tgt_a, src, tgt_b, tgt_c, own = pl.pallas_call(
         first_kernel,
         name="first_step",
         out_shape=(
@@ -280,30 +299,53 @@
     )(*[pltpu.with_memory_space_constraint(x, pltpu.HBM) for x in operands])
     tgt_a = send(tgt_a, "first_tgt_a")
     src = send(src, "first_src")
-    moved = send(moved, "moved")
     tgt_b = send(tgt_b, "first_tgt_b")
-    tgt_a, src, tgt_b = pl.pallas_call(
+    tgt_c = send(tgt_c, "first_tgt_c")
+    tgt_a, src_a, tgt = pl.pallas_call(
         functools.partial(second_kernel, negs),
         name="second_step",
-        out_shape=(block, block, block),
-        in_specs=[vmem] * 5,
+        out_shape=(block,) * 3,
+        in_specs=[vmem] * 4,
         out_specs=(vmem,) * 3,
         compiler_params=params,
-    )(tgt_a, src, moved, tgt_b, own)
+        cost_estimate=cost(0.001),
+    )(tgt_a, src, tgt_b, own)
     tgt_a = send(tgt_a, "second_tgt_a")
-    src = send(src, "second_src")
+    src_a = send(src_a, "second_src")
+    tgt_b, src_c = pl.pallas_call(
+        functools.partial(last_kernel, negs),
+        name="last_second_step",
+        out_shape=(block,) * 2,
+        in_specs=[vmem] * 4,
+        out_specs=(vmem,) * 2,
+        compiler_params=params,
+        cost_estimate=cost(0.001),
+    )(tgt, tgt_c, src, own)
+    src_c = send(src_c, "second_src_c")
     tgt_b = send(tgt_b, "second_tgt_b")
     table = pltpu.HBM((width, entities), f32)
     sums = pltpu.HBM((1, 1, entities), f32)
-    src, src_sums, tgt, tgt_sums = pl.pallas_call(
+    out = pl.pallas_call(
         unpack_kernel,
         name="unpack",
         out_shape=(table, sums, table, sums),
-        in_specs=[vmem] * 3,
+        in_specs=[vmem] * 2,
         out_specs=(hbm,) * 4,
-        scratch_shapes=[pltpu.SemaphoreType.DMA((4,))],
-        compiler_params=params,
-    )(tgt_a, src, tgt_b)
+        scratch_shapes=[pltpu.SemaphoreType.DMA((2,))] * 2,
+        compiler_params=params,
+        cost_estimate=cost(FINAL_COST),
+    )(tgt_a, src_a)
+    src, src_sums, tgt, tgt_sums = pl.pallas_call(
+        unpack_rest_kernel,
+        name="unpack_rest",
+        out_shape=(table, sums, table, sums),
+        in_specs=[hbm] * 4 + [vmem] * 2,
+        out_specs=(hbm,) * 4,
+        input_output_aliases={i: i for i in range(4)},
+        scratch_shapes=[pltpu.SemaphoreType.DMA((2,))] * 2,
+        compiler_params=params,
+        cost_estimate=cost(FINAL_COST),
+    )(*out, src_c, tgt_b)
     return src.T[None, None], src_sums, tgt.T[None, None], tgt_sums
 
 

time: 52.8 us -> 47.6 us (0.902)
  the two profiles are of different devices: /device:TPU:1 before, /device:TPU:672 now
where the time goes in v8:
time: 47.6 us; the launch traced here: 47.3 us
  waiting for transfers between devices  22.8 us (48%)
  starting transfers between devices  16.4 us (34%)
  Pallas kernels  7.41 us (16%)
  between operations  0.76 us (2%)
    ppermute x8, waiting for transfers between devices, send(): return lax.ppermute(x, ('row', 'col'), route[name])  22.8 us
    ppermute x8, starting transfers between devices, send(): return lax.ppermute(x, ('row', 'col'), route[name])  16.4 us
    pallas_call x1, Pallas kernels, on_device(): pl.pallas_call(first_kernel, name='first_step', out_shape=(block, block,...  4.88 us
    pallas_call x1, Pallas kernels, on_device(): pl.pallas_call(functools.partial(second_kernel, negs), name='second_step'...  1.05 us
  transfers between devices with their start and end apart: 8, of which 3 were waited for; matrix products, arithmetic and copies ran while one was open for 0% of the time, Pallas kernels for 4%

profile of v8, /device:TPU:672, one launch (start us, length us, event | category | flops | bytes accessed | tf_op | source)
XLA Modules:
  0.0 47.3 jit_solution(17564729736709685055)
XLA Ops:
  0.6 4.9 %first_step.1 = (f32[408,128]{1,0:T(8,128)S(1)}, f32[408,128]{1,0:T(8,128)S(1)}, f32[408,128]{1,0:T(8,128)S(1)}, f32[408,128]{1,0:T(8,128)S(1)}, f32[408,128]{1,0:T(8,128)S(1)}) custom-call(f32[400,128]{1,0:T(8,128)} %bitcast.14, f32[1,1,128]{2,1,0:T(1,128)} %src_sums_hbm.1, f32[400,128]{1,0:T(8,128)} %bitcast.15, f32[1,1,128]{2,1,0:T(1,128)} %tgt_sums_hbm.1, ...), custom_call_target="tpu_custom_call" | custom-call | tf_op jit(solution)/shard_map/first_step/pallas_call | solution.py:284
  5.5 4.3 %collective-permute-start = (f32[408,128]{1,0:T(8,128)S(1)}, f32[408,128]{1,0:T(8,128)S(1)}, u32[]{:S(2)}, u32[]{:S(2)}) collective-permute-start(f32[408,128]{1,0:T(8,128)S(1)} %get-tuple-element.22), channel_id=1, source_target_pairs={{5,6},{6,7},{13,14},{14,15},{21,22},{22,23},{29,30},{30,31},{37,38... | collective-permute-start | bytes 626696 | tf_op jit(solution)/shard_map/ppermute | solution.py:277
  9.8 1.9 %collective-permute-start.1 = (f32[408,128]{1,0:T(8,128)S(1)}, f32[408,128]{1,0:T(8,128)S(1)}, u32[]{:S(2)}, u32[]{:S(2)}) collective-permute-start(f32[408,128]{1,0:T(8,128)S(1)} %get-tuple-element.23), channel_id=1, source_target_pairs={{0,32},{1,33},{2,34},{3,35},{4,36},{5,37},{6,38},{7,39},{8,40},{9,... | collective-permute-start | bytes 626696 | tf_op jit(solution)/shard_map/ppermute | solution.py:277
  11.8 1.3 %collective-permute-start.2 = (f32[408,128]{1,0:T(8,128)S(1)}, f32[408,128]{1,0:T(8,128)S(1)}, u32[]{:S(2)}, u32[]{:S(2)}) collective-permute-start(f32[408,128]{1,0:T(8,128)S(1)} %get-tuple-element.24), channel_id=1, source_target_pairs={{0,1},{1,2},{2,3},{3,4},{4,5},{8,9},{9,10},{10,11},{11,12},{12,13}... | collective-permute-start | bytes 626696 | tf_op jit(solution)/shard_map/ppermute | solution.py:277
  13.1 0.7 %collective-permute-start.5 = (f32[408,128]{1,0:T(8,128)S(1)}, f32[408,128]{1,0:T(8,128)S(1)}, u32[]{:S(2)}, u32[]{:S(2)}) collective-permute-start(f32[408,128]{1,0:T(8,128)S(1)} %get-tuple-element.33), channel_id=1, source_target_pairs={{7,8},{15,16},{23,24},{31,0},{519,520},{527,528},{535,536},{543,512}} | collective-permute-start | bytes 626696 | tf_op jit(solution)/shard_map/ppermute | solution.py:277
  13.7 0.5 %collective-permute-done.tgt_a_ref = f32[408,128]{1,0:T(8,128)S(1)} collective-permute-done((f32[408,128]{1,0:T(8,128)S(1)}, f32[408,128]{1,0:T(8,128)S(1)}, u32[]{:S(2)}, u32[]{:S(2)}) %collective-permute-start) | collective-permute-done | bytes 208928 | tf_op jit(solution)/shard_map/ppermute | solution.py:277
  14.2 11.2 %collective-permute-done.1.src_ref = f32[408,128]{1,0:T(8,128)S(1)} collective-permute-done((f32[408,128]{1,0:T(8,128)S(1)}, f32[408,128]{1,0:T(8,128)S(1)}, u32[]{:S(2)}, u32[]{:S(2)}) %collective-permute-start.1) | collective-permute-done | bytes 208928 | tf_op jit(solution)/shard_map/ppermute | solution.py:277
  25.4 0.0 collective-permute-done.2.tgt_b_ref
  25.4 1.0 %second_step.1 = (f32[408,128]{1,0:T(8,128)S(1)}, f32[408,128]{1,0:T(8,128)S(1)}, f32[408,128]{1,0:T(8,128)S(1)}) custom-call(f32[408,128]{1,0:T(8,128)S(1)} %collective-permute-done.tgt_a_ref, f32[408,128]{1,0:T(8,128)S(1)} %collective-permute-done.1.src_ref, f32[408,128]{1,0:T(8,128)S(1)} %collective-permute-done.2.tgt_b_ref, ...), custom_call_target="tpu_custom_call" | custom-call | flops 1000000 | tf_op jit(solution)/shard_map/second_step/pallas_call | solution.py:304
  26.5 4.3 %collective-permute-start.3 = (f32[408,128]{1,0:T(8,128)S(1)}, f32[408,128]{1,0:T(8,128)S(1)}, u32[]{:S(2)}, u32[]{:S(2)}) collective-permute-start(f32[408,128]{1,0:T(8,128)S(1)} %get-tuple-element.26), channel_id=1, source_target_pairs={{5,6},{6,7},{7,8},{13,14},{14,15},{15,16},{21,22},{22,23},{23,24},... | collective-permute-start | bytes 626696 | tf_op jit(solution)/shard_map/ppermute | solution.py:277
  30.8 1.9 %collective-permute-start.4 = (f32[408,128]{1,0:T(8,128)S(1)}, f32[408,128]{1,0:T(8,128)S(1)}, u32[]{:S(2)}, u32[]{:S(2)}) collective-permute-start(f32[408,128]{1,0:T(8,128)S(1)} %get-tuple-element.27), channel_id=1, source_target_pairs={{1,33},{2,34},{3,35},{4,36},{5,37},{6,38},{7,39},{9,41},{10,42},{1... | collective-permute-start | bytes 626696 | tf_op jit(solution)/shard_map/ppermute | solution.py:277
  32.7 0.0 collective-permute-done.5.tgt_c_ref
  32.8 0.7 %collective-permute-start.6 = (f32[408,128]{1,0:T(8,128)S(1)}, f32[408,128]{1,0:T(8,128)S(1)}, u32[]{:S(2)}, u32[]{:S(2)}) collective-permute-start(f32[408,128]{1,0:T(8,128)S(1)} %get-tuple-element.34), channel_id=1, source_target_pairs={{0,32},{8,40},{16,48},{24,56},{512,544},{520,552},{528,560},{536,5... | collective-permute-start | bytes 626696 | tf_op jit(solution)/shard_map/ppermute | solution.py:277
  33.5 1.3 %collective-permute-start.7 = (f32[408,128]{1,0:T(8,128)S(1)}, f32[408,128]{1,0:T(8,128)S(1)}, u32[]{:S(2)}, u32[]{:S(2)}) collective-permute-start(f32[408,128]{1,0:T(8,128)S(1)} %get-tuple-element.35), channel_id=1, source_target_pairs={{0,1},{1,2},{2,3},{3,4},{4,5},{8,9},{9,10},{10,11},{11,12},{12,13}... | collective-permute-start | bytes 626696 | tf_op jit(solution)/shard_map/ppermute | solution.py:277
  34.8 0.0 collective-permute-done.3.tgt_ref
  34.8 11.1 %collective-permute-done.4.src_ref = f32[408,128]{1,0:T(8,128)S(1)} collective-permute-done((f32[408,128]{1,0:T(8,128)S(1)}, f32[408,128]{1,0:T(8,128)S(1)}, u32[]{:S(2)}, u32[]{:S(2)}) %collective-permute-start.4) | collective-permute-done | bytes 208928 | tf_op jit(solution)/shard_map/ppermute | solution.py:277
  45.8 0.7 %unpack.1 = (f32[400,128]{1,0:T(8,128)}, f32[1,1,128]{2,1,0:T(1,128)}, f32[400,128]{1,0:T(8,128)}, f32[1,1,128]{2,1,0:T(1,128)}) custom-call(f32[408,128]{1,0:T(8,128)S(1)} %collective-permute-done.3.tgt_ref, f32[408,128]{1,0:T(8,128)S(1)} %collective-permute-done.4.src_ref), custom_call_target="tpu_custom_call" | custom-call | flops 49999998976 | tf_op jit(solution)/shard_map/unpack/pallas_call | solution.py:328
  46.6 0.0 collective-permute-done.6.src_ref
  46.6 0.0 collective-permute-done.7.tgt_ref
  46.6 0.7 %unpack_rest.1 = (f32[400,128]{1,0:T(8,128)}, f32[1,1,128]{2,1,0:T(1,128)}, f32[400,128]{1,0:T(8,128)}, f32[1,1,128]{2,1,0:T(1,128)}) custom-call(f32[400,128]{1,0:T(8,128)} %get-tuple-element.28._0, f32[1,1,128]{2,1,0:T(1,128)} %get-tuple-element.29._1, ...), custom_call_target="tpu_custom_call", output_to_operand_aliasing={{0}: (0, {}), {1}: (1, {}), {2}: (2, {}), {3}: (3, {})} | custom-call | flops 49999998976 | tf_op jit(solution)/shard_map/unpack_rest/pallas_call | solution.py:338
  (1 shorter events, 0.0 us)
Async XLA Ops:
  5.5 8.7 %collective-permute-start = (f32[408,128]{1,0:T(8,128)S(1)}, f32[408,128]{1,0:T(8,128)S(1)}, u32[]{:S(2)}, u32[]{:S(2)}) collective-permute-start(f32[408,128]{1,0:T(8,128)S(1)} %get-tuple-element.22), channel_id=1, source_target_pairs={{5,6},{6,7},{13,14},{14,15},{21,22},{22,23},{29,30},{30,31},{37,38... | collective-permute-start | bytes 626696 | tf_op jit(solution)/shard_map/ppermute | solution.py:277
  9.8 15.6 %collective-permute-start.1 = (f32[408,128]{1,0:T(8,128)S(1)}, f32[408,128]{1,0:T(8,128)S(1)}, u32[]{:S(2)}, u32[]{:S(2)}) collective-permute-start(f32[408,128]{1,0:T(8,128)S(1)} %get-tuple-element.23), channel_id=1, source_target_pairs={{0,32},{1,33},{2,34},{3,35},{4,36},{5,37},{6,38},{7,39},{8,40},{9,... | collective-permute-start | bytes 626696 | tf_op jit(solution)/shard_map/ppermute | solution.py:277
  11.8 13.7 %collective-permute-start.2 = (f32[408,128]{1,0:T(8,128)S(1)}, f32[408,128]{1,0:T(8,128)S(1)}, u32[]{:S(2)}, u32[]{:S(2)}) collective-permute-start(f32[408,128]{1,0:T(8,128)S(1)} %get-tuple-element.24), channel_id=1, source_target_pairs={{0,1},{1,2},{2,3},{3,4},{4,5},{8,9},{9,10},{10,11},{11,12},{12,13}... | collective-permute-start | bytes 626696 | tf_op jit(solution)/shard_map/ppermute | solution.py:277
  13.1 19.7 %collective-permute-start.5 = (f32[408,128]{1,0:T(8,128)S(1)}, f32[408,128]{1,0:T(8,128)S(1)}, u32[]{:S(2)}, u32[]{:S(2)}) collective-permute-start(f32[408,128]{1,0:T(8,128)S(1)} %get-tuple-element.33), channel_id=1, source_target_pairs={{7,8},{15,16},{23,24},{31,0},{519,520},{527,528},{535,536},{543,512}} | collective-permute-start | bytes 626696 | tf_op jit(solution)/shard_map/ppermute | solution.py:277
  26.5 8.3 %collective-permute-start.3 = (f32[408,128]{1,0:T(8,128)S(1)}, f32[408,128]{1,0:T(8,128)S(1)}, u32[]{:S(2)}, u32[]{:S(2)}) collective-permute-start(f32[408,128]{1,0:T(8,128)S(1)} %get-tuple-element.26), channel_id=1, source_target_pairs={{5,6},{6,7},{7,8},{13,14},{14,15},{15,16},{21,22},{22,23},{23,24},... | collective-permute-start | bytes 626696 | tf_op jit(solution)/shard_map/ppermute | solution.py:277
  30.8 15.0 %collective-permute-start.4 = (f32[408,128]{1,0:T(8,128)S(1)}, f32[408,128]{1,0:T(8,128)S(1)}, u32[]{:S(2)}, u32[]{:S(2)}) collective-permute-start(f32[408,128]{1,0:T(8,128)S(1)} %get-tuple-element.27), channel_id=1, source_target_pairs={{1,33},{2,34},{3,35},{4,36},{5,37},{6,38},{7,39},{9,41},{10,42},{1... | collective-permute-start | bytes 626696 | tf_op jit(solution)/shard_map/ppermute | solution.py:277
  32.8 13.8 %collective-permute-start.6 = (f32[408,128]{1,0:T(8,128)S(1)}, f32[408,128]{1,0:T(8,128)S(1)}, u32[]{:S(2)}, u32[]{:S(2)}) collective-permute-start(f32[408,128]{1,0:T(8,128)S(1)} %get-tuple-element.34), channel_id=1, source_target_pairs={{0,32},{8,40},{16,48},{24,56},{512,544},{520,552},{528,560},{536,5... | collective-permute-start | bytes 626696 | tf_op jit(solution)/shard_map/ppermute | solution.py:277
  33.5 13.1 %collective-permute-start.7 = (f32[408,128]{1,0:T(8,128)S(1)}, f32[408,128]{1,0:T(8,128)S(1)}, u32[]{:S(2)}, u32[]{:S(2)}) collective-permute-start(f32[408,128]{1,0:T(8,128)S(1)} %get-tuple-element.35), channel_id=1, source_target_pairs={{0,1},{1,2},{2,3},{3,4},{4,5},{8,9},{9,10},{10,11},{11,12},{12,13}... | collective-permute-start | bytes 626696 | tf_op jit(solution)/shard_map/ppermute | solution.py:277

commit v9 on v8

--- a/solution.py
+++ b/solution.py
@@ -14,7 +14,8 @@
 PAD = 8
 CHUNK = 512
 RUN = 8
-LATE = 5
+LATE_FIRST = 6
+LATE_SECOND = 7
 FINAL_COST = 50
 VMEM_LIMIT = 32 * 1024 * 1024
 
@@ -163,7 +164,7 @@
 
     @pl.when(jnp.logical_not(is_last(row, col, lax.axis_size("row"))))
     def _():
-        tgt = jnp.where(from_late(col, LATE), tgt_a_ref[...], tgt_b_ref[...])
+        tgt = jnp.where(from_late(col, LATE_FIRST), tgt_a_ref[...], tgt_b_ref[...])
         src, src_sums, tgt, tgt_sums = second(negs, tgt, src_ref, own_ref)
         store_block(src_out, src, src_sums)
         store_block(tgt_a_out, tgt, tgt_sums)
@@ -206,7 +207,7 @@
 
 
 def receives(row, col, rows):
-    return jnp.logical_not(is_last(row + rows - 1, col, rows)), from_late(col, LATE)
+    return jnp.logical_not(is_last(row + rows - 1, col, rows)), from_late(col, LATE_SECOND)
 
 
 def unpack_kernel(tgt_ref, src_ref, src_out, src_sums_out, tgt_out, tgt_sums_out, src_sems, tgt_sems):
@@ -242,8 +243,11 @@
     def next_col(r, c):
         return r, (c + 1) % cols
 
-    def late(r, c):
-        return c % RUN >= LATE
+    def late_first(r, c):
+        return c % RUN >= LATE_FIRST
+
+    def late_second(r, c):
+        return c % RUN >= LATE_SECOND
 
     def last(r, c):
         return r % (rows // 2) == 0 and c % RUN == 0
@@ -252,14 +256,14 @@
         return last(*next_col(r, c))
 
     return {
-        "first_tgt_a": pairs(next_col, lambda r, c: late(r, c) and not to_last(r, c)),
+        "first_tgt_a": pairs(next_col, lambda r, c: late_first(r, c) and not to_last(r, c)),
         "first_src": pairs(next_row, lambda r, c: True),
-        "first_tgt_b": pairs(next_col, lambda r, c: not late(r, c)),
+        "first_tgt_b": pairs(next_col, lambda r, c: not late_first(r, c)),
         "first_tgt_c": pairs(next_col, to_last),
-        "second_tgt_a": pairs(next_col, late),
+        "second_tgt_a": pairs(next_col, late_second),
         "second_src": pairs(next_row, lambda r, c: not last(r, c)),
         "second_src_c": pairs(next_row, last),
-        "second_tgt_b": pairs(next_col, lambda r, c: not late(r, c)),
+        "second_tgt_b": pairs(next_col, lambda r, c: not late_second(r, c)),
     }
 
 

time: 47.6 us -> 45.7 us (0.960)
  the two profiles are of different devices: /device:TPU:672 before, /device:TPU:1 now
where the time goes in v9:
time: 45.7 us; the launch traced here: 45.2 us
  starting transfers between devices  20.6 us (45%)
  waiting for transfers between devices  16.5 us (36%)
  Pallas kernels  7.41 us (16%)
  between operations  0.75 us (2%)
    ppermute x8, starting transfers between devices, send(): return lax.ppermute(x, ('row', 'col'), route[name])  20.6 us
    ppermute x8, waiting for transfers between devices, send(): return lax.ppermute(x, ('row', 'col'), route[name])  16.5 us
    pallas_call x1, Pallas kernels, on_device(): pl.pallas_call(first_kernel, name='first_step', out_shape=(block, block,...  4.89 us
    pallas_call x1, Pallas kernels, on_device(): pl.pallas_call(functools.partial(second_kernel, negs), name='second_step'...  1.05 us
  transfers between devices with their start and end apart: 8, of which 3 were waited for; matrix products, arithmetic and copies ran while one was open for 0% of the time, Pallas kernels for 4%

profile of v9, /device:TPU:1, one launch (start us, length us, event | category | flops | bytes accessed | tf_op | source)
XLA Modules:
  0.0 45.2 jit_solution(12436868950344418185)
XLA Ops:
  0.6 4.9 %first_step.1 = (f32[408,128]{1,0:T(8,128)S(1)}, f32[408,128]{1,0:T(8,128)S(1)}, f32[408,128]{1,0:T(8,128)S(1)}, f32[408,128]{1,0:T(8,128)S(1)}, f32[408,128]{1,0:T(8,128)S(1)}) custom-call(f32[400,128]{1,0:T(8,128)} %bitcast.14, f32[1,1,128]{2,1,0:T(1,128)} %src_sums_hbm.1, f32[400,128]{1,0:T(8,128)} %bitcast.15, f32[1,1,128]{2,1,0:T(1,128)} %tgt_sums_hbm.1, ...), custom_call_target="tpu_custom_call" | custom-call | tf_op jit(solution)/shard_map/first_step/pallas_call | solution.py:288
  5.5 1.3 %collective-permute-start = (f32[408,128]{1,0:T(8,128)S(1)}, f32[408,128]{1,0:T(8,128)S(1)}, u32[]{:S(2)}, u32[]{:S(2)}) collective-permute-start(f32[408,128]{1,0:T(8,128)S(1)} %get-tuple-element.22), channel_id=1, source_target_pairs={{6,7},{14,15},{22,23},{30,31},{38,39},{39,40},{46,47},{47,48},{54,... | collective-permute-start | bytes 626696 | tf_op jit(solution)/shard_map/ppermute | solution.py:281
  6.8 4.5 %collective-permute-start.1 = (f32[408,128]{1,0:T(8,128)S(1)}, f32[408,128]{1,0:T(8,128)S(1)}, u32[]{:S(2)}, u32[]{:S(2)}) collective-permute-start(f32[408,128]{1,0:T(8,128)S(1)} %get-tuple-element.23), channel_id=1, source_target_pairs={{0,32},{1,33},{2,34},{3,35},{4,36},{5,37},{6,38},{7,39},{8,40},{9,... | collective-permute-start | bytes 626696 | tf_op jit(solution)/shard_map/ppermute | solution.py:281
  11.3 4.3 %collective-permute-start.2 = (f32[408,128]{1,0:T(8,128)S(1)}, f32[408,128]{1,0:T(8,128)S(1)}, u32[]{:S(2)}, u32[]{:S(2)}) collective-permute-start(f32[408,128]{1,0:T(8,128)S(1)} %get-tuple-element.24), channel_id=1, source_target_pairs={{0,1},{1,2},{2,3},{3,4},{4,5},{5,6},{8,9},{9,10},{10,11},{11,12},{... | collective-permute-start | bytes 626696 | tf_op jit(solution)/shard_map/ppermute | solution.py:281
  15.7 0.7 %collective-permute-start.5 = (f32[408,128]{1,0:T(8,128)S(1)}, f32[408,128]{1,0:T(8,128)S(1)}, u32[]{:S(2)}, u32[]{:S(2)}) collective-permute-start(f32[408,128]{1,0:T(8,128)S(1)} %get-tuple-element.33), channel_id=1, source_target_pairs={{7,8},{15,16},{23,24},{31,0},{519,520},{527,528},{535,536},{543,512}} | collective-permute-start | bytes 626696 | tf_op jit(solution)/shard_map/ppermute | solution.py:281
  16.3 13.6 %collective-permute-done.tgt_a_ref = f32[408,128]{1,0:T(8,128)S(1)} collective-permute-done((f32[408,128]{1,0:T(8,128)S(1)}, f32[408,128]{1,0:T(8,128)S(1)}, u32[]{:S(2)}, u32[]{:S(2)}) %collective-permute-start) | collective-permute-done | bytes 208928 | tf_op jit(solution)/shard_map/ppermute | solution.py:281
  30.0 0.0 collective-permute-done.1.src_ref
  30.0 0.0 collective-permute-done.2.tgt_b_ref
  30.0 1.1 %second_step.1 = (f32[408,128]{1,0:T(8,128)S(1)}, f32[408,128]{1,0:T(8,128)S(1)}, f32[408,128]{1,0:T(8,128)S(1)}) custom-call(f32[408,128]{1,0:T(8,128)S(1)} %collective-permute-done.tgt_a_ref, f32[408,128]{1,0:T(8,128)S(1)} %collective-permute-done.1.src_ref, f32[408,128]{1,0:T(8,128)S(1)} %collective-permute-done.2.tgt_b_ref, ...), custom_call_target="tpu_custom_call" | custom-call | flops 1000000 | tf_op jit(solution)/shard_map/second_step/pallas_call | solution.py:308
  31.0 1.3 %collective-permute-start.3 = (f32[408,128]{1,0:T(8,128)S(1)}, f32[408,128]{1,0:T(8,128)S(1)}, u32[]{:S(2)}, u32[]{:S(2)}) collective-permute-start(f32[408,128]{1,0:T(8,128)S(1)} %get-tuple-element.26), channel_id=1, source_target_pairs={{7,8},{15,16},{23,24},{31,0},{39,40},{47,48},{55,56},{63,32},{71,7... | collective-permute-start | bytes 626696 | tf_op jit(solution)/shard_map/ppermute | solution.py:281
  32.3 5.9 %collective-permute-start.4 = (f32[408,128]{1,0:T(8,128)S(1)}, f32[408,128]{1,0:T(8,128)S(1)}, u32[]{:S(2)}, u32[]{:S(2)}) collective-permute-start(f32[408,128]{1,0:T(8,128)S(1)} %get-tuple-element.27), channel_id=1, source_target_pairs={{1,33},{2,34},{3,35},{4,36},{5,37},{6,38},{7,39},{9,41},{10,42},{1... | collective-permute-start | bytes 626696 | tf_op jit(solution)/shard_map/ppermute | solution.py:281
  38.3 0.0 collective-permute-done.5.tgt_c_ref
  38.3 1.3 %collective-permute-start.6 = (f32[408,128]{1,0:T(8,128)S(1)}, f32[408,128]{1,0:T(8,128)S(1)}, u32[]{:S(2)}, u32[]{:S(2)}) collective-permute-start(f32[408,128]{1,0:T(8,128)S(1)} %get-tuple-element.34), channel_id=1, source_target_pairs={{0,32},{8,40},{16,48},{24,56},{512,544},{520,552},{528,560},{536,5... | collective-permute-start | bytes 626696 | tf_op jit(solution)/shard_map/ppermute | solution.py:281
  39.6 1.3 %collective-permute-start.7 = (f32[408,128]{1,0:T(8,128)S(1)}, f32[408,128]{1,0:T(8,128)S(1)}, u32[]{:S(2)}, u32[]{:S(2)}) collective-permute-start(f32[408,128]{1,0:T(8,128)S(1)} %get-tuple-element.35), channel_id=1, source_target_pairs={{0,1},{1,2},{2,3},{3,4},{4,5},{5,6},{6,7},{8,9},{9,10},{10,11},{11... | collective-permute-start | bytes 626696 | tf_op jit(solution)/shard_map/ppermute | solution.py:281
  40.9 0.5 %collective-permute-done.3.tgt_ref = f32[408,128]{1,0:T(8,128)S(1)} collective-permute-done((f32[408,128]{1,0:T(8,128)S(1)}, f32[408,128]{1,0:T(8,128)S(1)}, u32[]{:S(2)}, u32[]{:S(2)}) %collective-permute-start.3) | collective-permute-done | bytes 208928 | tf_op jit(solution)/shard_map/ppermute | solution.py:281
  41.5 0.0 collective-permute-done.4.src_ref
  41.5 0.7 %unpack.1 = (f32[400,128]{1,0:T(8,128)}, f32[1,1,128]{2,1,0:T(1,128)}, f32[400,128]{1,0:T(8,128)}, f32[1,1,128]{2,1,0:T(1,128)}) custom-call(f32[408,128]{1,0:T(8,128)S(1)} %collective-permute-done.3.tgt_ref, f32[408,128]{1,0:T(8,128)S(1)} %collective-permute-done.4.src_ref), custom_call_target="tpu_custom_call" | custom-call | flops 49999998976 | tf_op jit(solution)/shard_map/unpack/pallas_call | solution.py:332
  42.2 0.0 collective-permute-done.6.src_ref
  42.2 2.3 %collective-permute-done.7.tgt_ref = f32[408,128]{1,0:T(8,128)S(1)} collective-permute-done((f32[408,128]{1,0:T(8,128)S(1)}, f32[408,128]{1,0:T(8,128)S(1)}, u32[]{:S(2)}, u32[]{:S(2)}) %collective-permute-start.7) | collective-permute-done | bytes 208928 | tf_op jit(solution)/shard_map/ppermute | solution.py:281
  44.5 0.7 %unpack_rest.1 = (f32[400,128]{1,0:T(8,128)}, f32[1,1,128]{2,1,0:T(1,128)}, f32[400,128]{1,0:T(8,128)}, f32[1,1,128]{2,1,0:T(1,128)}) custom-call(f32[400,128]{1,0:T(8,128)} %get-tuple-element.28._0, f32[1,1,128]{2,1,0:T(1,128)} %get-tuple-element.29._1, ...), custom_call_target="tpu_custom_call", output_to_operand_aliasing={{0}: (0, {}), {1}: (1, {}), {2}: (2, {}), {3}: (3, {})} | custom-call | flops 49999998976 | tf_op jit(solution)/shard_map/unpack_rest/pallas_call | solution.py:342
  (1 shorter events, 0.0 us)
Async XLA Ops:
  5.5 24.4 %collective-permute-start = (f32[408,128]{1,0:T(8,128)S(1)}, f32[408,128]{1,0:T(8,128)S(1)}, u32[]{:S(2)}, u32[]{:S(2)}) collective-permute-start(f32[408,128]{1,0:T(8,128)S(1)} %get-tuple-element.22), channel_id=1, source_target_pairs={{6,7},{14,15},{22,23},{30,31},{38,39},{39,40},{46,47},{47,48},{54,... | collective-permute-start | bytes 626696 | tf_op jit(solution)/shard_map/ppermute | solution.py:281
  6.8 23.1 %collective-permute-start.1 = (f32[408,128]{1,0:T(8,128)S(1)}, f32[408,128]{1,0:T(8,128)S(1)}, u32[]{:S(2)}, u32[]{:S(2)}) collective-permute-start(f32[408,128]{1,0:T(8,128)S(1)} %get-tuple-element.23), channel_id=1, source_target_pairs={{0,32},{1,33},{2,34},{3,35},{4,36},{5,37},{6,38},{7,39},{8,40},{9,... | collective-permute-start | bytes 626696 | tf_op jit(solution)/shard_map/ppermute | solution.py:281
  11.3 18.6 %collective-permute-start.2 = (f32[408,128]{1,0:T(8,128)S(1)}, f32[408,128]{1,0:T(8,128)S(1)}, u32[]{:S(2)}, u32[]{:S(2)}) collective-permute-start(f32[408,128]{1,0:T(8,128)S(1)} %get-tuple-element.24), channel_id=1, source_target_pairs={{0,1},{1,2},{2,3},{3,4},{4,5},{5,6},{8,9},{9,10},{10,11},{11,12},{... | collective-permute-start | bytes 626696 | tf_op jit(solution)/shard_map/ppermute | solution.py:281
  15.7 22.6 %collective-permute-start.5 = (f32[408,128]{1,0:T(8,128)S(1)}, f32[408,128]{1,0:T(8,128)S(1)}, u32[]{:S(2)}, u32[]{:S(2)}) collective-permute-start(f32[408,128]{1,0:T(8,128)S(1)} %get-tuple-element.33), channel_id=1, source_target_pairs={{7,8},{15,16},{23,24},{31,0},{519,520},{527,528},{535,536},{543,512}} | collective-permute-start | bytes 626696 | tf_op jit(solution)/shard_map/ppermute | solution.py:281
  31.0 10.5 %collective-permute-start.3 = (f32[408,128]{1,0:T(8,128)S(1)}, f32[408,128]{1,0:T(8,128)S(1)}, u32[]{:S(2)}, u32[]{:S(2)}) collective-permute-start(f32[408,128]{1,0:T(8,128)S(1)} %get-tuple-element.26), channel_id=1, source_target_pairs={{7,8},{15,16},{23,24},{31,0},{39,40},{47,48},{55,56},{63,32},{71,7... | collective-permute-start | bytes 626696 | tf_op jit(solution)/shard_map/ppermute | solution.py:281
  32.3 9.2 %collective-permute-start.4 = (f32[408,128]{1,0:T(8,128)S(1)}, f32[408,128]{1,0:T(8,128)S(1)}, u32[]{:S(2)}, u32[]{:S(2)}) collective-permute-start(f32[408,128]{1,0:T(8,128)S(1)} %get-tuple-element.27), channel_id=1, source_target_pairs={{1,33},{2,34},{3,35},{4,36},{5,37},{6,38},{7,39},{9,41},{10,42},{1... | collective-permute-start | bytes 626696 | tf_op jit(solution)/shard_map/ppermute | solution.py:281
  38.3 3.9 %collective-permute-start.6 = (f32[408,128]{1,0:T(8,128)S(1)}, f32[408,128]{1,0:T(8,128)S(1)}, u32[]{:S(2)}, u32[]{:S(2)}) collective-permute-start(f32[408,128]{1,0:T(8,128)S(1)} %get-tuple-element.34), channel_id=1, source_target_pairs={{0,32},{8,40},{16,48},{24,56},{512,544},{520,552},{528,560},{536,5... | collective-permute-start | bytes 626696 | tf_op jit(solution)/shard_map/ppermute | solution.py:281
  39.6 4.9 %collective-permute-start.7 = (f32[408,128]{1,0:T(8,128)S(1)}, f32[408,128]{1,0:T(8,128)S(1)}, u32[]{:S(2)}, u32[]{:S(2)}) collective-permute-start(f32[408,128]{1,0:T(8,128)S(1)} %get-tuple-element.35), channel_id=1, source_target_pairs={{0,1},{1,2},{2,3},{3,4},{4,5},{5,6},{6,7},{8,9},{9,10},{10,11},{11... | collective-permute-start | bytes 626696 | tf_op jit(solution)/shard_map/ppermute | solution.py:281

commit v10 on v9

--- a/solution.py
+++ b/solution.py
@@ -190,7 +190,8 @@
 
 
 def is_last(row, col, rows):
-    return jnp.logical_and(lax.rem(col, RUN) == 0, lax.rem(row, rows // 2) == 0)
+    wrap = jnp.logical_and(lax.rem(col, RUN) == 0, lax.rem(row, rows // 2) == 0)
+    return jnp.logical_or(wrap, jnp.logical_and(col == 0, lax.rem(row, 2) == 0))
 
 
 def unpack(ref, out, sums_out, sems):
@@ -219,11 +220,13 @@
     pl.when(jnp.logical_and(jnp.logical_not(takes_src), takes_tgt))(lambda: run(tgt()))
 
 
-def unpack_rest_kernel(
-    _0, _1, _2, _3, src_ref, tgt_ref, src_out, src_sums_out, tgt_out, tgt_sums_out, src_sems, tgt_sems
-):
-    takes_src, takes_tgt = receives(lax.axis_index("row"), lax.axis_index("col"), lax.axis_size("row"))
+def unpack_src_kernel(_0, _1, src_ref, src_out, src_sums_out, src_sems):
+    takes_src, _ = receives(lax.axis_index("row"), lax.axis_index("col"), lax.axis_size("row"))
     pl.when(jnp.logical_not(takes_src))(lambda: run(unpack(src_ref, src_out, src_sums_out, src_sems)))
+
+
+def unpack_tgt_kernel(_0, _1, tgt_ref, tgt_out, tgt_sums_out, tgt_sems):
+    _, takes_tgt = receives(lax.axis_index("row"), lax.axis_index("col"), lax.axis_size("row"))
     pl.when(jnp.logical_not(takes_tgt))(lambda: run(unpack(tgt_ref, tgt_out, tgt_sums_out, tgt_sems)))
 
 
@@ -250,7 +253,7 @@
         return c % RUN >= LATE_SECOND
 
     def last(r, c):
-        return r % (rows // 2) == 0 and c % RUN == 0
+        return (r % (rows // 2) == 0 and c % RUN == 0) or (c == 0 and r % 2 == 0)
 
     def to_last(r, c):
         return last(*next_col(r, c))
@@ -339,17 +342,23 @@
         compiler_params=params,
         cost_estimate=cost(FINAL_COST),
     )(tgt_a, src_a)
-    src, src_sums, tgt, tgt_sums = pl.pallas_call(
-        unpack_rest_kernel,
-        name="unpack_rest",
-        out_shape=(table, sums, table, sums),
-        in_specs=[hbm] * 4 + [vmem] * 2,
-        out_specs=(hbm,) * 4,
-        input_output_aliases={i: i for i in range(4)},
-        scratch_shapes=[pltpu.SemaphoreType.DMA((2,))] * 2,
-        compiler_params=params,
-        cost_estimate=cost(FINAL_COST),
-    )(*out, src_c, tgt_b)
+    src, src_sums, tgt, tgt_sums = out
+
+    def rest(kernel, aliases, *inputs):
+        return pl.pallas_call(
+            kernel,
+            name=kernel.__name__,
+            out_shape=(table, sums),
+            in_specs=[hbm] * (len(inputs) - 1) + [vmem],
+            out_specs=(hbm,) * 2,
+            input_output_aliases=aliases,
+            scratch_shapes=[pltpu.SemaphoreType.DMA((2,))],
+            compiler_params=params,
+            cost_estimate=cost(FINAL_COST),
+        )(*inputs)
+
+    src, src_sums = rest(unpack_src_kernel, {0: 0, 1: 1}, src, src_sums, src_c)
+    tgt, tgt_sums = rest(unpack_tgt_kernel, {0: 0, 1: 1}, tgt, tgt_sums, tgt_b)
     return src.T[None, None], src_sums, tgt.T[None, None], tgt_sums
 
 

time: 45.7 us -> 45.5 us (level)
  the two profiles are of different devices: /device:TPU:1 before, /device:TPU:16 now
where the time goes in v10:
time: 45.5 us; the launch traced here: 45.2 us
  waiting for transfers between devices  20.3 us (45%)
  starting transfers between devices  17.4 us (38%)
  Pallas kernels  6.78 us (15%)
  between operations  0.76 us (2%)
    ppermute x8, waiting for transfers between devices, send(): return lax.ppermute(x, ('row', 'col'), route[name])  20.3 us
    ppermute x8, starting transfers between devices, send(): return lax.ppermute(x, ('row', 'col'), route[name])  17.4 us
    pallas_call x1, Pallas kernels, on_device(): pl.pallas_call(first_kernel, name='first_step', out_shape=(block, block,...  4.89 us
    pallas_call x1, Pallas kernels, on_device(): pl.pallas_call(functools.partial(last_kernel, negs), name='last_second_st...  1.03 us
  transfers between devices with their start and end apart: 8, of which 4 were waited for; matrix products, arithmetic and copies ran while one was open for 0% of the time, Pallas kernels for 4%

profile of v10, /device:TPU:16, one launch (start us, length us, event | category | flops | bytes accessed | tf_op | source)
XLA Modules:
  0.0 45.2 jit_solution(6472870890007851078)
XLA Ops:
  0.6 4.9 %first_step.1 = (f32[408,128]{1,0:T(8,128)S(1)}, f32[408,128]{1,0:T(8,128)S(1)}, f32[408,128]{1,0:T(8,128)S(1)}, f32[408,128]{1,0:T(8,128)S(1)}, f32[408,128]{1,0:T(8,128)S(1)}) custom-call(f32[400,128]{1,0:T(8,128)} %bitcast.14, f32[1,1,128]{2,1,0:T(1,128)} %src_sums_hbm.1, f32[400,128]{1,0:T(8,128)} %bitcast.15, f32[1,1,128]{2,1,0:T(1,128)} %tgt_sums_hbm.1, ...), custom_call_target="tpu_custom_call" | custom-call | tf_op jit(solution)/shard_map/first_step/pallas_call | solution.py:291
  5.5 0.7 %collective-permute-start = (f32[408,128]{1,0:T(8,128)S(1)}, f32[408,128]{1,0:T(8,128)S(1)}, u32[]{:S(2)}, u32[]{:S(2)}) collective-permute-start(f32[408,128]{1,0:T(8,128)S(1)} %get-tuple-element.22), channel_id=1, source_target_pairs={{6,7},{14,15},{22,23},{30,31},{38,39},{39,40},{46,47},{47,48},{54,... | collective-permute-start | bytes 626696 | tf_op jit(solution)/shard_map/ppermute | solution.py:284
  6.2 2.4 %collective-permute-start.1 = (f32[408,128]{1,0:T(8,128)S(1)}, f32[408,128]{1,0:T(8,128)S(1)}, u32[]{:S(2)}, u32[]{:S(2)}) collective-permute-start(f32[408,128]{1,0:T(8,128)S(1)} %get-tuple-element.23), channel_id=1, source_target_pairs={{0,32},{1,33},{2,34},{3,35},{4,36},{5,37},{6,38},{7,39},{8,40},{9,... | collective-permute-start | bytes 626696 | tf_op jit(solution)/shard_map/ppermute | solution.py:284
  8.6 4.7 %collective-permute-start.2 = (f32[408,128]{1,0:T(8,128)S(1)}, f32[408,128]{1,0:T(8,128)S(1)}, u32[]{:S(2)}, u32[]{:S(2)}) collective-permute-start(f32[408,128]{1,0:T(8,128)S(1)} %get-tuple-element.24), channel_id=1, source_target_pairs={{0,1},{1,2},{2,3},{3,4},{4,5},{5,6},{8,9},{9,10},{10,11},{11,12},{... | collective-permute-start | bytes 626696 | tf_op jit(solution)/shard_map/ppermute | solution.py:284
  13.3 1.3 %collective-permute-start.5 = (f32[408,128]{1,0:T(8,128)S(1)}, f32[408,128]{1,0:T(8,128)S(1)}, u32[]{:S(2)}, u32[]{:S(2)}) collective-permute-start(f32[408,128]{1,0:T(8,128)S(1)} %get-tuple-element.31), channel_id=1, source_target_pairs={{7,8},{15,16},{23,24},{31,0},{95,64},{159,128},{223,192},{287,256}... | collective-permute-start | bytes 626696 | tf_op jit(solution)/shard_map/ppermute | solution.py:284
  14.6 0.0 collective-permute-done.tgt_a_ref
  14.6 6.5 %collective-permute-done.1.src_ref = f32[408,128]{1,0:T(8,128)S(1)} collective-permute-done((f32[408,128]{1,0:T(8,128)S(1)}, f32[408,128]{1,0:T(8,128)S(1)}, u32[]{:S(2)}, u32[]{:S(2)}) %collective-permute-start.1) | collective-permute-done | bytes 208928 | tf_op jit(solution)/shard_map/ppermute | solution.py:284
  21.1 0.0 collective-permute-done.2.tgt_b_ref
  21.1 1.3 %collective-permute-start.3 = (f32[408,128]{1,0:T(8,128)S(1)}, f32[408,128]{1,0:T(8,128)S(1)}, u32[]{:S(2)}, u32[]{:S(2)}) collective-permute-start(f32[408,128]{1,0:T(8,128)S(1)} %get-tuple-element.26), channel_id=1, source_target_pairs={{7,8},{15,16},{23,24},{31,0},{39,40},{47,48},{55,56},{63,32},{71,7... | collective-permute-start | bytes 626696 | tf_op jit(solution)/shard_map/ppermute | solution.py:284
  22.4 1.3 %collective-permute-start.4 = (f32[408,128]{1,0:T(8,128)S(1)}, f32[408,128]{1,0:T(8,128)S(1)}, u32[]{:S(2)}, u32[]{:S(2)}) collective-permute-start(f32[408,128]{1,0:T(8,128)S(1)} %get-tuple-element.27), channel_id=1, source_target_pairs={{1,33},{2,34},{3,35},{4,36},{5,37},{6,38},{7,39},{9,41},{10,42},{1... | collective-permute-start | bytes 626696 | tf_op jit(solution)/shard_map/ppermute | solution.py:284
  23.7 6.4 %collective-permute-done.5.tgt_c_ref = f32[408,128]{1,0:T(8,128)S(1)} collective-permute-done((f32[408,128]{1,0:T(8,128)S(1)}, f32[408,128]{1,0:T(8,128)S(1)}, u32[]{:S(2)}, u32[]{:S(2)}) %collective-permute-start.5) | collective-permute-done | bytes 208928 | tf_op jit(solution)/shard_map/ppermute | solution.py:284
  30.1 1.0 %last_second_step.1 = (f32[408,128]{1,0:T(8,128)S(1)}, f32[408,128]{1,0:T(8,128)S(1)}) custom-call(f32[408,128]{1,0:T(8,128)S(1)} %get-tuple-element.30.done_tgt_ref, f32[408,128]{1,0:T(8,128)S(1)} %collective-permute-done.5.tgt_c_ref, f32[408,128]{1,0:T(8,128)S(1)} %collective-permute-done.1.src_ref, f32[408,128]{1,0:T(8,128)S(1)} %get-tuple-element.25.own_ref), custom_call_target="tpu_custom_call" | custom-call | flops 1000000 | tf_op jit(solution)/shard_map/last_second_step/pallas_call | solution.py:322
  31.2 4.5 %collective-permute-start.6 = (f32[408,128]{1,0:T(8,128)S(1)}, f32[408,128]{1,0:T(8,128)S(1)}, u32[]{:S(2)}, u32[]{:S(2)}) collective-permute-start(f32[408,128]{1,0:T(8,128)S(1)} %get-tuple-element.32), channel_id=1, source_target_pairs={{0,32},{8,40},{16,48},{24,56},{64,96},{128,160},{192,224},{256,288... | collective-permute-start | bytes 626696 | tf_op jit(solution)/shard_map/ppermute | solution.py:284
  35.7 1.3 %collective-permute-start.7 = (f32[408,128]{1,0:T(8,128)S(1)}, f32[408,128]{1,0:T(8,128)S(1)}, u32[]{:S(2)}, u32[]{:S(2)}) collective-permute-start(f32[408,128]{1,0:T(8,128)S(1)} %get-tuple-element.37), channel_id=1, source_target_pairs={{0,1},{1,2},{2,3},{3,4},{4,5},{5,6},{6,7},{8,9},{9,10},{10,11},{11... | collective-permute-start | bytes 626696 | tf_op jit(solution)/shard_map/ppermute | solution.py:284
  37.0 7.1 %collective-permute-done.3.tgt_ref = f32[408,128]{1,0:T(8,128)S(1)} collective-permute-done((f32[408,128]{1,0:T(8,128)S(1)}, f32[408,128]{1,0:T(8,128)S(1)}, u32[]{:S(2)}, u32[]{:S(2)}) %collective-permute-start.3) | collective-permute-done | bytes 208928 | tf_op jit(solution)/shard_map/ppermute | solution.py:284
  44.0 0.3 collective-permute-done.4.src_ref
  44.3 0.8 %unpack.1 = (f32[400,128]{1,0:T(8,128)}, f32[1,1,128]{2,1,0:T(1,128)}, f32[400,128]{1,0:T(8,128)}, f32[1,1,128]{2,1,0:T(1,128)}) custom-call(f32[408,128]{1,0:T(8,128)S(1)} %collective-permute-done.3.tgt_ref, f32[408,128]{1,0:T(8,128)S(1)} %collective-permute-done.4.src_ref), custom_call_target="tpu_custom_call" | custom-call | flops 49999998976 | tf_op jit(solution)/shard_map/unpack/pallas_call | solution.py:335
  45.1 0.0 collective-permute-done.6.src_ref
  45.2 0.0 collective-permute-done.7.tgt_ref
  (3 shorter events, 0.1 us)
Async XLA Ops:
  5.5 9.1 %collective-permute-start = (f32[408,128]{1,0:T(8,128)S(1)}, f32[408,128]{1,0:T(8,128)S(1)}, u32[]{:S(2)}, u32[]{:S(2)}) collective-permute-start(f32[408,128]{1,0:T(8,128)S(1)} %get-tuple-element.22), channel_id=1, source_target_pairs={{6,7},{14,15},{22,23},{30,31},{38,39},{39,40},{46,47},{47,48},{54,... | collective-permute-start | bytes 626696 | tf_op jit(solution)/shard_map/ppermute | solution.py:284
  6.2 14.9 %collective-permute-start.1 = (f32[408,128]{1,0:T(8,128)S(1)}, f32[408,128]{1,0:T(8,128)S(1)}, u32[]{:S(2)}, u32[]{:S(2)}) collective-permute-start(f32[408,128]{1,0:T(8,128)S(1)} %get-tuple-element.23), channel_id=1, source_target_pairs={{0,32},{1,33},{2,34},{3,35},{4,36},{5,37},{6,38},{7,39},{8,40},{9,... | collective-permute-start | bytes 626696 | tf_op jit(solution)/shard_map/ppermute | solution.py:284
  8.6 12.5 %collective-permute-start.2 = (f32[408,128]{1,0:T(8,128)S(1)}, f32[408,128]{1,0:T(8,128)S(1)}, u32[]{:S(2)}, u32[]{:S(2)}) collective-permute-start(f32[408,128]{1,0:T(8,128)S(1)} %get-tuple-element.24), channel_id=1, source_target_pairs={{0,1},{1,2},{2,3},{3,4},{4,5},{5,6},{8,9},{9,10},{10,11},{11,12},{... | collective-permute-start | bytes 626696 | tf_op jit(solution)/shard_map/ppermute | solution.py:284
  13.3 16.8 %collective-permute-start.5 = (f32[408,128]{1,0:T(8,128)S(1)}, f32[408,128]{1,0:T(8,128)S(1)}, u32[]{:S(2)}, u32[]{:S(2)}) collective-permute-start(f32[408,128]{1,0:T(8,128)S(1)} %get-tuple-element.31), channel_id=1, source_target_pairs={{7,8},{15,16},{23,24},{31,0},{95,64},{159,128},{223,192},{287,256}... | collective-permute-start | bytes 626696 | tf_op jit(solution)/shard_map/ppermute | solution.py:284
  21.1 22.9 %collective-permute-start.3 = (f32[408,128]{1,0:T(8,128)S(1)}, f32[408,128]{1,0:T(8,128)S(1)}, u32[]{:S(2)}, u32[]{:S(2)}) collective-permute-start(f32[408,128]{1,0:T(8,128)S(1)} %get-tuple-element.26), channel_id=1, source_target_pairs={{7,8},{15,16},{23,24},{31,0},{39,40},{47,48},{55,56},{63,32},{71,7... | collective-permute-start | bytes 626696 | tf_op jit(solution)/shard_map/ppermute | solution.py:284
  22.4 21.9 %collective-permute-start.4 = (f32[408,128]{1,0:T(8,128)S(1)}, f32[408,128]{1,0:T(8,128)S(1)}, u32[]{:S(2)}, u32[]{:S(2)}) collective-permute-start(f32[408,128]{1,0:T(8,128)S(1)} %get-tuple-element.27), channel_id=1, source_target_pairs={{1,33},{2,34},{3,35},{4,36},{5,37},{6,38},{7,39},{9,41},{10,42},{1... | collective-permute-start | bytes 626696 | tf_op jit(solution)/shard_map/ppermute | solution.py:284
  31.2 14.0 %collective-permute-start.6 = (f32[408,128]{1,0:T(8,128)S(1)}, f32[408,128]{1,0:T(8,128)S(1)}, u32[]{:S(2)}, u32[]{:S(2)}) collective-permute-start(f32[408,128]{1,0:T(8,128)S(1)} %get-tuple-element.32), channel_id=1, source_target_pairs={{0,32},{8,40},{16,48},{24,56},{64,96},{128,160},{192,224},{256,288... | collective-permute-start | bytes 626696 | tf_op jit(solution)/shard_map/ppermute | solution.py:284
  35.7 9.5 %collective-permute-start.7 = (f32[408,128]{1,0:T(8,128)S(1)}, f32[408,128]{1,0:T(8,128)S(1)}, u32[]{:S(2)}, u32[]{:S(2)}) collective-permute-start(f32[408,128]{1,0:T(8,128)S(1)} %get-tuple-element.37), channel_id=1, source_target_pairs={{0,1},{1,2},{2,3},{3,4},{4,5},{5,6},{6,7},{8,9},{9,10},{10,11},{11... | collective-permute-start | bytes 626696 | tf_op jit(solution)/shard_map/ppermute | solution.py:284
